TPU v7x, 32 devices: a whole 2x2x4 slice. The times are simulated.
32 devices in a mesh: dp: 8 (over y, x, core), seq: 4 (over z).
Axes of the slice: x: 2, y: 2, z: 4, core: 2. Of those that a mesh axis runs over, the one named last changes fastest.
Arguments:
- tokens: bfloat16 [8, 1024, 1152], P('dp', 'seq'), may hold values from -38 to 38
- doc_ids: int32 [8, 1024], P('dp', 'seq'), may hold values from 0 to 33, as said below
- token_expert: int32 [8, 1024, 1], P('dp', 'seq'), may hold values from 0 to 1; in each aligned block of 256 rows (0 to 255, 256 to 511, ..., all dimensions but the last counted through in order) at most 160 rows name the same one
- out_grad: bfloat16 [8, 1024, 1152], P('dp', 'seq'), may hold values from -38 to 38
- norm_gains: bfloat16 [2, 1152], P(None, 'dp'), may hold values from 0.5 to 1.5
- in_proj: bfloat16 [1152, 4608], P(None, ('dp', 'seq')), may hold values from -0.1875 to 0.1875
- conv_weight: bfloat16 [4, 2304], P(None, ('dp', 'seq')), may hold values from -3 to 3
- conv_bias: bfloat16 [2304], P(('dp', 'seq')), may hold values from -1 to 1
- select_proj: bfloat16 [2304, 104], P(('dp', 'seq')), may hold values from -0.125 to 0.125
- step_proj: bfloat16 [72, 2304], P(None, ('dp', 'seq')), may hold values from -0.75 to 0.75
- step_bias: bfloat16 [2304], P(('dp', 'seq')), may hold values from -7 to -2
- decay_log: bfloat16 [2304, 16], P(('dp', 'seq')), may hold values from -1.59375 to 0.69921875
- skip_gain: bfloat16 [2304], P(('dp', 'seq')), may hold values from 0.25 to 1
- out_proj: bfloat16 [2304, 1152], P(('dp', 'seq')), may hold values from -1 to 1
- router: bfloat16 [1152, 2], P('dp'), may hold values from -0.125 to 0.125
- expert_up: bfloat16 [2, 1152, 3072], P(None, None, ('dp', 'seq')), may hold values from -0.1875 to 0.1875
- expert_down: bfloat16 [2, 3072, 1152], P(None, ('dp', 'seq')), may hold values from -0.4375 to 0.4375
Outputs:
- layer_out: bfloat16 [8, 1024, 1152], P('dp', 'seq')
- tokens_grad: bfloat16 [8, 1024, 1152], P('dp', 'seq')
- gains_grad: float32 [2, 1152], P(None, 'dp')
- in_proj_grad: float32 [1152, 4608], P(None, ('dp', 'seq'))
- conv_weight_grad: float32 [4, 2304], P(None, ('dp', 'seq'))
- conv_bias_grad: float32 [2304], P(('dp', 'seq'))
- select_proj_grad: float32 [2304, 104], P(('dp', 'seq'))
- step_proj_grad: float32 [72, 2304], P(None, ('dp', 'seq'))
- step_bias_grad: float32 [2304], P(('dp', 'seq'))
- decay_log_grad: float32 [2304, 16], P(('dp', 'seq'))
- skip_gain_grad: float32 [2304], P(('dp', 'seq'))
- out_proj_grad: float32 [2304, 1152], P(('dp', 'seq'))
- router_grad: float32 [1152, 2], P('dp')
- expert_up_grad: float32 [2, 1152, 3072], P(None, None, ('dp', 'seq'))
- expert_down_grad: float32 [2, 3072, 1152], P(None, ('dp', 'seq'))
- stats: float32 [3], replicated
Inputs may be any that keep to these rules, and one draw needn't show every extreme that they name: `doc_ids`: each packed row starts at document 0, and its numbers never fall and rise by at most one from one position to the next. `token_expert`: of the 256 tokens of one device at most 160 name the same expert, and in every draw the tokens of some device name one expert exactly 160 times.
All inputs are finite; a program needn't handle non-finite values.
Results may differ from a plain program's by a relative error of at most 0.012.
The roundings to bfloat16 on the way count: a program that leaves them out, or rounds other values in their place, can miss the bound.
Values may be sent and summed in bfloat16 or wider, within the bound.
No kernel may reach another device: no remote copies, remote signals or barrier semaphores. Data moves between devices by JAX's collectives and lax.ppermute only.
A program may use at most 384 MiB of HBM per device.

v0:
```python
from functools import reduce
import math

import jax
import jax.numpy as jnp
from jax import lax
from jax.sharding import PartitionSpec as P

MODEL_WIDTH = 1152
DI = 2304
R = 72
NS = 16
KC = 4
EXPERT_COUNT = 2


EPS = 1e-05


def passed_along(array, axis, by):
    size = lax.axis_size(axis)
    pairs = [(i, i + by) for i in range(size) if 0 <= i + by < size]
    return lax.ppermute(array, axis, pairs)


def entering(array, axis, combine, identity, reverse):
    size, mine = (lax.axis_size(axis), lax.axis_index(axis))
    everything = jax.tree.map(
        lambda part, kind: lax.all_gather(part.astype(kind), axis),
        array,
        (jnp.bfloat16, jnp.bfloat16),
    )
    start = jax.tree.map(
        lambda part, zero: jnp.broadcast_to(jnp.asarray(zero, part.dtype), part.shape),
        array,
        identity,
    )

    def hop(k, before):
        at = size - 1 - k if reverse else k
        reached = at > mine if reverse else at < mine
        new = combine(
            before, jax.tree.map(lambda part, own: part[at].astype(own.dtype), everything, array)
        )
        return jax.tree.map(lambda a, b: jnp.where(reached, a, b), new, before)

    return lax.fori_loop(0, size, hop, start)


def silu_slope(value):
    logistic = jax.nn.sigmoid(value)
    return logistic * (1.0 + value * (1.0 - logistic))


def gelu_slope(value):
    return 0.5 * (1.0 + lax.erf(value / math.sqrt(2.0))) + value * jnp.exp(
        -0.5 * value * value
    ) / math.sqrt(2.0 * math.pi)


def chain_join(earlier, later):
    return (earlier[0] * later[0], later[0] * earlier[1] + later[1])


def advance_state(state, delta_t, inner_t, select_in, kept_t, decay_rate):
    factor = kept_t * jnp.exp(delta_t[None, :] * decay_rate)
    return factor * state + select_in[:, None] * (delta_t * inner_t)[None, :]


def forward_tokens(state, inputs, decay_rate):

    def forward_advance(state, item):
        delta_t, inner_t, select_in, select_out, kept_t = item
        state = advance_state(state, delta_t, inner_t, select_in, kept_t, decay_rate)
        return (state, jnp.sum(select_out[:, None] * state, 0))

    return lax.scan(forward_advance, state, inputs, unroll=8)


def block_states(start, inputs, decay_rate):

    def block_advance(state, item):
        delta_t, inner_t, select_in, kept_t = item
        state = advance_state(state, delta_t, inner_t, select_in, kept_t, decay_rate)
        return (state, state)

    return lax.scan(block_advance, start, inputs, unroll=8)


def adjoint_total(zero_state, inputs, decay_rate):

    def adjoint_retreat(carry, item):
        grad_t, select_out, delta_t, kept_t = item
        adjoint = select_out[:, None] * grad_t[None, :] + carry
        return (kept_t * jnp.exp(delta_t[None, :] * decay_rate) * adjoint, None)

    final, _ = lax.scan(adjoint_retreat, zero_state, inputs, reverse=True, unroll=8)
    return final


def retreat_block(carry, inputs, decay_rate):

    def retreat_retreat(carry, item):
        adjoint_next, rate_sum = carry
        grad_t, select_in, select_out, delta_t, inner_t, kept_t, prior = item
        adjoint = select_out[:, None] * grad_t[None, :] + adjoint_next
        factor = kept_t * jnp.exp(delta_t[None, :] * decay_rate)
        through = adjoint * factor * prior
        weighted = jnp.sum(adjoint * select_in[:, None], 0)
        in_grad_t = jnp.sum(adjoint * (delta_t * inner_t)[None, :], 1)
        inner_grad_t = weighted * delta_t
        delta_grad_t = weighted * inner_t + jnp.sum(through * decay_rate, 0)
        return (
            (factor * adjoint, rate_sum + through * delta_t[None, :]),
            (in_grad_t, inner_grad_t, delta_grad_t),
        )

    return lax.scan(retreat_retreat, carry, inputs, reverse=True, unroll=8)


def per_device(
    tokens,
    doc_ids,
    token_expert,
    out_grad,
    norm_gains,
    in_proj,
    conv_weight,
    conv_bias,
    select_proj,
    step_proj,
    step_bias,
    decay_log,
    skip_gain,
    out_proj,
    router,
    expert_up,
    expert_down,
):
    rows = tokens.shape[1]
    slots_per = 5 * rows // (4 * EXPERT_COUNT)
    block = math.gcd(rows, 64)
    blocks = rows // block
    highest = lax.Precision.HIGHEST
    gains_all, router_all = (
        lax.all_gather(norm_gains, "dp", axis=1, tiled=True),
        lax.all_gather(router, "dp", axis=0, tiled=True),
    )
    gains_all = gains_all.astype(jnp.float32)
    router_all = router_all.astype(jnp.float32)
    (
        in_full,
        conv_full,
        bias_conv,
        select_full,
        step_full,
        bias_step,
        decay_full,
        skip_full,
        out_full,
    ) = (
        lax.all_gather(in_proj, ("dp", "seq"), axis=1, tiled=True),
        lax.all_gather(conv_weight, ("dp", "seq"), axis=1, tiled=True),
        lax.all_gather(conv_bias, ("dp", "seq"), axis=0, tiled=True),
        lax.all_gather(select_proj, ("dp", "seq"), axis=0, tiled=True),
        lax.all_gather(step_proj, ("dp", "seq"), axis=1, tiled=True),
        lax.all_gather(step_bias, ("dp", "seq"), axis=0, tiled=True),
        lax.all_gather(decay_log, ("dp", "seq"), axis=0, tiled=True),
        lax.all_gather(skip_gain, ("dp", "seq"), axis=0, tiled=True),
        lax.all_gather(out_proj, ("dp", "seq"), axis=0, tiled=True),
    )
    conv_taps = conv_full.astype(jnp.float32)
    skip_wide = skip_full.astype(jnp.float32)
    decay_rate = -jnp.exp(decay_full.astype(jnp.float32)).T
    stream = tokens[0].astype(jnp.float32)
    inv_first = lax.rsqrt(jnp.mean(stream * stream, -1, keepdims=True) + EPS)
    hat_first = stream * inv_first
    normed = (hat_first * gains_all[0]).astype(jnp.bfloat16)
    proj = jnp.dot(normed, in_full, preferred_element_type=jnp.float32).astype(jnp.bfloat16)
    front = proj[:, :DI]
    gate_half = proj[:, DI:].astype(jnp.float32)
    doc_row = doc_ids[0]
    prior_doc = passed_along(doc_row[rows - KC + 1 :], "seq", 1)
    prior_front = passed_along(front[rows - KC + 1 :], "seq", 1)
    ext_ids = jnp.concatenate([prior_doc, doc_row])
    ext_rows = jnp.concatenate([prior_front, front]).astype(jnp.float32)
    masks = [(ext_ids[k : k + rows] == doc_row)[:, None] for k in range(KC)]
    taps = [jnp.where(masks[k], ext_rows[k : k + rows], 0.0) for k in range(KC)]
    conv_sum = bias_conv.astype(jnp.float32)[None, :]
    for k in range(KC):
        conv_sum = conv_sum + conv_taps[k][None, :] * taps[k]
    inner = jax.nn.silu(conv_sum).astype(jnp.bfloat16)
    inner_wide = inner.astype(jnp.float32)
    select = jnp.dot(inner, select_full, preferred_element_type=jnp.float32)
    steps_low = select[:, :R].astype(jnp.bfloat16)
    in_select = select[:, R : R + NS]
    out_select = select[:, R + NS :]
    step_pre = (
        jnp.dot(steps_low, step_full, preferred_element_type=jnp.float32)
        + bias_step.astype(jnp.float32)[None, :]
    )
    delta = jax.nn.softplus(step_pre)
    kept_flag = (ext_ids[KC - 2 : KC - 2 + rows] == doc_row).astype(jnp.float32)
    inputs = (delta, inner_wide, in_select, out_select, kept_flag)
    zero_state = jnp.zeros((NS, DI), jnp.float32)
    local_end, _ = forward_tokens(zero_state, inputs, decay_rate)
    total_decay = jnp.exp(decay_rate * jnp.sum(delta, 0)[None, :]) * jnp.min(kept_flag)
    identity = (jnp.ones_like(total_decay), zero_state)
    _, state_in = entering((total_decay, local_end), "seq", chain_join, identity, False)
    blocked = jax.tree.map(
        lambda member: member.reshape((blocks, block) + member.shape[1:]), inputs
    )

    def run_block(state, part):
        end, outputs = forward_tokens(state, part, decay_rate)
        return (end, (outputs, state))

    _, (scan_out, block_starts) = lax.scan(run_block, state_in, blocked)
    scanned = scan_out.reshape(rows, DI) + skip_wide[None, :] * inner_wide
    silu_gate = jax.nn.silu(gate_half)
    gated = (scanned * silu_gate).astype(jnp.bfloat16)
    mixed = jnp.dot(gated, out_full, preferred_element_type=jnp.float32)
    resid = stream + mixed
    inv_second = lax.rsqrt(jnp.mean(resid * resid, -1, keepdims=True) + EPS)
    hat_second = resid * inv_second
    normed_moe = (hat_second * gains_all[1]).astype(jnp.bfloat16)
    normed_wide = normed_moe.astype(jnp.float32)
    logits = jnp.dot(normed_wide, router_all, precision=highest, preferred_element_type=jnp.float32)
    probs = jax.nn.softmax(logits, -1)
    route = token_expert[0, :, 0]
    route_hot = route[:, None] == jnp.arange(EXPERT_COUNT, dtype=jnp.int32)[None, :]
    hot_int = route_hot.astype(jnp.int32)
    hot_wide = route_hot.astype(jnp.float32)
    chosen = jnp.sum(probs * hot_wide, 1)
    rank_in = jnp.cumsum(hot_int, 0) - 1
    slot = jnp.sum(rank_in * hot_int, 1)
    target = route * slots_per + slot
    source = (
        jnp.full((EXPERT_COUNT * slots_per,), rows, jnp.int32)
        .at[target]
        .set(jnp.arange(rows, dtype=jnp.int32))
    )
    zero_row = jnp.zeros((1, MODEL_WIDTH), jnp.bfloat16)
    buffer = jnp.concatenate([normed_moe, zero_row])[source].reshape(
        EXPERT_COUNT, slots_per, MODEL_WIDTH
    )
    up_full, down_full = (
        lax.all_gather(expert_up, ("dp", "seq"), axis=2, tiled=True),
        lax.all_gather(expert_down, ("dp", "seq"), axis=1, tiled=True),
    )
    hidden = jnp.einsum("ecd,edf->ecf", buffer, up_full, preferred_element_type=jnp.float32)
    active = jax.nn.gelu(hidden, approximate=False).astype(jnp.bfloat16)
    returned_slots = jnp.einsum(
        "ecf,efd->ecd", active, down_full, preferred_element_type=jnp.float32
    )
    returned = returned_slots.reshape(EXPERT_COUNT * slots_per, MODEL_WIDTH)[target]
    branch = chosen[:, None] * returned
    layer_out = (resid + branch).astype(jnp.bfloat16)
    squared_values = jnp.stack(
        [jnp.sum(resid * resid), jnp.sum(mixed * mixed), jnp.sum(branch * branch)]
    )
    out_cot = out_grad[0].astype(jnp.float32)
    chosen_grad = jnp.sum(out_cot * returned, 1)
    returned_grad = (chosen[:, None] * out_cot).astype(jnp.bfloat16)
    returned_grad_slots = jnp.concatenate([returned_grad, zero_row])[source].reshape(
        EXPERT_COUNT, slots_per, MODEL_WIDTH
    )
    up_full, down_full = (
        lax.all_gather(expert_up, ("dp", "seq"), axis=2, tiled=True),
        lax.all_gather(expert_down, ("dp", "seq"), axis=1, tiled=True),
    )
    grad_down = jnp.einsum(
        "ecf,ecd->fed", active, returned_grad_slots, preferred_element_type=jnp.float32
    )
    active_grad = jnp.einsum(
        "ecd,efd->ecf", returned_grad_slots, down_full, preferred_element_type=jnp.float32
    )
    hidden_grad = (active_grad * gelu_slope(hidden)).astype(jnp.bfloat16)
    grad_up = jnp.einsum("ecd,ecf->fed", buffer, hidden_grad, preferred_element_type=jnp.float32)
    buffer_grad = jnp.einsum(
        "ecf,edf->ecd", hidden_grad, up_full, preferred_element_type=jnp.float32
    )
    logit_grad = (chosen_grad * chosen)[:, None] * (hot_wide - probs)
    grad_router = jnp.einsum(
        "td,te->de", normed_wide, logit_grad, precision=highest, preferred_element_type=jnp.float32
    )
    moe_grad = buffer_grad.reshape(EXPERT_COUNT * slots_per, MODEL_WIDTH)[target] + jnp.einsum(
        "te,de->td", logit_grad, router_all, precision=highest, preferred_element_type=jnp.float32
    )
    second_gain_grad = jnp.sum(moe_grad * hat_second, 0)
    scaled_second = moe_grad * gains_all[1]
    resid_grad = out_cot + inv_second * (
        scaled_second - hat_second * jnp.mean(scaled_second * hat_second, -1, keepdims=True)
    )
    (
        in_full,
        conv_full,
        bias_conv,
        select_full,
        step_full,
        bias_step,
        decay_full,
        skip_full,
        out_full,
    ) = (
        lax.all_gather(in_proj, ("dp", "seq"), axis=1, tiled=True),
        lax.all_gather(conv_weight, ("dp", "seq"), axis=1, tiled=True),
        lax.all_gather(conv_bias, ("dp", "seq"), axis=0, tiled=True),
        lax.all_gather(select_proj, ("dp", "seq"), axis=0, tiled=True),
        lax.all_gather(step_proj, ("dp", "seq"), axis=1, tiled=True),
        lax.all_gather(step_bias, ("dp", "seq"), axis=0, tiled=True),
        lax.all_gather(decay_log, ("dp", "seq"), axis=0, tiled=True),
        lax.all_gather(skip_gain, ("dp", "seq"), axis=0, tiled=True),
        lax.all_gather(out_proj, ("dp", "seq"), axis=0, tiled=True),
    )
    conv_taps = conv_full.astype(jnp.float32)
    skip_wide = skip_full.astype(jnp.float32)
    mixed_grad = resid_grad.astype(jnp.bfloat16)
    grad_out = jnp.einsum("tc,td->cd", gated, mixed_grad, preferred_element_type=jnp.float32)
    gated_grad = jnp.einsum("td,cd->tc", mixed_grad, out_full, preferred_element_type=jnp.float32)
    scan_grad = gated_grad * silu_gate
    gate_grad = gated_grad * scanned * silu_slope(gate_half)
    grad_skip = jnp.sum(scan_grad * inner_wide, 0)
    local_adjoint = adjoint_total(zero_state, (scan_grad, out_select, delta, kept_flag), decay_rate)
    _, adjoint_in = entering((total_decay, local_adjoint), "seq", chain_join, identity, True)
    grad_blocked = scan_grad.reshape(blocks, block, DI)

    def back_block(carry, part):
        start, delta_b, inner_b, in_b, out_b, kept_b, grad_b = part
        _, states = block_states(start, (delta_b, inner_b, in_b, kept_b), decay_rate)
        priors = jnp.concatenate([start[None], states[:-1]])
        out_grad_b = jnp.sum(grad_b[:, None, :] * states, 2)
        carry, (in_grad_b, inner_grad_b, delta_grad_b) = retreat_block(
            carry, (grad_b, in_b, out_b, delta_b, inner_b, kept_b, priors), decay_rate
        )
        return (carry, (in_grad_b, inner_grad_b, delta_grad_b, out_grad_b))

    (_, rate_sum), (in_select_grad, inner_scan_grad, delta_grad, out_select_grad) = lax.scan(
        back_block,
        (adjoint_in, zero_state),
        (block_starts,) + tuple(blocked) + (grad_blocked,),
        reverse=True,
    )
    in_select_grad = in_select_grad.reshape(rows, NS)
    out_select_grad = out_select_grad.reshape(rows, NS)
    inner_scan_grad = inner_scan_grad.reshape(rows, DI)
    delta_grad = delta_grad.reshape(rows, DI)
    grad_decay = (rate_sum * decay_rate).T
    pre_grad = delta_grad * jax.nn.sigmoid(step_pre)
    grad_step_bias = jnp.sum(pre_grad, 0)
    pre_low = pre_grad.astype(jnp.bfloat16)
    grad_step = jnp.einsum("tr,tc->cr", steps_low, pre_low, preferred_element_type=jnp.float32)
    steps_grad = jnp.einsum("tc,rc->tr", pre_low, step_full, preferred_element_type=jnp.float32)
    select_low = jnp.concatenate([steps_grad, in_select_grad, out_select_grad], 1).astype(
        jnp.bfloat16
    )
    grad_select = jnp.einsum("tc,tj->cj", inner, select_low, preferred_element_type=jnp.float32)
    inner_grad = (
        scan_grad * skip_wide[None, :]
        + inner_scan_grad
        + jnp.einsum("tj,cj->tc", select_low, select_full, preferred_element_type=jnp.float32)
    )
    conv_back = inner_grad * silu_slope(conv_sum)
    grad_conv_bias = jnp.sum(conv_back, 0)
    grad_conv = jnp.stack([jnp.sum(conv_back * taps[k], 0) for k in range(KC)], 1)
    spread = [
        jnp.pad(
            jnp.where(masks[k], conv_back * conv_taps[k][None, :], 0.0), ((k, KC - 1 - k), (0, 0))
        )
        for k in range(KC)
    ]
    ext_grad = reduce(jnp.add, spread)
    incoming = passed_along(ext_grad[: KC - 1], "seq", -1)
    front_grad = ext_grad[KC - 1 :] + jnp.pad(incoming, ((rows - KC + 1, 0), (0, 0)))
    proj_grad = jnp.concatenate([front_grad, gate_grad], 1).astype(jnp.bfloat16)
    grad_in = jnp.einsum("td,tj->jd", normed, proj_grad, preferred_element_type=jnp.float32)
    normed_grad = jnp.einsum("tj,dj->td", proj_grad, in_full, preferred_element_type=jnp.float32)
    first_gain_grad = jnp.sum(normed_grad * hat_first, 0)
    scaled_first = normed_grad * gains_all[0]
    stream_grad = resid_grad + inv_first * (
        scaled_first - hat_first * jnp.mean(scaled_first * hat_first, -1, keepdims=True)
    )
    summed = (
        lax.psum_scatter(grad_in, ("dp", "seq"), scatter_dimension=0, tiled=True),
        lax.psum_scatter(grad_conv, ("dp", "seq"), scatter_dimension=0, tiled=True),
        lax.psum_scatter(grad_conv_bias, ("dp", "seq"), scatter_dimension=0, tiled=True),
        lax.psum_scatter(grad_select, ("dp", "seq"), scatter_dimension=0, tiled=True),
        lax.psum_scatter(grad_step, ("dp", "seq"), scatter_dimension=0, tiled=True),
        lax.psum_scatter(grad_step_bias, ("dp", "seq"), scatter_dimension=0, tiled=True),
        lax.psum_scatter(grad_decay, ("dp", "seq"), scatter_dimension=0, tiled=True),
        lax.psum_scatter(grad_skip, ("dp", "seq"), scatter_dimension=0, tiled=True),
        lax.psum_scatter(grad_out, ("dp", "seq"), scatter_dimension=0, tiled=True),
        lax.psum_scatter(grad_up, ("dp", "seq"), scatter_dimension=0, tiled=True),
        lax.psum_scatter(grad_down, ("dp", "seq"), scatter_dimension=0, tiled=True),
    )
    gains_total, router_total, square_total = lax.psum(
        (jnp.stack([first_gain_grad, second_gain_grad]), grad_router, squared_values), ("dp", "seq")
    )
    width = MODEL_WIDTH // lax.axis_size("dp")
    offset = lax.axis_index("dp") * width
    gains_part = lax.dynamic_slice_in_dim(gains_total, offset, width, 1)
    router_part = lax.dynamic_slice_in_dim(router_total, offset, width, 0)
    count = rows * lax.axis_size("dp") * lax.axis_size("seq") * MODEL_WIDTH
    stats = jnp.sqrt(square_total / count)
    return (
        layer_out[None],
        stream_grad.astype(jnp.bfloat16)[None],
        gains_part,
        summed[0].T,
        summed[1].T,
        summed[2],
        summed[3],
        summed[4].T,
        summed[5],
        summed[6],
        summed[7],
        summed[8],
        router_part,
        jnp.transpose(summed[9], (1, 2, 0)),
        jnp.transpose(summed[10], (1, 0, 2)),
        stats,
    )


def solution(mesh):
    return jax.shard_map(
        per_device,
        mesh=mesh,
        in_specs=(
            P("dp", "seq", None),
            P("dp", "seq"),
            P("dp", "seq", None),
            P("dp", "seq", None),
            P(None, "dp"),
            P(None, ("dp", "seq")),
            P(None, ("dp", "seq")),
            P(("dp", "seq")),
            P(("dp", "seq"), None),
            P(None, ("dp", "seq")),
            P(("dp", "seq")),
            P(("dp", "seq"), None),
            P(("dp", "seq")),
            P(("dp", "seq"), None),
            P("dp", None),
            P(None, None, ("dp", "seq")),
            P(None, ("dp", "seq"), None),
        ),
        out_specs=(
            P("dp", "seq", None),
            P("dp", "seq", None),
            P(None, "dp"),
            P(None, ("dp", "seq")),
            P(None, ("dp", "seq")),
            P(("dp", "seq")),
            P(("dp", "seq"), None),
            P(None, ("dp", "seq")),
            P(("dp", "seq")),
            P(("dp", "seq"), None),
            P(("dp", "seq")),
            P(("dp", "seq"), None),
            P("dp", None),
            P(None, None, ("dp", "seq")),
            P(None, ("dp", "seq"), None),
            P(),
        ),
        check_vma=False,
    )
```

profile of v0, /device:TPU:0, one launch (start us, length us, event | category | flops | bytes accessed | tf_op | source)
XLA Modules:
  0.0 4159.3 jit_solution(14044941782848562654)
XLA Ops:
  25.8 66.6 %all-gather.4 = bf16[32,72,4]{1,2,0:T(4,128)(2,1)S(1)} all-gather(bf16[1,72,4]{1,2,0:T(4,128)(2,1)} %bitcast.743), channel_id=1, replica_groups=mesh['dp'=8,'seq'=4] {'dp','seq'}, dimensions={0}, use_global_device_ids=true | all-gather | bytes 19008 | tf_op jit(solution)/shard_map/all_gather | solution.py:163
  94.0 38.1 all-reduce.21
  132.8 74.7 %all_gather.73 = bf16[72,2304]{0,1:T(8,128)(2,1)S(1)} all-gather(bf16[72,72]{0,1:T(8,128)(2,1)S(1)} %copy.99), channel_id=1, replica_groups=mesh['dp'=8,'seq'=4] {'dp','seq'}, dimensions={1}, use_global_device_ids=true | all-gather | bytes 342144 | tf_op jit(solution)/shard_map/all_gather | solution.py:166
  208.1 77.0 %all_gather.72 = bf16[2304,104]{1,0:T(8,128)(2,1)S(1)} all-gather(bf16[72,104]{1,0:T(8,128)(2,1)S(1)} %copy-done.64), channel_id=1, replica_groups=mesh['dp'=8,'seq'=4] {'dp','seq'}, dimensions={0}, use_global_device_ids=true | all-gather | bytes 494208 | tf_op jit(solution)/shard_map/all_gather | solution.py:165
  285.1 65.9 %all-gather.3 = bf16[32,72,16]{1,2,0:T(8,128)(2,1)S(1)} all-gather(bf16[1,72,16]{1,2,0:T(8,128)(2,1)S(1)} %bitcast.737), channel_id=1, replica_groups=mesh['dp'=8,'seq'=4] {'dp','seq'}, dimensions={0}, use_global_device_ids=true | all-gather | bytes 76032 | tf_op jit(solution)/shard_map/all_gather | solution.py:168
  397.4 14.9 all-gather
  412.4 272.0 %while.196 = (s32[]{:T(128)}, f32[16,2304]{1,0:T(8,128)S(1)}, f32[32,8]{0,1:T(8,128)S(1)}, f32[32,8,2304]{2,1,0:T(8,128)}, f32[16,2304]{1,0:T(8,128)S(1)}, /*ind...) while((s32[]{:T(128)}, f32[16,2304]{1,0:T(8,128)S(1)}, ...), condition=%wide.region_4.5_spmd.clone, body=%wide.region_3.4_spmd.clone.sunk | while | flops 1529866 | bytes 1108931 | solution.py:77
  684.5 14.0 all-gather.1
  702.1 363.3 %while.192 = (s32[]{:T(128)}, f32[16,2304]{1,0:T(8,128)S(1)}, f32[4,64,2304]{2,1,0:T(8,128)}, f32[4,16,2304]{2,1,0:T(8,128)}, f32[4,64,2304]{2,1,0:T(8,128)}, /*...) while((s32[]{:T(128)}, f32[16,2304]{1,0:T(8,128)S(1)}, ...), condition=%wide.region_18.19_spmd, body=%wide.region_7.18_spmd.sunk | while | flops 2801675 | bytes 7470158 | solution.py:218
  704.3 86.8 %while.200 = (s32[]{:T(128)}, f32[16,2304]{1,0:T(8,128)S(1)}, f32[8,8,2304]{2,1,0:T(8,128)}, f32[8,8]{1,0:T(8,128)S(1)}, f32[8,8,2304]{2,1,0:T(8,128)S(1)}, /*in...) while((s32[]{:T(128)}, f32[16,2304]{1,0:T(8,128)S(1)}, ...), condition=%wide.region_17.17_spmd, body=%wide.region_8.16_spmd.sunk | while | flops 2801673 | bytes 3618525 | solution.py:77
  795.1 86.8 %while.200 = (s32[]{:T(128)}, f32[16,2304]{1,0:T(8,128)S(1)}, f32[8,8,2304]{2,1,0:T(8,128)}, f32[8,8]{1,0:T(8,128)S(1)}, f32[8,8,2304]{2,1,0:T(8,128)S(1)}, /*in...) while((s32[]{:T(128)}, f32[16,2304]{1,0:T(8,128)S(1)}, ...), condition=%wide.region_17.17_spmd, body=%wide.region_8.16_spmd.sunk | while | flops 2801673 | bytes 3618525 | solution.py:77
  886.0 86.8 %while.200 = (s32[]{:T(128)}, f32[16,2304]{1,0:T(8,128)S(1)}, f32[8,8,2304]{2,1,0:T(8,128)}, f32[8,8]{1,0:T(8,128)S(1)}, f32[8,8,2304]{2,1,0:T(8,128)S(1)}, /*in...) while((s32[]{:T(128)}, f32[16,2304]{1,0:T(8,128)S(1)}, ...), condition=%wide.region_17.17_spmd, body=%wide.region_8.16_spmd.sunk | while | flops 2801673 | bytes 3618525 | solution.py:77
  976.8 86.8 %while.200 = (s32[]{:T(128)}, f32[16,2304]{1,0:T(8,128)S(1)}, f32[8,8,2304]{2,1,0:T(8,128)}, f32[8,8]{1,0:T(8,128)S(1)}, f32[8,8,2304]{2,1,0:T(8,128)S(1)}, /*in...) while((s32[]{:T(128)}, f32[16,2304]{1,0:T(8,128)S(1)}, ...), condition=%wide.region_17.17_spmd, body=%wide.region_8.16_spmd.sunk | while | flops 2801673 | bytes 3618525 | solution.py:77
  1154.0 285.8 %while.198 = (s32[]{:T(128)}, f32[16,2304]{1,0:T(8,128)S(1)}, f32[32,8]{0,1:T(8,128)S(1)}, f32[32,8,2304]{2,1,0:T(8,128)}, f32[16,2304]{1,0:T(8,128)S(1)}, /*ind...) while((s32[]{:T(128)}, f32[16,2304]{1,0:T(8,128)S(1)}, ...), condition=%wide.region_30.31_spmd.clone, body=%wide.region_29.30_spmd.clone.sunk | while | flops 1511435 | bytes 887767 | solution.py:97
  1439.8 13.9 all-gather.2
  1461.0 1249.2 %while.195 = (s32[]{:T(128)}, f32[16,2304]{1,0:T(8,128)S(1)}, f32[16,2304]{1,0:T(8,128)S(1)}, bf16[4,64,16]{2,1,0:T(8,128)(2,1)S(1)}, f32[4,64,2304]{2,1,0:T(8,1...) while((s32[]{:T(128)}, f32[16,2304]{1,0:T(8,128)S(1)}, ...), condition=%wide.region_63.64_spmd, body=%wide.region_33.63_spmd.sunk | while | flops 17380244 | bytes 73256120 | solution.py:338
  1467.6 130.4 %while.201 = (s32[]{:T(128)}, f32[16,2304]{1,0:T(8,128)S(1)}, f32[8,8,16,2304]{3,2,1,0:T(8,128)}, f32[8,8]{1,0:T(8,128)S(1)}, f32[8,8,2304]{2,1,0:T(8,128)S(1)},...) while((s32[]{:T(128)}, f32[16,2304]{1,0:T(8,128)S(1)}, ...), condition=%wide.region_35.35_spmd, body=%wide.region_34.34_spmd.sunk | while | flops 3704840 | bytes 7206965 | solution.py:87
  1608.3 159.4 %while.202 = (s32[]{:T(128)}, f32[16,2304]{1,0:T(8,128)S(1)}, f32[16,2304]{1,0:T(8,128)S(1)}, bf16[8,8,16]{2,1,0:T(8,128)(2,1)S(1)}, f32[8,8,2304]{2,1,0:T(8,128...) while((s32[]{:T(128)}, f32[16,2304]{1,0:T(8,128)S(1)}, ...), condition=%wide.region_61.61_spmd, body=%wide.region_36.60_spmd.sunk | while | flops 6598538 | bytes 8453509 | solution.py:118
  1779.9 130.4 %while.201 = (s32[]{:T(128)}, f32[16,2304]{1,0:T(8,128)S(1)}, f32[8,8,16,2304]{3,2,1,0:T(8,128)}, f32[8,8]{1,0:T(8,128)S(1)}, f32[8,8,2304]{2,1,0:T(8,128)S(1)},...) while((s32[]{:T(128)}, f32[16,2304]{1,0:T(8,128)S(1)}, ...), condition=%wide.region_35.35_spmd, body=%wide.region_34.34_spmd.sunk | while | flops 3704840 | bytes 7206965 | solution.py:87
  1920.6 159.4 %while.202 = (s32[]{:T(128)}, f32[16,2304]{1,0:T(8,128)S(1)}, f32[16,2304]{1,0:T(8,128)S(1)}, bf16[8,8,16]{2,1,0:T(8,128)(2,1)S(1)}, f32[8,8,2304]{2,1,0:T(8,128...) while((s32[]{:T(128)}, f32[16,2304]{1,0:T(8,128)S(1)}, ...), condition=%wide.region_61.61_spmd, body=%wide.region_36.60_spmd.sunk | while | flops 6598538 | bytes 8453509 | solution.py:118
  2092.2 130.4 %while.201 = (s32[]{:T(128)}, f32[16,2304]{1,0:T(8,128)S(1)}, f32[8,8,16,2304]{3,2,1,0:T(8,128)}, f32[8,8]{1,0:T(8,128)S(1)}, f32[8,8,2304]{2,1,0:T(8,128)S(1)},...) while((s32[]{:T(128)}, f32[16,2304]{1,0:T(8,128)S(1)}, ...), condition=%wide.region_35.35_spmd, body=%wide.region_34.34_spmd.sunk | while | flops 3704840 | bytes 7206965 | solution.py:87
  2232.9 159.4 %while.202 = (s32[]{:T(128)}, f32[16,2304]{1,0:T(8,128)S(1)}, f32[16,2304]{1,0:T(8,128)S(1)}, bf16[8,8,16]{2,1,0:T(8,128)(2,1)S(1)}, f32[8,8,2304]{2,1,0:T(8,128...) while((s32[]{:T(128)}, f32[16,2304]{1,0:T(8,128)S(1)}, ...), condition=%wide.region_61.61_spmd, body=%wide.region_36.60_spmd.sunk | while | flops 6598538 | bytes 8453509 | solution.py:118
  2404.5 130.4 %while.201 = (s32[]{:T(128)}, f32[16,2304]{1,0:T(8,128)S(1)}, f32[8,8,16,2304]{3,2,1,0:T(8,128)}, f32[8,8]{1,0:T(8,128)S(1)}, f32[8,8,2304]{2,1,0:T(8,128)S(1)},...) while((s32[]{:T(128)}, f32[16,2304]{1,0:T(8,128)S(1)}, ...), condition=%wide.region_35.35_spmd, body=%wide.region_34.34_spmd.sunk | while | flops 3704840 | bytes 7206965 | solution.py:87
  2545.2 159.4 %while.202 = (s32[]{:T(128)}, f32[16,2304]{1,0:T(8,128)S(1)}, f32[16,2304]{1,0:T(8,128)S(1)}, bf16[8,8,16]{2,1,0:T(8,128)(2,1)S(1)}, f32[8,8,2304]{2,1,0:T(8,128...) while((s32[]{:T(128)}, f32[16,2304]{1,0:T(8,128)S(1)}, ...), condition=%wide.region_61.61_spmd, body=%wide.region_36.60_spmd.sunk | while | flops 6598538 | bytes 8453509 | solution.py:118
  2754.1 41.3 copy.111
  2836.1 25.4 all-reduce.25.cloned.1.call-done
  2870.5 94.1 %reduce-scatter.20.cloned.1.call-done = f32[72,72]{1,0:T(8,128)} async-done(((f32[2304,72]{1,0:T(8,128)}), f32[72,72]{1,0:T(8,128)}) %reduce-scatter.20.cloned.1.call-update) | async-done | bytes 20752
  2966.0 440.4 %all-reduce.27.cloned.1.call-done = (f32[2304,16]{0,1:T(8,128)}, f32[3072,2,1152]{2,1,0:T(2,128)}) async-done(((f32[2304,16]{0,1:T(8,128)}, f32[3072,2,1152]{2,1,0:T(2,128)}), (f32[2304,16]{0,1:T(8,128)}, f32[3072,2,1152]{2,1,0:T(2,128)})) %all-reduce.27.cloned.1.call-update) | async-done | bytes 28459024
  3410.1 98.4 %reduce-scatter.18.cloned.1.call-done = f32[72,104]{1,0:T(8,128)} async-done(((f32[2304,104]{1,0:T(8,128)}), f32[72,104]{1,0:T(8,128)}) %reduce-scatter.18.cloned.1.call-update) | async-done | bytes 29968
  3508.5 148.7 %reduce-scatter.22.cloned.1.call-done = f32[72,1152]{1,0:T(8,128)} async-done(((f32[2304,1152]{1,0:T(8,128)}), f32[72,1152]{1,0:T(8,128)}) %reduce-scatter.22.cloned.1.call-update) | async-done | bytes 331792
  3657.2 226.7 %reduce-scatter.14.cloned.1.call-done = f32[144,1152]{1,0:T(8,128)} async-done(((f32[4608,1152]{1,0:T(8,128)}), f32[144,1152]{1,0:T(8,128)}) %reduce-scatter.14.cloned.1.call-update) | async-done | bytes 663568 | tf_op jit(solution)/shard_map/reduce_scatter | solution.py:384
  3883.9 268.4 %reduce-scatter.16.cloned.1.call-done = f32[96,2,1152]{2,0,1:T(8,128)} async-done(((f32[3072,2,1152]{2,0,1:T(8,128)}), f32[96,2,1152]{2,0,1:T(8,128)}) %reduce-scatter.16.cloned.1.call-update) | async-done | bytes 884752 | tf_op jit(solution)/shard_map/reduce_scatter | solution.py:393
  (3833 shorter events, 2422.9 us)
Async XLA Ops:
  7.2 86.1 %copy-start.85 = (bf16[72]{0:T(256)(128)(2,1)S(1)}, bf16[72]{0:T(256)(128)(2,1)}, u32[]{:S(2)}) copy-start(bf16[72]{0:T(256)(128)(2,1)} %param.42) | copy-start | bytes 436
  7.2 86.3 %copy-start.86 = (bf16[72]{0:T(256)(128)(2,1)S(1)}, bf16[72]{0:T(256)(128)(2,1)}, u32[]{:S(2)}) copy-start(bf16[72]{0:T(256)(128)(2,1)} %param.45) | copy-start | bytes 436
  7.2 86.5 %copy-start.87 = (bf16[72]{0:T(256)(128)(2,1)S(1)}, bf16[72]{0:T(256)(128)(2,1)}, u32[]{:S(2)}) copy-start(bf16[72]{0:T(256)(128)(2,1)} %param.47) | copy-start | bytes 436
  7.2 125.5 %copy-start.67 = (bf16[72,72]{1,0:T(8,128)(2,1)S(1)}, bf16[72,72]{1,0:T(8,128)(2,1)}, u32[]{:S(2)}) copy-start(bf16[72,72]{1,0:T(8,128)(2,1)} %param.44) | copy-start | bytes 31108
  7.2 200.9 %copy-start.64 = (bf16[72,104]{1,0:T(8,128)(2,1)S(1)}, bf16[72,104]{1,0:T(8,128)(2,1)}, u32[]{:S(2)}) copy-start(bf16[72,104]{1,0:T(8,128)(2,1)} %param.43) | copy-start | bytes 44932
  7.2 277.9 %copy-start.76 = (bf16[72,16]{0,1:T(8,128)(2,1)S(1)}, bf16[72,16]{0,1:T(8,128)(2,1)}, u32[]{:S(2)}) copy-start(bf16[72,16]{0,1:T(8,128)(2,1)} %param.46) | copy-start | bytes 6916
  7.2 362.5 %all-gather.12.cloned.1.call-start = ((), (), s32[]{:S(2)}) async-start(), calls=%async_computation.5 | async-start | bytes 10948608 | tf_op jit(solution)/shard_map/all_gather | solution.py:162
  8.0 1061.7 %all-gather.14.cloned.1.call-start = ((), (), s32[]{:S(2)}) async-start(), calls=%async_computation.6 | async-start | bytes 5474304 | tf_op jit(solution)/shard_map/all_gather | solution.py:170
  8.7 343.1 %copy-start.62 = (s32[1,256]{1,0:T(1,128)S(1)}, s32[1,256]{1,0:T(1,128)}, u32[]{:S(2)}) copy-start(s32[1,256]{1,0:T(1,128)} %param.36) | copy-start | bytes 3076
  8.7 344.5 %copy-start.59 = (s32[1,256,1]{1,2,0:T(1,128)S(1)}, s32[1,256,1]{1,2,0:T(1,128)}, u32[]{:S(2)}) copy-start(s32[1,256,1]{1,2,0:T(1,128)} %param.37) | copy-start | bytes 3076
  8.7 348.3 %copy-start.84 = (bf16[144,2]{0,1:T(2,128)(2,1)S(1)}, bf16[144,2]{0,1:T(2,128)(2,1)}, u32[]{:S(2)}) copy-start(bf16[144,2]{0,1:T(2,128)(2,1)} %param.49) | copy-start | bytes 1732
  8.8 1071.8 %all-gather.16.cloned.1.call-start = ((), (), s32[]{:S(2)}) async-start(), calls=%async_computation.7 | async-start | bytes 14598144 | tf_op jit(solution)/shard_map/all_gather | solution.py:248
  9.5 360.3 %copy-start.21 = (bf16[1,256,1152]{2,1,0:T(8,128)(2,1)S(1)}, bf16[1,256,1152]{2,1,0:T(8,128)(2,1)}, u32[]{:S(2)}) copy-start(bf16[1,256,1152]{2,1,0:T(8,128)(2,1)} %param.35) | copy-start | bytes 1769476
  9.5 1094.8 %all-gather.18.cloned.1.call-start = ((), (), s32[]{:S(2)}) async-start(), calls=%async_computation.8 | async-start | bytes 14598144 | tf_op jit(solution)/shard_map/all_gather | solution.py:249
  10.3 357.3 %collective-permute-start = (s32[3]{0:T(128)S(1)}, s32[3]{0:T(128)S(1)}, u32[]{:S(2)}, u32[]{:S(2)}) collective-permute-start(s32[3]{0:T(128)S(1)} %slice_bitcast_fusion.56), channel_id=1, source_target_pairs={{0,1},{1,2},{2,3},{4,5},{5,6},{6,7},{8,9},{9,10},{10,11},{12,13},{... | collective-permute-start | bytes 44 | tf_op jit(solution)/shard_map/ppermute | solution.py:23
  15.3 2846.3 %all-reduce.25.cloned.1.call-start = ((), (), s32[]{:S(2)}) async-start(), calls=%async_computation.14 | async-start | bytes 185344 | tf_op jit(solution)/shard_map/psum | solution.py:396
  24.6 356.6 %copy-start.46 = (f32[1152]{0:T(1024)}, f32[1152]{0:T(1024)S(1)}, u32[]{:S(2)}) copy-start(f32[1152]{0:T(1024)S(1)} %get-tuple-element.1697) | copy-start | bytes 13828
  25.8 355.4 %copy-start.74 = (f32[256]{0:T(256)}, f32[256]{0:T(256)S(1)}, u32[]{:S(2)}) copy-start(f32[256]{0:T(256)S(1)} %add_rsqrt_fusion.1) | copy-start | bytes 3076
  207.5 185.3 %copy-start.26 = (bf16[72,2304]{0,1:T(8,128)(2,1)}, bf16[72,2304]{0,1:T(8,128)(2,1)S(1)}, u32[]{:S(2)}) copy-start(bf16[72,2304]{0,1:T(8,128)(2,1)S(1)} %all_gather.73) | copy-start | bytes 995332
  285.1 107.1 %copy-start.35 = (bf16[2304,104]{1,0:T(8,128)(2,1)}, bf16[2304,104]{1,0:T(8,128)(2,1)S(1)}, u32[]{:S(2)}) copy-start(bf16[2304,104]{1,0:T(8,128)(2,1)S(1)} %all_gather.72) | copy-start | bytes 1437700
  369.8 16.3 copy-start.66
  382.7 4.9 collective-permute-start.1
  392.2 752.8 %copy-start.4 = (bf16[256,2304]{1,0:T(8,128)(2,1)}, bf16[256,2304]{1,0:T(8,128)(2,1)S(1)}, u32[]{:S(2)}) copy-start(bf16[256,2304]{1,0:T(8,128)(2,1)S(1)} %get-tuple-element.1892) | copy-start | bytes 3538948
  1461.0 1249.3 %copy-start.45 = (f32[2304]{0:T(1024)S(1)}, f32[2304]{0:T(1024)}, u32[]{:S(2)}) copy-start(f32[2304]{0:T(1024)} %convert_element_type.182) | copy-start | bytes 27652
  2725.3 9.3 slice-start.2
  2728.4 6.0 collective-permute-start.2
  2739.6 224.9 %reduce-scatter.20.cloned.1.call-start = ((), (), s32[]{:S(2)}) async-start(), calls=%async_computation.12 | async-start | bytes 1216512
  2742.7 663.8 %all-reduce.27.cloned.1.call-start = ((), (), s32[]{:S(2)}) async-start(), calls=%async_computation.15 | async-start | bytes 56918016
  2796.2 712.3 %reduce-scatter.18.cloned.1.call-start = ((), (), s32[]{:S(2)}) async-start(), calls=%async_computation.11 | async-start | bytes 1216512
  2799.0 858.1 %reduce-scatter.22.cloned.1.call-start = ((), (), s32[]{:S(2)}) async-start(), calls=%async_computation.13 | async-start | bytes 10948608
  2806.1 1077.8 %reduce-scatter.14.cloned.1.call-start = ((), (), s32[]{:S(2)}) async-start(), calls=%async_computation.9 | async-start | bytes 21897216 | tf_op jit(solution)/shard_map/reduce_scatter | solution.py:384
  2819.2 1333.1 %reduce-scatter.16.cloned.1.call-start = ((), (), s32[]{:S(2)}) async-start(), calls=%async_computation.10 | async-start | bytes 29196288 | tf_op jit(solution)/shard_map/reduce_scatter | solution.py:393
  (77 other events, 265.6 us)
Sparse Core Ops, SparseCore 0:
  10.9 90.1 all-gather.11
  103.9 65.9 all-gather.13
  173.1 109.3 all-gather.15
  285.4 103.5 all-gather.17
  2739.8 121.7 all-reduce.24
  2867.3 97.2 reduce-scatter.19
  2972.7 433.7 all-reduce.26
  3412.9 95.5 reduce-scatter.17
  3516.2 140.9 reduce-scatter.21
  3665.2 218.7 reduce-scatter.13
  3890.9 261.3 reduce-scatter.15
where the time goes:
time: 4200 us; the launch traced here: 4160 us
  other arithmetic  1730 us (41%)
  waiting for transfers between devices  1310 us (31%)
  local copies, waits for them, and re-layouts  573 us (14%)
  blocking collectives  384 us (9%)
  matrix products  125 us (3%)
    unnamed x15, waiting for transfers between devices  784 us
    while x224, other arithmetic  358 us
    reduce_sum x64, other arithmetic, retreat_retreat(): delta_grad_t = weighted * inner_t + jnp.sum(through * decay_rate, 0)  308 us
    reduce_sum x160, other arithmetic, forward_advance(): return (state, jnp.sum(select_out[:, None] * state, 0))  278 us
    reduce_scatter x1, waiting for transfers between devices, per_device(): lax.psum_scatter(grad_up, ('dp', 'seq'), scatter_dimension=0, tiled=True)  268 us
    reduce_scatter x1, waiting for transfers between devices, per_device(): lax.psum_scatter(grad_in, ('dp', 'seq'), scatter_dimension=0, tiled=True)  227 us
    add x32, other arithmetic, advance_state(): return factor * state + select_in[:, None] * (delta_t * inner_t)[None, :]  177 us
    mul x32, other arithmetic, adjoint_retreat(): return (kept_t * jnp.exp(delta_t[None, :] * decay_rate) * adjoint, None)  172 us
  transfers between devices with their start and end apart: 14, of which 8 were waited for; matrix products, arithmetic and copies ran while one was open for 19% of the time, Pallas kernels for 0%

commit v1 on v0

v1 whole, which is shorter than its diff:
```python
import functools, math
import jax
import jax.numpy as jnp
from jax import lax
from jax.experimental import pallas as pl
from jax.experimental.pallas import tpu as pltpu
from jax.sharding import PartitionSpec as P

NS = 16
SEG = 8
LANE = 128
FAR = 1e30


def spread_columns(wide, columns):
    for n in range(NS):
        wide[n] = jnp.broadcast_to(columns[:, n : n + 1], wide.shape[1:])


def rows_of(i):
    return pl.ds(pl.multiple_of(i * SEG, SEG), SEG)


def rate_rows(rate):
    return [jnp.broadcast_to(rate[n : n + 1, :], (SEG, rate.shape[1])) for n in range(NS)]


def tiled_lanes(block, width):
    return block if width == LANE else jnp.concatenate([block] * (width // LANE), 1)


def prefix_pairs(decay, value, reverse):
    place = lax.broadcasted_iota(jnp.int32, decay.shape, 0)

    def shifted(array, by, fill):
        if reverse:
            return jnp.where(place < SEG - by, pltpu.roll(array, SEG - by, 0), fill)
        return jnp.where(place >= by, pltpu.roll(array, by, 0), fill)

    for by in (1, 2, 4):
        value = decay * shifted(value, by, 0.0) + value
        decay = decay * shifted(decay, by, 1.0)
    last = slice(0, 1) if reverse else slice(SEG - 1, SEG)
    return shifted(decay, 1, 1.0), shifted(value, 1, 0.0), decay[last], value[last]


def ends_kernel(
    reverse, delta, driven, kept, select, rate, pre_decay, pre_value, all_decay, all_value, wide
):
    @pl.when(pl.program_id(0) == 0)
    def _():
        spread_columns(wide, select)

    width = delta.shape[1]
    length = delta.shape[0] // SEG
    rates = rate_rows(rate)
    zero = jnp.zeros((SEG, width), jnp.float32)

    def step(k, carry):
        total, states = carry
        i = length - 1 - k if reverse else k
        rows = rows_of(i)
        reach = jnp.where(tiled_lanes(kept[rows, :], width) > 0, delta[rows, :], FAR)
        drive = driven[rows, :]
        new = []
        for n in range(NS):
            factor = jnp.exp2(reach * rates[n])
            term = drive * tiled_lanes(wide[n, rows, :], width)
            new.append(factor * (states[n] + term) if reverse else factor * states[n] + term)
        return total + reach, tuple(new)

    total, states = lax.fori_loop(0, length, step, (zero, (zero,) * NS))
    for n in range(NS):
        before_decay, before_value, whole_decay, whole_value = prefix_pairs(
            jnp.exp2(total * rates[n]), states[n], reverse
        )
        pre_decay[n] = before_decay
        pre_value[n] = before_value
        all_decay[n : n + 1, :] = whole_decay
        all_value[n : n + 1, :] = whole_value


def output_kernel(
    delta, driven, inner, gate, kept, in_select, out_select, rate, skip, pre_decay, pre_value,
    entry, scanned, gated, wide_in, wide_out,
):
    @pl.when(pl.program_id(0) == 0)
    def _():
        spread_columns(wide_in, in_select)
        spread_columns(wide_out, out_select)

    width = delta.shape[1]
    length = delta.shape[0] // SEG
    rates = rate_rows(rate)
    start = tuple(pre_decay[n] * entry[n : n + 1, :] + pre_value[n] for n in range(NS))

    def step(i, states):
        rows = rows_of(i)
        reach = jnp.where(tiled_lanes(kept[rows, :], width) > 0, delta[rows, :], FAR)
        drive = driven[rows, :]
        new, parts = [], [0.0] * 4
        for n in range(NS):
            state = jnp.exp2(reach * rates[n]) * states[n] + drive * tiled_lanes(
                wide_in[n, rows, :], width
            )
            parts[n % 4] = parts[n % 4] + state * tiled_lanes(wide_out[n, rows, :], width)
            new.append(state)
        scanned[rows, :] = (parts[0] + parts[1]) + (parts[2] + parts[3])
        return tuple(new)

    lax.fori_loop(0, length, step, start)
    value = scanned[...] + skip[...] * inner[...].astype(jnp.float32)
    scanned[...] = value
    half = gate[...].astype(jnp.float32)
    gated[...] = (value * (half * jax.nn.sigmoid(half))).astype(jnp.bfloat16)


def adjoint_kernel(
    delta, driven, inner, grad, kept, in_select, out_select, rate, pre_decay, pre_value, entry,
    post_decay, post_value, exit_, inner_grad, delta_grad, rate_sum, in_grad, out_grad,
    states, wide_in, wide_out, in_total, out_total,
):
    j = pl.program_id(0)

    @pl.when(j == 0)
    def _():
        spread_columns(wide_in, in_select)
        spread_columns(wide_out, out_select)
        in_total[...] = jnp.zeros_like(in_total)
        out_total[...] = jnp.zeros_like(out_total)

    width = delta.shape[1]
    length = delta.shape[0] // SEG
    rates = rate_rows(rate)
    start = tuple(pre_decay[n] * entry[n : n + 1, :] + pre_value[n] for n in range(NS))

    def folded(value):
        return sum(value[:, k : k + LANE] for k in range(0, width, LANE))

    def advance(i, carry):
        rows = rows_of(i)
        reach = jnp.where(tiled_lanes(kept[rows, :], width) > 0, delta[rows, :], FAR)
        drive, grad_t = driven[rows, :], grad[rows, :]
        new = []
        for n in range(NS):
            states[i, n] = carry[n]
            state = jnp.exp2(reach * rates[n]) * carry[n] + drive * tiled_lanes(
                wide_in[n, rows, :], width
            )
            out_total[n, rows, :] = out_total[n, rows, :] + folded(grad_t * state)
            new.append(state)
        return tuple(new)

    lax.fori_loop(0, length, advance, start)
    back = tuple(post_decay[n] * exit_[n : n + 1, :] + post_value[n] for n in range(NS))
    zero = jnp.zeros((SEG, width), jnp.float32)

    def retreat(k, carry):
        backs, sums = carry
        i = length - 1 - k
        rows = rows_of(i)
        step_t = delta[rows, :]
        reach = jnp.where(tiled_lanes(kept[rows, :], width) > 0, step_t, FAR)
        drive, grad_t = driven[rows, :], grad[rows, :]
        new_backs, new_sums = [], []
        weighted, slope = [0.0] * 2, [0.0] * 2
        for n in range(NS):
            adjoint = grad_t * tiled_lanes(wide_out[n, rows, :], width) + backs[n]
            passed = jnp.exp2(reach * rates[n]) * adjoint
            through = passed * states[i, n]
            weighted[n % 2] = weighted[n % 2] + adjoint * tiled_lanes(wide_in[n, rows, :], width)
            slope[n % 2] = slope[n % 2] + through * rates[n]
            in_total[n, rows, :] = in_total[n, rows, :] + folded(adjoint * drive)
            new_backs.append(passed)
            new_sums.append(sums[n] + through * step_t)
        all_weighted = weighted[0] + weighted[1]
        inner_grad[rows, :] = all_weighted * step_t
        delta_grad[rows, :] = all_weighted * inner[rows, :] + (slope[0] + slope[1]) * math.log(2.0)
        return tuple(new_backs), tuple(new_sums)

    _, sums = lax.fori_loop(0, length, retreat, (back, (zero,) * NS))
    for n in range(NS):
        rate_sum[n : n + 1, :] = jnp.sum(sums[n], 0, keepdims=True)

    @pl.when(j == pl.num_programs(0) - 1)
    def _():
        place = lax.broadcasted_iota(jnp.int32, in_grad.shape, 1)
        for total, result in ((in_total, in_grad), (out_total, out_grad)):
            value = jnp.zeros(result.shape, jnp.float32)
            for n in range(NS):
                column = jnp.sum(total[n], 1, keepdims=True)
                value = jnp.where(place == n, column, value)
            result[...] = value


def column_specs(rows, width):
    return (
        pl.BlockSpec((rows, width), lambda j: (0, j)),
        pl.BlockSpec((rows, LANE), lambda j: (0, 0)),
        pl.BlockSpec((rows, NS), lambda j: (0, 0)),
        pl.BlockSpec((NS, width), lambda j: (0, j)),
        pl.BlockSpec((NS, SEG, width), lambda j: (0, 0, j)),
        pl.BlockSpec((1, width), lambda j: (0, j)),
    )


def params(mib):
    return pltpu.CompilerParams(
        dimension_semantics=("arbitrary",), vmem_limit_bytes=mib * 2**20
    )


def segment_ends(delta, driven, kept, select, rate, reverse, width=LANE):
    rows, channels = delta.shape
    block, flag, columns, state, segments, _ = column_specs(rows, width)
    return pl.pallas_call(
        functools.partial(ends_kernel, reverse),
        grid=(channels // width,),
        in_specs=[block, block, flag, columns, state],
        out_specs=[segments, segments, state, state],
        out_shape=[jax.ShapeDtypeStruct((NS, SEG, channels), jnp.float32)] * 2
        + [jax.ShapeDtypeStruct((NS, channels), jnp.float32)] * 2,
        scratch_shapes=[pltpu.VMEM((NS, rows, LANE), jnp.float32)],
        compiler_params=params(24),
    )(delta, driven, kept, select, rate)


def scan_output(
    delta, driven, inner, gate, kept, in_select, out_select, rate, skip, pre, entry, width=LANE
):
    rows, channels = delta.shape
    block, flag, columns, state, segments, line = column_specs(rows, width)
    wide = pltpu.VMEM((NS, rows, LANE), jnp.float32)
    return pl.pallas_call(
        output_kernel,
        grid=(channels // width,),
        in_specs=[block] * 4 + [flag, columns, columns, state, line, segments, segments, state],
        out_specs=[block, block],
        out_shape=[
            jax.ShapeDtypeStruct((rows, channels), jnp.float32),
            jax.ShapeDtypeStruct((rows, channels), jnp.bfloat16),
        ],
        scratch_shapes=[wide, wide],
        compiler_params=params(24),
    )(delta, driven, inner, gate, kept, in_select, out_select, rate, skip, *pre, entry)


def scan_adjoint(
    delta, driven, inner, grad, kept, in_select, out_select, rate, pre, entry, post, exit_,
    width=LANE,
):
    rows, channels = delta.shape
    block, flag, columns, state, segments, _ = column_specs(rows, width)
    wide = pltpu.VMEM((NS, rows, LANE), jnp.float32)
    return pl.pallas_call(
        adjoint_kernel,
        grid=(channels // width,),
        in_specs=[block] * 4
        + [flag, columns, columns, state, segments, segments, state, segments, segments, state],
        out_specs=[block, block, state, columns, columns],
        out_shape=[jax.ShapeDtypeStruct((rows, channels), jnp.float32)] * 2
        + [jax.ShapeDtypeStruct((NS, channels), jnp.float32)]
        + [jax.ShapeDtypeStruct((rows, NS), jnp.float32)] * 2,
        scratch_shapes=[
            pltpu.VMEM((rows // SEG, NS, SEG, width), jnp.float32),
            wide, wide, wide, wide,
        ],
        compiler_params=params(32),
    )(
        delta, driven, inner, grad, kept, in_select, out_select, rate, *pre, entry, *post, exit_
    )


MODEL_WIDTH = 1152
DI = 2304
R = 72
KC = 4
EXPERT_COUNT = 2
EPS = 1e-05
REACH = KC - 1
BOTH = ("dp", "seq")
HIGHEST = lax.Precision.HIGHEST
F32 = jnp.float32
BF16 = jnp.bfloat16


def passed_along(array, axis, by):
    size = lax.axis_size(axis)
    pairs = [(i, i + by) for i in range(size) if 0 <= i + by < size]
    return lax.ppermute(array, axis, pairs)


def interleave(array):
    split = array.reshape((SEG, array.shape[0] // SEG) + array.shape[1:])
    return split.swapaxes(0, 1).reshape(array.shape)


def in_order(array):
    split = array.reshape((array.shape[0] // SEG, SEG) + array.shape[1:])
    return split.swapaxes(0, 1).reshape(array.shape)


def with_earlier(array, earlier):
    last = array[array.shape[0] - REACH * SEG :].reshape((REACH, SEG) + array.shape[1:])
    front = jnp.concatenate([earlier[:, None], last[:, : SEG - 1]], 1)
    return jnp.concatenate([front.reshape((REACH * SEG,) + array.shape[1:]), array])


def entering(decay, value, reverse):
    size, mine = lax.axis_size("seq"), lax.axis_index("seq")
    gathered = lax.all_gather(jnp.stack([decay, value]).astype(BF16), "seq").astype(F32)
    state = jnp.zeros_like(value)
    for k in range(size):
        at = size - 1 - k if reverse else k
        reached = at > mine if reverse else at < mine
        state = jnp.where(reached, gathered[at, 0] * state + gathered[at, 1], state)
    return state


def silu_slope(value):
    logistic = jax.nn.sigmoid(value)
    return logistic * (1.0 + value * (1.0 - logistic))


def gelu_slope(value):
    return 0.5 * (1.0 + lax.erf(value / math.sqrt(2.0))) + value * jnp.exp(
        -0.5 * value * value
    ) / math.sqrt(2.0 * math.pi)


def dot(left, right, contract, precision=None):
    return lax.dot_general(
        left, right, (contract, ((), ())), precision=precision, preferred_element_type=F32
    )


def gathered(shard):
    return lax.all_gather(shard, BOTH, axis=0, tiled=True)


def scattered(whole):
    return lax.psum_scatter(whole.astype(BF16), BOTH, scatter_dimension=0, tiled=True).astype(F32)


def per_device(
    tokens,
    doc_ids,
    token_expert,
    out_grad,
    norm_gains,
    in_proj,
    conv_weight,
    conv_bias,
    select_proj,
    step_proj,
    step_bias,
    decay_log,
    skip_gain,
    out_proj,
    router,
    expert_up,
    expert_down,
):
    rows = tokens.shape[1]
    slots_per = 5 * rows // (4 * EXPERT_COUNT)
    slots = EXPERT_COUNT * slots_per
    wide = DI // 6

    prior_tokens = passed_along(tokens[0, rows - REACH :], "seq", 1)
    prior_doc = passed_along(doc_ids[0, rows - REACH :], "seq", 1)
    lines = lax.all_gather(jnp.concatenate([norm_gains, router.T]), "dp", axis=1, tiled=True)
    gains_all = lines[:2].astype(F32)
    router_all = lines[2:].astype(F32)

    in_full = gathered(in_proj.T)
    small = jnp.concatenate(
        [
            select_proj,
            step_proj.T,
            decay_log,
            conv_weight.T,
            conv_bias[:, None],
            step_bias[:, None],
            skip_gain[:, None],
        ],
        1,
    )
    small_full = gathered(small)
    select_full = small_full[:, : R + 2 * NS]
    step_full = small_full[:, R + 2 * NS : 2 * R + 2 * NS]
    line_full = small_full[:, 2 * R + 2 * NS :].astype(F32).T
    decay_rate = -jnp.exp(line_full[:NS])
    conv_taps = line_full[NS : NS + KC]
    bias_conv, bias_step, skip_wide = (line_full[NS + KC + k][None] for k in range(3))
    out_full = gathered(out_proj)
    up_full = [gathered(expert_up[e].T) for e in range(EXPERT_COUNT)]
    down_full = [gathered(expert_down[e]) for e in range(EXPERT_COUNT)]

    mine = interleave(tokens[0])
    doc_row = interleave(doc_ids[0])
    route = interleave(token_expert[0, :, 0])
    out_cot = interleave(out_grad[0]).astype(F32)

    extended = jnp.concatenate([mine, prior_tokens, jnp.zeros_like(mine[: SEG - REACH])])
    stream_ext = extended.astype(F32)
    inv_ext = lax.rsqrt(jnp.mean(stream_ext * stream_ext, -1, keepdims=True) + EPS)
    hat_ext = stream_ext * inv_ext
    normed_ext = (hat_ext * gains_all[0]).astype(BF16)
    stream, inv_first, hat_first, normed = (
        a[:rows] for a in (stream_ext, inv_ext, hat_ext, normed_ext)
    )
    proj_ext = dot(normed_ext, in_full, ((1,), (1,))).astype(BF16)
    front = proj_ext[:rows, :DI]
    gate = proj_ext[:rows, DI:]
    ext_ids = with_earlier(doc_row, prior_doc)
    ext_rows = with_earlier(front.astype(F32), proj_ext[rows : rows + REACH, :DI].astype(F32))
    masks = [(ext_ids[k * SEG : k * SEG + rows] == doc_row)[:, None] for k in range(KC)]
    taps = [jnp.where(masks[k], ext_rows[k * SEG : k * SEG + rows], 0.0) for k in range(KC)]
    conv_sum = bias_conv
    for k in range(KC):
        conv_sum = conv_sum + conv_taps[k][None] * taps[k]
    inner = jax.nn.silu(conv_sum).astype(BF16)
    inner_wide = inner.astype(F32)
    select = dot(inner, select_full, ((1,), (0,)))
    steps_low = select[:, :R].astype(BF16)
    in_select = select[:, R : R + NS]
    out_select = select[:, R + NS :]
    step_pre = dot(steps_low, step_full, ((1,), (1,))) + bias_step
    delta = jax.nn.softplus(step_pre)
    driven = delta * inner_wide
    kept = jnp.broadcast_to(masks[REACH - 1].astype(F32), (rows, LANE))
    rate = decay_rate * math.log2(math.e)

    *pre, all_decay, all_state = segment_ends(delta, driven, kept, in_select, rate, False, wide)
    state_in = entering(all_decay, all_state, False)
    scanned, gated = scan_output(
        delta, driven, inner, gate, kept, in_select, out_select, rate, skip_wide, pre, state_in, wide
    )
    mixed = dot(gated, out_full, ((1,), (0,)))
    resid = stream + mixed
    inv_second = lax.rsqrt(jnp.mean(resid * resid, -1, keepdims=True) + EPS)
    hat_second = resid * inv_second
    normed_moe = (hat_second * gains_all[1]).astype(BF16)
    normed_wide = normed_moe.astype(F32)
    logits = dot(normed_wide, router_all, ((1,), (1,)), HIGHEST)
    probs = jax.nn.softmax(logits, -1)
    route_hot = route[:, None] == jnp.arange(EXPERT_COUNT, dtype=jnp.int32)[None, :]
    hot_wide = route_hot.astype(F32)
    chosen = jnp.sum(probs * hot_wide, 1, keepdims=True)
    place = jnp.arange(rows, dtype=jnp.int32)
    lower = (place[:, None] >= place[None, :]).astype(BF16)
    rank_in = dot(lower, route_hot.astype(BF16), ((1,), (0,))) - 1.0
    slot = jnp.sum(rank_in * hot_wide, 1).astype(jnp.int32)
    target = route * slots_per + slot
    pick = (jnp.arange(slots, dtype=jnp.int32)[:, None] == target[None, :]).astype(BF16)

    def to_slots(values):
        placed = dot(pick, values, ((1,), (0,))).astype(BF16)
        return [placed[e * slots_per : (e + 1) * slots_per] for e in range(EXPERT_COUNT)]

    def from_slots(parts):
        return dot(pick.astype(F32), jnp.concatenate(parts), ((0,), (0,)), HIGHEST)

    buffers = to_slots(normed_moe)
    hidden = [dot(buffers[e], up_full[e], ((1,), (1,))) for e in range(EXPERT_COUNT)]
    active = [jax.nn.gelu(h, approximate=False).astype(BF16) for h in hidden]
    returned = from_slots(
        [dot(active[e], down_full[e], ((1,), (0,))) for e in range(EXPERT_COUNT)]
    )
    branch = chosen * returned
    layer_out = (resid + branch).astype(BF16)
    squared_values = jnp.stack(
        [jnp.sum(resid * resid), jnp.sum(mixed * mixed), jnp.sum(branch * branch)]
    )
    chosen_grad = jnp.sum(out_cot * returned, 1, keepdims=True)
    returned_grad = to_slots((chosen * out_cot).astype(BF16))
    grad_down = [dot(active[e], returned_grad[e], ((0,), (0,))) for e in range(EXPERT_COUNT)]
    active_grad = [
        dot(returned_grad[e], down_full[e], ((1,), (1,))) for e in range(EXPERT_COUNT)
    ]
    hidden_grad = [
        (active_grad[e] * gelu_slope(hidden[e])).astype(BF16) for e in range(EXPERT_COUNT)
    ]
    grad_up = [dot(hidden_grad[e], buffers[e], ((0,), (0,))) for e in range(EXPERT_COUNT)]
    expert_sums = [scattered(g) for g in (*grad_down, *grad_up)]
    buffer_grad = from_slots(
        [dot(hidden_grad[e], up_full[e], ((1,), (0,))) for e in range(EXPERT_COUNT)]
    )
    logit_grad = chosen_grad * chosen * (hot_wide - probs)
    grad_router = dot(logit_grad, normed_wide, ((0,), (0,)), HIGHEST)
    moe_grad = buffer_grad + dot(logit_grad, router_all, ((1,), (0,)), HIGHEST)
    second_gain_grad = jnp.sum(moe_grad * hat_second, 0)
    scaled_second = moe_grad * gains_all[1]
    resid_grad = out_cot + inv_second * (
        scaled_second - hat_second * jnp.mean(scaled_second * hat_second, -1, keepdims=True)
    )
    mixed_grad = resid_grad.astype(BF16)
    grad_out = dot(gated, mixed_grad, ((0,), (0,)))
    out_sum = scattered(grad_out)
    gated_grad = dot(mixed_grad, out_full, ((1,), (1,)))
    gate_half = gate.astype(F32)
    scan_grad = gated_grad * jax.nn.silu(gate_half)
    gate_grad = gated_grad * scanned * silu_slope(gate_half)
    grad_skip = jnp.sum(scan_grad * inner_wide, 0)
    *post, back_decay, back_adjoint = segment_ends(
        delta, scan_grad, kept, out_select, rate, True, wide
    )
    adjoint_in = entering(back_decay, back_adjoint, True)
    inner_scan_grad, delta_grad, rate_sum, in_select_grad, out_select_grad = scan_adjoint(
        delta, driven, inner_wide, scan_grad, kept, in_select, out_select, rate, pre, state_in,
        post, adjoint_in, wide,
    )
    grad_decay = rate_sum * decay_rate
    pre_grad = delta_grad * jax.nn.sigmoid(step_pre)
    grad_step_bias = jnp.sum(pre_grad, 0)
    pre_low = pre_grad.astype(BF16)
    grad_step = dot(pre_low, steps_low, ((0,), (0,)))
    steps_grad = dot(pre_low, step_full, ((1,), (0,)))
    select_low = jnp.concatenate([steps_grad, in_select_grad, out_select_grad], 1).astype(BF16)
    grad_select = dot(inner, select_low, ((0,), (0,)))
    inner_grad = (
        scan_grad * skip_wide + inner_scan_grad + dot(select_low, select_full, ((1,), (1,)))
    )
    conv_back = inner_grad * silu_slope(conv_sum)
    grad_lines = jnp.concatenate(
        [
            grad_decay,
            jnp.stack(
                [jnp.sum(conv_back * taps[k], 0) for k in range(KC)]
                + [jnp.sum(conv_back, 0), grad_step_bias, grad_skip]
            ),
        ]
    )
    ext_grad = sum(
        jnp.pad(
            jnp.where(masks[k], conv_back * conv_taps[k][None], 0.0),
            ((k * SEG, (REACH - k) * SEG), (0, 0)),
        )
        for k in range(KC)
    )
    early = ext_grad[: REACH * SEG].reshape(REACH, SEG, DI)
    incoming = passed_along(early[:, 0], "seq", -1)
    tail = jnp.concatenate([early[:, 1:], incoming[:, None]], 1).reshape(REACH * SEG, DI)
    front_grad = ext_grad[REACH * SEG :] + jnp.pad(tail, ((rows - REACH * SEG, 0), (0, 0)))
    proj_grad = jnp.concatenate([front_grad, gate_grad], 1).astype(BF16)
    grad_in = dot(proj_grad, normed, ((0,), (0,)))
    in_sum = scattered(grad_in)
    normed_grad = dot(proj_grad, in_full, ((1,), (0,)))
    first_gain_grad = jnp.sum(normed_grad * hat_first, 0)
    scaled_first = normed_grad * gains_all[0]
    stream_grad = resid_grad + inv_first * (
        scaled_first - hat_first * jnp.mean(scaled_first * hat_first, -1, keepdims=True)
    )

    parts = lax.axis_size("dp")
    repeats = lax.axis_size("seq")
    grad_small = jnp.concatenate([grad_select, grad_step, grad_lines.T], 1)
    columns = grad_small.shape[1]
    unit = DI // (parts * repeats)
    shared = jnp.concatenate([first_gain_grad[None], second_gain_grad[None], grad_router])
    width = MODEL_WIDTH // parts
    shared = shared.reshape(4, parts, width).swapaxes(0, 1).reshape(parts, 1, 4 * width)
    extra = -(-4 * width // unit)
    shared = jnp.pad(shared, ((0, 0), (0, 0), (0, extra * unit - 4 * width)))
    shared = jnp.broadcast_to(shared, (parts, repeats, extra * unit)).reshape(DI, extra)
    small_sum = lax.psum_scatter(
        jnp.concatenate([grad_small, shared], 1), BOTH, scatter_dimension=0, tiled=True
    )
    shared_sum = small_sum[:, columns:].reshape(extra * unit)[: 4 * width].reshape(4, width)
    at = R + 2 * NS
    square_total = lax.psum(squared_values, BOTH)
    stats = jnp.sqrt(square_total / (rows * parts * repeats * MODEL_WIDTH))
    line_sum = small_sum[:, at + R : columns]
    return (
        in_order(layer_out)[None],
        in_order(stream_grad.astype(BF16))[None],
        shared_sum[:2],
        in_sum.T,
        line_sum[:, NS : NS + KC].T,
        line_sum[:, NS + KC],
        small_sum[:, :at],
        small_sum[:, at : at + R].T,
        line_sum[:, NS + KC + 1],
        line_sum[:, :NS],
        line_sum[:, NS + KC + 2],
        out_sum,
        shared_sum[2:].T,
        jnp.stack([s.T for s in expert_sums[EXPERT_COUNT:]]),
        jnp.stack(expert_sums[:EXPERT_COUNT]),
        stats,
    )


def solution(mesh):
    return jax.shard_map(
        per_device,
        mesh=mesh,
        in_specs=(
            P("dp", "seq", None),
            P("dp", "seq"),
            P("dp", "seq", None),
            P("dp", "seq", None),
            P(None, "dp"),
            P(None, ("dp", "seq")),
            P(None, ("dp", "seq")),
            P(("dp", "seq")),
            P(("dp", "seq"), None),
            P(None, ("dp", "seq")),
            P(("dp", "seq")),
            P(("dp", "seq"), None),
            P(("dp", "seq")),
            P(("dp", "seq"), None),
            P("dp", None),
            P(None, None, ("dp", "seq")),
            P(None, ("dp", "seq"), None),
        ),
        out_specs=(
            P("dp", "seq", None),
            P("dp", "seq", None),
            P(None, "dp"),
            P(None, ("dp", "seq")),
            P(None, ("dp", "seq")),
            P(("dp", "seq")),
            P(("dp", "seq"), None),
            P(None, ("dp", "seq")),
            P(("dp", "seq")),
            P(("dp", "seq"), None),
            P(("dp", "seq")),
            P(("dp", "seq"), None),
            P("dp", None),
            P(None, None, ("dp", "seq")),
            P(None, ("dp", "seq"), None),
            P(),
        ),
        check_vma=False,
    )
```

time: 4200 us -> 1500 us (0.36)
  other arithmetic: 1730 us -> 31.2 us
  local copies, waits for them, and re-layouts: 573 us -> 48.9 us
  waiting for transfers between devices: 1310 us -> 983 us
  blocking collectives: 384 us -> 175 us
  Pallas kernels: 0 us -> 84.5 us
    reduce_sum x328 -> x2, other arithmetic: 719 us -> 0.93 us  [the longest x1 0.59 us: per_device(): chosen = jnp.sum(probs * hot_wide, 1, keepdims=True)]
    unnamed x15, waiting for transfers between devices: 784 us -> 112 us
    while x224 -> x0, other arithmetic: 358 us -> none
    add x130 -> x2, other arithmetic: 320 us -> 0.54 us  [the longest x1 0.54 us: per_device(): sum((jnp.pad(jnp.where(masks[k], conv_back * conv_taps[k][None], 0.0), ((...]
    slice x399 -> x17, local copies, waits for them, and re-layouts: 306 us -> 10.6 us  [the longest x1 1.84 us: per_device(): down_full = [gathered(expert_down[e]) for e in range(EXPERT_COUNT)]]
    all_gather x4 -> x6, waiting for transfers between devices: 0.04 us -> 229 us  [gathered(): return lax.all_gather(shard, BOTH, axis=0, tiled=True)]
    all_gather x9 -> x4, blocking collectives: 346 us -> 136 us  [the longest x1 91.6 us: gathered(): return lax.all_gather(shard, BOTH, axis=0, tiled=True)]
    mul x1089 -> x4, other arithmetic: 182 us -> 2 us  [the longest x1 1.29 us: per_device(): hat_ext = stream_ext * inv_ext]
  transfers between devices with their start and end apart: 14 -> 16, of which waited for: 8 -> 12; matrix products, arithmetic and copies ran while one was open for 19% -> 9% of each run, Pallas kernels for 0% -> 2%
where the time goes in v1:
time: 1500 us; the launch traced here: 1490 us
  waiting for transfers between devices  983 us (66%)
  blocking collectives  175 us (12%)
  matrix products  144 us (10%)
  Pallas kernels  84.5 us (6%)
  local copies, waits for them, and re-layouts  48.9 us (3%)
  other arithmetic  31.2 us (2%)
  between operations  16 us (1%)
    reduce_scatter x5, waiting for transfers between devices, scattered(): lax.psum_scatter(whole.astype(BF16), BOTH, scatter_dimension=0, tiled=True)  640 us
    all_gather x6, waiting for transfers between devices, gathered(): return lax.all_gather(shard, BOTH, axis=0, tiled=True)  229 us
    dot_general x32, matrix products, dot(): lax.dot_general(left, right, (contract, ((), ())), precision=precision, p...  144 us
    unnamed x15, waiting for transfers between devices  112 us
    all_gather x1, blocking collectives, gathered(): return lax.all_gather(shard, BOTH, axis=0, tiled=True)  91.6 us
    pallas_call x1, Pallas kernels, scan_adjoint(): pl.pallas_call(adjoint_kernel, grid=(channels // width,), in_specs=[block...  45.5 us
    psum x1, blocking collectives, per_device(): square_total = lax.psum(squared_values, BOTH)  38.7 us
    all_gather x2, blocking collectives, entering(): lax.all_gather(jnp.stack([decay, value]).astype(BF16), 'seq').astype(F32)  35.8 us
  transfers between devices with their start and end apart: 16, of which 12 were waited for; matrix products, arithmetic and copies ran while one was open for 9% of the time, Pallas kernels for 2%

profile of v1, /device:TPU:0, one launch (start us, length us, event | category | flops | bytes accessed | tf_op | source)
XLA Modules:
  0.0 1492.8 jit_solution(6874119497344563949)
XLA Ops:
  24.1 91.6 %all_gather.32 = bf16[2304,199]{1,0:T(8,128)(2,1)S(1)} all-gather(bf16[72,199]{1,0:T(8,128)(2,1)S(1)} %concatenate.71), channel_id=1, replica_groups=mesh['dp'=8,'seq'=4] {'dp','seq'}, dimensions={0}, use_global_device_ids=true | all-gather | bytes 945648 | tf_op jit(solution)/shard_map/all_gather | solution.py:338
  119.2 9.1 all-gather.2
  134.3 12.1 convolution_convert_fusion.6
  159.6 12.0 shard_map.288
  171.7 19.1 %all_gather.35 = bf16[4,2,16,2304]{3,2,1,0:T(8,128)(2,1)S(1)} all-gather(bf16[1,2,16,2304]{3,2,1,0:T(8,128)(2,1)S(1)} %pad_maximum_fusion.5), channel_id=1, replica_groups=mesh['dp'=8,'seq'=4] {'seq'}, dimensions={0}, use_global_device_ids=true | all-gather | bytes 737280 | tf_op jit(solution)/shard_map/all_gather | solution.py:311
  191.0 15.4 %shard_map.289 = (f32[256,2304]{1,0:T(8,128)S(1)}, bf16[256,2304]{1,0:T(8,128)(2,1)S(1)}) custom-call(f32[256,2304]{1,0:T(8,128)S(1)} %get-tuple-element.139.delta, f32[256,2304]{1,0:T(8,128)S(1)} %get-tuple-element.138.driven, bf16[256,2304]{1,0:T(8,128)(2,1)S(1)} %get-tuple-element.123.inner, bf16[256,2304]{1,0:T(8,128)(2,1)S(1)} %copy-done.9, ...), custom_call_target="tpu_custom_call" | custom-call | tf_op jit(solution)/shard_map/pallas_call | solution.py:234
  209.5 5.6 multiply_reduce_fusion.13
  220.3 40.2 %all-gather.16.cloned.1.call-done = bf16[3072,1152]{1,0:T(8,128)(2,1)} async-done(((bf16[96,1152]{1,0:T(8,128)(2,1)}), bf16[3072,1152]{1,0:T(8,128)(2,1)}) %all-gather.16.cloned.1.call-update) | async-done | bytes 7077904 | tf_op jit(solution)/shard_map/all_gather | solution.py:338
  260.5 9.3 fusion.40
  269.8 65.2 %all-gather.20.cloned.1.call-done = bf16[1,3072,1152]{2,1,0:T(8,128)(2,1)} async-done(((bf16[1,96,1152]{2,1,0:T(8,128)(2,1)}), bf16[1,3072,1152]{2,1,0:T(8,128)(2,1)}) %all-gather.20.cloned.1.call-update) | async-done | bytes 7077904 | tf_op jit(solution)/shard_map/all_gather | solution.py:338
  335.0 5.6 fusion.2
  340.6 68.8 %all-gather.14.cloned.1.call-done = bf16[3072,1152]{1,0:T(8,128)(2,1)} async-done(((bf16[96,1152]{1,0:T(8,128)(2,1)}), bf16[3072,1152]{1,0:T(8,128)(2,1)}) %all-gather.14.cloned.1.call-update) | async-done | bytes 7077904 | tf_op jit(solution)/shard_map/all_gather | solution.py:338
  409.5 19.3 %fusion.37 = (bf16[160,3072]{1,0:T(8,128)(2,1)}, f32[160,3072]{1,0:T(8,128)}) fusion(bf16[3072,1152]{1,0:T(8,128)(2,1)} %all-gather.14.cloned.1.call-done, bf16[320,1152]{1,0:T(8,128)(2,1)} %convolution_convert_fusion.8), kind=kOutput, calls=%fused_computation.69 | convolution fusion | flops 1164410880 | bytes 10395648 | tf_op jit(solution)/shard_map/dot_general | solution.py:332
  428.8 55.1 %all-gather.18.cloned.1.call-done = bf16[1,3072,1152]{2,1,0:T(8,128)(2,1)} async-done(((bf16[1,96,1152]{2,1,0:T(8,128)(2,1)}), bf16[1,3072,1152]{2,1,0:T(8,128)(2,1)}) %all-gather.18.cloned.1.call-update) | async-done | bytes 7077904 | tf_op jit(solution)/shard_map/all_gather | solution.py:338
  508.5 5.2 multiply_reduce_fusion
  513.8 11.6 shard_map.290
  525.5 16.7 %all_gather.41 = bf16[4,2,16,2304]{3,2,1,0:T(8,128)(2,1)S(1)} all-gather(bf16[1,2,16,2304]{3,2,1,0:T(8,128)(2,1)S(1)} %pad_maximum_fusion.6), channel_id=1, replica_groups=mesh['dp'=8,'seq'=4] {'seq'}, dimensions={0}, use_global_device_ids=true | all-gather | bytes 737280 | tf_op jit(solution)/shard_map/all_gather | solution.py:311
  542.4 45.5 %shard_map.291 = (f32[256,2304]{1,0:T(8,128)S(1)}, f32[256,2304]{1,0:T(8,128)S(1)}, f32[16,2304]{1,0:T(8,128)S(1)}, f32[256,16]{1,0:T(8,128)S(1)}, f32[256,16]{1,0:T(8,128)S(1)}) custom-call(f32[256,2304]{1,0:T(8,128)S(1)} %get-tuple-element.139.delta, f32[256,2304]{1,0:T(8,128)S(1)} %copy-done.1, f32[256,2304]{1,0:T(8,128)S(1)} %copy-done.4, ...), custom_call_target="tpu_custom_call" | custom-call | tf_op jit(solution)/shard_map/pallas_call | solution.py:255
  600.2 8.2 fusion.146
  617.5 8.9 multiply_reduce_fusion.9
  638.3 5.1 convolution_convert_fusion.4
  644.7 5.2 convolution_convert_fusion.3
  651.3 5.1 convolution_convert_fusion.2
  664.2 8.6 convolution_convert_fusion
  675.0 38.7 %psum.7 = f32[3]{0:T(128)S(1)} all-reduce(f32[3]{0:T(128)S(1)} %pad_maximum_fusion.10), channel_id=1, replica_groups=mesh['dp'=8,'seq'=4] {'dp','seq'}, use_global_device_ids=true, to_apply=%region_28.29 | all-reduce | flops 3 | bytes 24 | tf_op jit(solution)/shard_map/psum | solution.py:571
  717.6 11.0 reduce-scatter.22.cloned.1.call-done
  739.5 98.5 %reduce-scatter.24.cloned.1.call-done = bf16[72,1152]{1,0:T(8,128)(2,1)} async-done(((bf16[2304,1152]{1,0:T(8,128)(2,1)}), bf16[72,1152]{1,0:T(8,128)(2,1)}) %reduce-scatter.24.cloned.1.call-update) | async-done | bytes 165904
  839.7 123.3 %reduce-scatter.14.cloned.1.call-done = bf16[96,1152]{1,0:T(8,128)(2,1)} async-done(((bf16[3072,1152]{1,0:T(8,128)(2,1)}), bf16[96,1152]{1,0:T(8,128)(2,1)}) %reduce-scatter.14.cloned.1.call-update) | async-done | bytes 221200 | tf_op jit(solution)/shard_map/reduce_scatter | solution.py:342
  963.0 124.0 %reduce-scatter.16.cloned.1.call-done = bf16[96,1152]{1,0:T(8,128)(2,1)} async-done(((bf16[3072,1152]{1,0:T(8,128)(2,1)}), bf16[96,1152]{1,0:T(8,128)(2,1)}) %reduce-scatter.16.cloned.1.call-update) | async-done | bytes 221200 | tf_op jit(solution)/shard_map/reduce_scatter | solution.py:342
  1089.0 122.9 %reduce-scatter.18.cloned.1.call-done = bf16[96,1152]{1,0:T(8,128)(2,1)} async-done(((bf16[3072,1152]{1,0:T(8,128)(2,1)}), bf16[96,1152]{1,0:T(8,128)(2,1)}) %reduce-scatter.18.cloned.1.call-update) | async-done | bytes 221200 | tf_op jit(solution)/shard_map/reduce_scatter | solution.py:342
  1211.9 124.1 %reduce-scatter.20.cloned.1.call-done = bf16[96,1152]{1,0:T(8,128)(2,1)} async-done(((bf16[3072,1152]{1,0:T(8,128)(2,1)}), bf16[96,1152]{1,0:T(8,128)(2,1)}) %reduce-scatter.20.cloned.1.call-update) | async-done | bytes 221200 | tf_op jit(solution)/shard_map/reduce_scatter | solution.py:342
  1338.0 146.2 %reduce-scatter.12.cloned.1.call-done = bf16[144,1152]{1,0:T(8,128)(2,1)} async-done(((bf16[4608,1152]{1,0:T(8,128)(2,1)}), bf16[144,1152]{1,0:T(8,128)(2,1)}) %reduce-scatter.12.cloned.1.call-update) | async-done | bytes 331792 | tf_op jit(solution)/shard_map/reduce_scatter | solution.py:342
  (458 shorter events, 139.6 us)
Async XLA Ops:
  7.3 127.0 %all-gather.10.cloned.1.call-start = ((), (), s32[]{:S(2)}) async-start(), calls=%async_computation.7 | async-start | bytes 10948608 | tf_op jit(solution)/shard_map/all_gather | solution.py:338
  8.0 201.5 %all-gather.12.cloned.1.call-start = ((), (), s32[]{:S(2)}) async-start(), calls=%async_computation.8 | async-start | bytes 5474304 | tf_op jit(solution)/shard_map/all_gather | solution.py:338
  8.8 251.8 %all-gather.16.cloned.1.call-start = ((), (), s32[]{:S(2)}) async-start(), calls=%async_computation.10 | async-start | bytes 7299072 | tf_op jit(solution)/shard_map/all_gather | solution.py:338
  10.7 324.3 %all-gather.20.cloned.1.call-start = ((), (), s32[]{:S(2)}) async-start(), calls=%async_computation.17 | async-start | bytes 7299072 | tf_op jit(solution)/shard_map/all_gather | solution.py:338
  12.6 396.9 %all-gather.14.cloned.1.call-start = ((), (), s32[]{:S(2)}) async-start(), calls=%async_computation.9 | async-start | bytes 7299072 | tf_op jit(solution)/shard_map/all_gather | solution.py:338
  13.2 470.7 %all-gather.18.cloned.1.call-start = ((), (), s32[]{:S(2)}) async-start(), calls=%async_computation.16 | async-start | bytes 7299072 | tf_op jit(solution)/shard_map/all_gather | solution.py:338
  13.3 117.1 %collective-permute-start.1 = (s32[3]{0:T(128)S(1)}, s32[3]{0:T(128)S(1)}, u32[]{:S(2)}, u32[]{:S(2)}) collective-permute-start(s32[3]{0:T(128)S(1)} %slice_bitcast_fusion.17), channel_id=1, source_target_pairs={{0,1},{1,2},{2,3},{4,5},{5,6},{6,7},{8,9},{9,10},{10,11},{12,13},{... | collective-permute-start | bytes 44 | tf_op jit(solution)/shard_map/ppermute | solution.py:290
  18.2 113.2 %collective-permute-start = (bf16[3,1152]{1,0:T(4,128)(2,1)S(1)}, bf16[3,1152]{1,0:T(4,128)(2,1)S(1)}, u32[]{:S(2)}, u32[]{:S(2)}) collective-permute-start(bf16[3,1152]{1,0:T(4,128)(2,1)S(1)} %slice_bitcast_fusion.16), channel_id=1, source_target_pairs={{0,1},{1,2},{2,3},{4,5},{5,6},{6,7},{8,9},{9,10},{10,11},{12,13},{... | collective-permute-start | bytes 20744 | tf_op jit(solution)/shard_map/ppermute | solution.py:290
  21.8 706.7 %reduce-scatter.22.cloned.1.call-start = ((), (), s32[]{:S(2)}) async-start(), calls=%async_computation.18 | async-start | bytes 2433024
  24.1 93.6 %copy-start.119 = (s32[1,256,1]{1,2,0:T(1,128)S(1)}, s32[1,256,1]{1,2,0:T(1,128)}, u32[]{:S(2)}) copy-start(s32[1,256,1]{1,2,0:T(1,128)} %param.19) | copy-start | bytes 3076
  24.1 94.7 %copy-start.121 = (bf16[144,2]{0,1:T(2,128)(2,1)S(1)}, bf16[144,2]{0,1:T(2,128)(2,1)}, u32[]{:S(2)}) copy-start(bf16[144,2]{0,1:T(2,128)(2,1)} %param.31) | copy-start | bytes 1732
  24.1 94.7 %copy-start.122 = (bf16[2,144]{1,0:T(2,128)(2,1)S(1)}, bf16[2,144]{1,0:T(2,128)(2,1)}, u32[]{:S(2)}) copy-start(bf16[2,144]{1,0:T(2,128)(2,1)} %param.21) | copy-start | bytes 1732
  115.8 36.5 %copy-start.33 = (bf16[2304,199]{1,0:T(8,128)(2,1)}, bf16[2304,199]{1,0:T(8,128)(2,1)S(1)}, u32[]{:S(2)}) copy-start(bf16[2304,199]{1,0:T(8,128)(2,1)S(1)} %all_gather.32) | copy-start | bytes 2750980
  117.0 31.4 %copy-start.78 = (f32[2304]{0:T(1024)}, f32[2304]{0:T(1024)S(1)}, u32[]{:S(2)}) copy-start(f32[2304]{0:T(1024)S(1)} %get-tuple-element.111) | copy-start | bytes 27652
  117.0 31.4 %copy-start.80 = (f32[2304]{0:T(1024)}, f32[2304]{0:T(1024)S(1)}, u32[]{:S(2)}) copy-start(f32[2304]{0:T(1024)S(1)} %get-tuple-element.112) | copy-start | bytes 27652
  117.0 31.5 %copy-start.82 = (f32[2304]{0:T(1024)}, f32[2304]{0:T(1024)S(1)}, u32[]{:S(2)}) copy-start(f32[2304]{0:T(1024)S(1)} %get-tuple-element.113) | copy-start | bytes 27652
  117.0 31.5 %copy-start.84 = (f32[2304]{0:T(1024)}, f32[2304]{0:T(1024)S(1)}, u32[]{:S(2)}) copy-start(f32[2304]{0:T(1024)S(1)} %get-tuple-element.114) | copy-start | bytes 27652
  159.5 31.4 %copy-start = (f32[256,2304]{1,0:T(8,128)}, f32[256,2304]{1,0:T(8,128)S(1)}, u32[]{:S(2)}) copy-start(f32[256,2304]{1,0:T(8,128)S(1)} %get-tuple-element.138.driven) | copy-start | bytes 7077892
  159.6 31.3 %copy-start.12 = (f32[256,128]{1,0:T(8,128)}, f32[256,128]{1,0:T(8,128)S(1)}, u32[]{:S(2)}) copy-start(f32[256,128]{1,0:T(8,128)S(1)} %broadcast_in_dim.110.kept) | copy-start | bytes 393220
  513.7 28.6 %copy-start.2 = (f32[256,2304]{1,0:T(8,128)}, f32[256,2304]{1,0:T(8,128)S(1)}, u32[]{:S(2)}) copy-start(f32[256,2304]{1,0:T(8,128)S(1)} %get-tuple-element.119.driven.grad) | copy-start | bytes 7077892
  542.4 45.5 %copy-start.47 = (f32[256,2304]{1,0:T(8,128)S(1)}, f32[256,2304]{1,0:T(8,128)}, u32[]{:S(2)}) copy-start(f32[256,2304]{1,0:T(8,128)} %get-tuple-element.158) | copy-start | bytes 7077892
  609.5 5.9 collective-permute-start.2
  631.3 206.8 %reduce-scatter.24.cloned.1.call-start = ((), (), s32[]{:S(2)}) async-start(), calls=%async_computation.19 | async-start | bytes 5474304
  636.9 326.1 %reduce-scatter.14.cloned.1.call-start = ((), (), s32[]{:S(2)}) async-start(), calls=%async_computation.12 | async-start | bytes 7299072 | tf_op jit(solution)/shard_map/reduce_scatter | solution.py:342
  643.5 443.5 %reduce-scatter.16.cloned.1.call-start = ((), (), s32[]{:S(2)}) async-start(), calls=%async_computation.13 | async-start | bytes 7299072 | tf_op jit(solution)/shard_map/reduce_scatter | solution.py:342
  649.9 562.0 %reduce-scatter.18.cloned.1.call-start = ((), (), s32[]{:S(2)}) async-start(), calls=%async_computation.14 | async-start | bytes 7299072 | tf_op jit(solution)/shard_map/reduce_scatter | solution.py:342
  656.5 679.5 %reduce-scatter.20.cloned.1.call-start = ((), (), s32[]{:S(2)}) async-start(), calls=%async_computation.15 | async-start | bytes 7299072 | tf_op jit(solution)/shard_map/reduce_scatter | solution.py:342
  662.8 821.4 %reduce-scatter.12.cloned.1.call-start = ((), (), s32[]{:S(2)}) async-start(), calls=%async_computation.11 | async-start | bytes 10948608 | tf_op jit(solution)/shard_map/reduce_scatter | solution.py:342
  672.8 40.9 %copy-start.55 = (bf16[8,32,1152]{2,0,1:T(8,128)(2,1)S(1)}, bf16[8,32,1152]{2,0,1:T(8,128)(2,1)}, u32[]{:S(2)}) copy-start(bf16[8,32,1152]{2,0,1:T(8,128)(2,1)} %get-tuple-element.140) | copy-start | bytes 1769476
  672.8 42.3 %copy-start.120 = (f32[256]{0:T(256)S(1)}, f32[256]{0:T(256)}, u32[]{:S(2)}) copy-start(f32[256]{0:T(256)} %get-tuple-element.98) | copy-start | bytes 3076
  672.8 42.3 %slice-start.6 = ((f32[264]{0:T(512)}), f32[256]{0:T(256)S(1)}, s32[]{:S(2)}) async-start(f32[264]{0:T(512)} %copy-done.101), calls=%async_computation.26 | async-start | bytes 2048 | tf_op jit(solution)/shard_map/slice | solution.py:410
  672.8 42.3 %copy-start.59 = (f32[256,1152]{1,0:T(8,128)S(1)}, f32[256,1152]{1,0:T(8,128)}, u32[]{:S(2)}) copy-start(f32[256,1152]{1,0:T(8,128)} %get-tuple-element.166) | copy-start | bytes 3538948
  (120 other events, 735.9 us)
Sparse Core Ops, SparseCore 0:
  10.9 101.8 all-gather.9
  115.6 70.2 all-gather.11
  189.3 71.2 all-gather.15
  263.8 71.1 all-gather.19
  338.2 71.1 all-gather.13
  412.7 71.1 all-gather.17
  631.4 97.0 reduce-scatter.21
  735.2 102.8 reduce-scatter.23
  844.7 118.2 reduce-scatter.13
  968.5 118.3 reduce-scatter.15
  1093.6 118.2 reduce-scatter.17
  1217.4 118.5 reduce-scatter.19
  1343.1 141.0 reduce-scatter.11

commit v2 on v1

--- a/solution.py
+++ b/solution.py
@@ -116,9 +116,10 @@
 
 
 def adjoint_kernel(
-    delta, driven, inner, grad, kept, in_select, out_select, rate, pre_decay, pre_value, entry,
-    post_decay, post_value, exit_, inner_grad, delta_grad, rate_sum, in_grad, out_grad,
-    states, wide_in, wide_out, in_total, out_total,
+    delta, driven, inner, grad, step_pre, kept, in_select, out_select, rate, skip, pre_decay,
+    pre_value, entry, post_decay, post_value, exit_, pre_low, inner_part, rate_sum, step_sum,
+    skip_sum, in_grad, out_grad, states, wide_in, wide_out, in_total, out_total, inner_grad,
+    delta_grad,
 ):
     j = pl.program_id(0)
 
@@ -173,14 +174,20 @@
             in_total[n, rows, :] = in_total[n, rows, :] + folded(adjoint * drive)
             new_backs.append(passed)
             new_sums.append(sums[n] + through * step_t)
-        all_weighted = weighted[0] + weighted[1]
-        inner_grad[rows, :] = all_weighted * step_t
-        delta_grad[rows, :] = all_weighted * inner[rows, :] + (slope[0] + slope[1]) * math.log(2.0)
+        inner_grad[rows, :] = weighted[0] + weighted[1]
+        delta_grad[rows, :] = slope[0] + slope[1]
         return tuple(new_backs), tuple(new_sums)
 
     _, sums = lax.fori_loop(0, length, retreat, (back, (zero,) * NS))
     for n in range(NS):
         rate_sum[n : n + 1, :] = jnp.sum(sums[n], 0, keepdims=True)
+    weighted, value, grads = inner_grad[...], inner[...].astype(jnp.float32), grad[...]
+    slope = weighted * value + delta_grad[...] * math.log(2.0)
+    pre = slope * jax.nn.sigmoid(step_pre[...])
+    pre_low[...] = pre.astype(jnp.bfloat16)
+    step_sum[...] = jnp.sum(pre, 0, keepdims=True)
+    skip_sum[...] = jnp.sum(grads * value, 0, keepdims=True)
+    inner_part[...] = grads * skip[...] + weighted * delta[...]
 
     @pl.when(j == pl.num_programs(0) - 1)
     def _():
@@ -193,6 +200,92 @@
             result[...] = value
 
 
+def earlier_rows(ext, front, rows):
+    own = front[0:rows, :].astype(jnp.float32)
+    halo = front[rows : rows + SEG, :].astype(jnp.float32)
+    place = lax.broadcasted_iota(jnp.int32, (SEG, own.shape[1]), 0)
+    for b in range(3):
+        at = rows - (3 - b) * SEG
+        group = pltpu.roll(own[at : at + SEG], 1, 0)
+        ext[b * SEG : (b + 1) * SEG, :] = jnp.where(place == 0, halo[b : b + 1], group)
+    ext[3 * SEG :, :] = own
+
+
+def masked_tap(ext, same, k, rows, width):
+    tap = ext[k * SEG : k * SEG + rows, :]
+    return tap if k == 3 else tap * tiled_lanes(same[k], width)
+
+
+def conv_kernel(front, same, taps, bias, conv_sum, inner, ext):
+    rows, width = conv_sum.shape
+    earlier_rows(ext, front, rows)
+    total = jnp.broadcast_to(bias[...], (rows, width))
+    for k in range(4):
+        total = total + taps[k : k + 1, :] * masked_tap(ext, same, k, rows, width)
+    conv_sum[...] = total
+    inner[...] = (total * jax.nn.sigmoid(total)).astype(jnp.bfloat16)
+
+
+def conv_back_kernel(
+    front, same, taps, conv_sum, inner_part, select_low, select, front_grad, early, sums, ext
+):
+    rows, width = conv_sum.shape
+    total = conv_sum[...]
+    logistic = jax.nn.sigmoid(total)
+    back = lax.dot_general(
+        select_low[...], select[...], (((1,), (1,)), ((), ())), preferred_element_type=jnp.float32
+    )
+    back = (inner_part[...] + back) * (logistic * (1.0 + total * (1.0 - logistic)))
+    earlier_rows(ext, front, rows)
+    for k in range(4):
+        sums[k : k + 1, :] = jnp.sum(back * masked_tap(ext, same, k, rows, width), 0, keepdims=True)
+    sums[4:5, :] = jnp.sum(back, 0, keepdims=True)
+    sums[5:8, :] = jnp.zeros((3, width), jnp.float32)
+    ext[0 : 3 * SEG, :] = jnp.zeros((3 * SEG, width), jnp.float32)
+    ext[3 * SEG :, :] = back * taps[3:4, :]
+    for k in range(3):
+        part = back * taps[k : k + 1, :] * tiled_lanes(same[k], width)
+        ext[k * SEG : k * SEG + rows, :] = ext[k * SEG : k * SEG + rows, :] + part
+    place = lax.broadcasted_iota(jnp.int32, (SEG, width), 0)
+    early[...] = ext[0 : 3 * SEG, :]
+    for b in range(3):
+        at = rows + b * SEG
+        later = pltpu.roll(ext[b * SEG : (b + 1) * SEG, :], SEG - 1, 0)
+        ext[at : at + SEG, :] = ext[at : at + SEG, :] + jnp.where(place < SEG - 1, later, 0.0)
+    front_grad[...] = ext[3 * SEG :, :]
+
+
+def expert_kernel(
+    buffer, grads, up, down, returned, buffer_grad, up_left, up_right, down_left, down_right
+):
+    def product(left, right, contract):
+        return lax.dot_general(
+            left, right, (contract, ((), ())), preferred_element_type=jnp.float32
+        )
+
+    @pl.when(pl.program_id(0) == 0)
+    def _():
+        returned[...] = jnp.zeros_like(returned)
+        buffer_grad[...] = jnp.zeros_like(buffer_grad)
+
+    values, cot = buffer[...], grads[...]
+    hidden = product(values, up[...], ((1,), (1,)))
+    below = 0.5 * (1.0 + lax.erf(hidden * math.sqrt(0.5)))
+    density = jnp.exp(-0.5 * hidden * hidden) * (1.0 / math.sqrt(2.0 * math.pi))
+    active = (hidden * below).astype(jnp.bfloat16)
+    active_grad = product(cot, down[...], ((1,), (1,)))
+    hidden_grad = (active_grad * (below + hidden * density)).astype(jnp.bfloat16)
+    returned[...] += product(active, down[...], ((1,), (0,)))
+    buffer_grad[...] += product(hidden_grad, up[...], ((1,), (0,)))
+    cut = up_left.shape[1]
+    down_grad = product(active, cot, ((0,), (0,))).astype(jnp.bfloat16)
+    down_left[...] = down_grad[:, :cut]
+    down_right[...] = down_grad[:, cut:]
+    up_grad = product(hidden_grad, values, ((0,), (0,))).astype(jnp.bfloat16)
+    up_left[...] = up_grad[:, :cut]
+    up_right[...] = up_grad[:, cut:]
+
+
 def column_specs(rows, width):
     return (
         pl.BlockSpec((rows, width), lambda j: (0, j)),
@@ -207,6 +300,12 @@
 def params(mib):
     return pltpu.CompilerParams(
         dimension_semantics=("arbitrary",), vmem_limit_bytes=mib * 2**20
+    )
+
+
+def cost(rows, channels, passes):
+    return pl.CostEstimate(
+        flops=0, bytes_accessed=int(rows * channels * passes), transcendentals=0
     )
 
 
@@ -222,6 +321,7 @@
         + [jax.ShapeDtypeStruct((NS, channels), jnp.float32)] * 2,
         scratch_shapes=[pltpu.VMEM((NS, rows, LANE), jnp.float32)],
         compiler_params=params(24),
+        cost_estimate=cost(rows, channels, 75),
     )(delta, driven, kept, select, rate)
 
 
@@ -242,33 +342,122 @@
         ],
         scratch_shapes=[wide, wide],
         compiler_params=params(24),
+        cost_estimate=cost(rows, channels, 95),
     )(delta, driven, inner, gate, kept, in_select, out_select, rate, skip, *pre, entry)
 
 
 def scan_adjoint(
-    delta, driven, inner, grad, kept, in_select, out_select, rate, pre, entry, post, exit_,
-    width=LANE,
+    delta, driven, inner, grad, step_pre, kept, in_select, out_select, rate, skip, pre, entry,
+    post, exit_, width=LANE,
 ):
     rows, channels = delta.shape
-    block, flag, columns, state, segments, _ = column_specs(rows, width)
+    block, flag, columns, state, segments, line = column_specs(rows, width)
     wide = pltpu.VMEM((NS, rows, LANE), jnp.float32)
+    whole = pltpu.VMEM((rows, width), jnp.float32)
     return pl.pallas_call(
         adjoint_kernel,
         grid=(channels // width,),
-        in_specs=[block] * 4
-        + [flag, columns, columns, state, segments, segments, state, segments, segments, state],
-        out_specs=[block, block, state, columns, columns],
-        out_shape=[jax.ShapeDtypeStruct((rows, channels), jnp.float32)] * 2
-        + [jax.ShapeDtypeStruct((NS, channels), jnp.float32)]
+        in_specs=[block] * 5
+        + [flag, columns, columns, state, line]
+        + [segments, segments, state, segments, segments, state],
+        out_specs=[block, block, state, line, line, columns, columns],
+        out_shape=[
+            jax.ShapeDtypeStruct((rows, channels), jnp.bfloat16),
+            jax.ShapeDtypeStruct((rows, channels), jnp.float32),
+            jax.ShapeDtypeStruct((NS, channels), jnp.float32),
+        ]
+        + [jax.ShapeDtypeStruct((1, channels), jnp.float32)] * 2
         + [jax.ShapeDtypeStruct((rows, NS), jnp.float32)] * 2,
         scratch_shapes=[
             pltpu.VMEM((rows // SEG, NS, SEG, width), jnp.float32),
-            wide, wide, wide, wide,
+            wide, wide, wide, wide, whole, whole,
         ],
-        compiler_params=params(32),
+        compiler_params=params(40),
+        cost_estimate=cost(rows, channels, 280),
     )(
-        delta, driven, inner, grad, kept, in_select, out_select, rate, *pre, entry, *post, exit_
-    )
+        delta, driven, inner, grad, step_pre, kept, in_select, out_select, rate, skip, *pre, entry,
+        *post, exit_,
+    )
+
+
+def conv_specs(rows, width):
+    return (
+        pl.BlockSpec((rows + SEG, width), lambda j: (0, j)),
+        pl.BlockSpec((3, rows, LANE), lambda j: (0, 0, 0)),
+        pl.BlockSpec((4, width), lambda j: (0, j)),
+        pl.BlockSpec((rows, width), lambda j: (0, j)),
+    )
+
+
+def convolved(front, same, taps, bias, width):
+    rows, channels = front.shape[0] - SEG, front.shape[1]
+    ahead, flags, weights, block = conv_specs(rows, width)
+    return pl.pallas_call(
+        conv_kernel,
+        grid=(channels // width,),
+        in_specs=[ahead, flags, weights, pl.BlockSpec((1, width), lambda j: (0, j))],
+        out_specs=[block, block],
+        out_shape=[
+            jax.ShapeDtypeStruct((rows, channels), jnp.float32),
+            jax.ShapeDtypeStruct((rows, channels), jnp.bfloat16),
+        ],
+        scratch_shapes=[pltpu.VMEM((rows + 3 * SEG, width), jnp.float32)],
+        compiler_params=params(24),
+        cost_estimate=cost(rows, channels, 25),
+    )(front, same, taps, bias)
+
+
+def convolved_back(front, same, taps, conv_sum, inner_part, select_low, select, width):
+    rows, channels = conv_sum.shape
+    ahead, flags, weights, block = conv_specs(rows, width)
+    inputs = select.shape[1]
+    return pl.pallas_call(
+        conv_back_kernel,
+        grid=(channels // width,),
+        in_specs=[
+            ahead,
+            flags,
+            weights,
+            block,
+            block,
+            pl.BlockSpec((rows, inputs), lambda j: (0, 0)),
+            pl.BlockSpec((width, inputs), lambda j: (j, 0)),
+        ],
+        out_specs=[
+            block,
+            pl.BlockSpec((3 * SEG, width), lambda j: (0, j)),
+            pl.BlockSpec((SEG, width), lambda j: (0, j)),
+        ],
+        out_shape=[
+            jax.ShapeDtypeStruct((rows, channels), jnp.float32),
+            jax.ShapeDtypeStruct((3 * SEG, channels), jnp.float32),
+            jax.ShapeDtypeStruct((SEG, channels), jnp.float32),
+        ],
+        scratch_shapes=[pltpu.VMEM((rows + 3 * SEG, width), jnp.float32)],
+        compiler_params=params(24),
+        cost_estimate=cost(rows, channels, 40),
+    )(front, same, taps, conv_sum, inner_part, select_low, select)
+
+
+def expert_pass(buffer, grads, up, down, tile):
+    slots, width = buffer.shape
+    units = up.shape[0]
+    whole = pl.BlockSpec((slots, width), lambda j: (0, 0))
+    strip = pl.BlockSpec((tile, width), lambda j: (j, 0))
+    cut = cut_of(width)
+    sizes = [cut, width - cut] * 2
+    return pl.pallas_call(
+        expert_kernel,
+        grid=(units // tile,),
+        in_specs=[whole, whole, strip, strip],
+        out_specs=[whole, whole] + [pl.BlockSpec((tile, n), lambda j: (j, 0)) for n in sizes],
+        out_shape=[jax.ShapeDtypeStruct((slots, width), jnp.float32)] * 2
+        + [jax.ShapeDtypeStruct((units, n), jnp.bfloat16) for n in sizes],
+        compiler_params=params(40),
+        cost_estimate=pl.CostEstimate(
+            flops=12 * slots * width * units, bytes_accessed=8 * units * width, transcendentals=0
+        ),
+    )(buffer, grads, up, down)
 
 
 MODEL_WIDTH = 1152
@@ -307,13 +496,11 @@
 
 
 def entering(decay, value, reverse):
-    size, mine = lax.axis_size("seq"), lax.axis_index("seq")
-    gathered = lax.all_gather(jnp.stack([decay, value]).astype(BF16), "seq").astype(F32)
+    pair = jnp.stack([decay, value]).astype(BF16)
     state = jnp.zeros_like(value)
-    for k in range(size):
-        at = size - 1 - k if reverse else k
-        reached = at > mine if reverse else at < mine
-        state = jnp.where(reached, gathered[at, 0] * state + gathered[at, 1], state)
+    for k in range(lax.axis_size("seq") - 1, 0, -1):
+        part = passed_along(pair, "seq", -k if reverse else k).astype(F32)
+        state = part[0] * state + part[1]
     return state
 
 
@@ -334,12 +521,131 @@
     )
 
 
-def gathered(shard):
-    return lax.all_gather(shard, BOTH, axis=0, tiled=True)
-
-
-def scattered(whole):
-    return lax.psum_scatter(whole.astype(BF16), BOTH, scatter_dimension=0, tiled=True).astype(F32)
+def sides():
+    return math.isqrt(lax.axis_size("dp") // 2)
+
+
+def moved(array, axis, by=1):
+    if axis == "z":
+        size = lax.axis_size("seq")
+        return lax.ppermute(array, "seq", [(i, (i + by) % size) for i in range(size)])
+    side = sides()
+    stride, size = {"core": (1, 2), "x": (2, side), "y": (2 * side, side)}[axis]
+    pairs = []
+    for i in range(lax.axis_size("dp")):
+        at = i // stride % size
+        pairs.append((i, i + stride * ((at + by) % size - at)))
+    return lax.ppermute(array, "dp", pairs)
+
+
+def size_of(axis):
+    return lax.axis_size("seq") if axis == "z" else 2 if axis == "core" else sides()
+
+
+def ring_gather(block, axis):
+    pieces = [block]
+    for _ in range(size_of(axis) - 1):
+        pieces.append(moved(pieces[-1], axis))
+    if axis == "z":
+        whole = jnp.zeros((len(pieces),) + block.shape, block.dtype)
+        for k, piece in enumerate(pieces):
+            whole = lax.dynamic_update_index_in_dim(whole, piece, depth_of(k), 0)
+        return whole
+    return jnp.stack(pieces)
+
+
+def depth_of(k):
+    size = lax.axis_size("seq")
+    return lax.rem(lax.axis_index("seq") + size - k, size)
+
+
+def added(left, right):
+    return (left.astype(F32) + right.astype(F32)).astype(BF16)
+
+
+def ring_scatter(parts, axis):
+    if axis == "z":
+        size = size_of(axis)
+        parts = [lax.dynamic_index_in_dim(parts, depth_of(k), 0, False) for k in range(size)]
+    total = parts[-1]
+    for k in range(size_of(axis) - 2, -1, -1):
+        total = added(parts[k], moved(total, axis, -1))
+    return total
+
+
+def cut_of(columns):
+    return (columns // LANE + 1) // 2 * LANE
+
+
+def after(value, *others):
+    if not others:
+        return value
+    return lax.optimization_barrier((value, *others))[0]
+
+
+def plane_gather(block, waits=((), (), ())):
+    cut = cut_of(block.shape[1])
+    pieces = ring_gather(after(block, *waits[0]), "z")
+    first = after(pieces, *waits[1])
+    left = after(ring_gather(first[..., :cut], "x"), *waits[2])
+    right = after(ring_gather(first[..., cut:], "y"), *waits[2])
+    left, right = ring_gather(left, "y"), ring_gather(right, "x")
+    return jnp.concatenate([left, right.swapaxes(0, 1)], -1), pieces, (left, right)
+
+
+def plane_scatter(left, right, waits=((), ())):
+    left = after(ring_scatter(left, "y"), *waits[0])
+    right = after(ring_scatter(right.swapaxes(0, 1), "x"), *waits[0])
+    left, right = ring_scatter(left, "x"), ring_scatter(right, "y")
+    return ring_scatter(after(jnp.concatenate([left, right], -1), *waits[1]), "z")
+
+
+def by_place(pieces, axis):
+    size = size_of(axis)
+    mine = lax.axis_index("dp") // (2 * sides())
+    order = []
+    for j in range(size):
+        piece = pieces[size - 1]
+        for k in range(size - 1):
+            piece = jnp.where(lax.rem(mine - j + size, size) == k, pieces[k], piece)
+        order.append(piece)
+    return order
+
+
+def unit_blocks(whole, inverse=False):
+    side = sides()
+    dp = lax.axis_index("dp")
+    at_x, at_core = lax.rem(dp // 2, side), lax.rem(dp, 2)
+    parts = whole.reshape((side // 2, side, 2, -1) + whole.shape[1:])
+    if inverse:
+        parts = whole.reshape((2, side // 2, side, -1) + whole.shape[1:]).transpose(1, 2, 0, 3, 4)
+    rows = []
+    for k in range(side):
+        piece = lax.dynamic_index_in_dim(parts, lax.rem(at_x - k + side, side), 1, False)
+        pair = [piece[:, 0], piece[:, 1]]
+        rows.append([jnp.where(at_core == 0, pair[c], pair[1 - c]) for c in range(2)])
+    if inverse:
+        return jnp.stack([jnp.stack(r, 1) for r in rows], 1).reshape(whole.shape)
+    return [jnp.stack([r[c] for r in rows], 1).reshape((-1,) + whole.shape[1:]) for c in range(2)]
+
+
+def unit_gather(block):
+    return unit_blocks(lax.all_gather(block, BOTH, axis=0, tiled=True))
+
+
+def unit_scatter(grads):
+    whole = unit_blocks(jnp.concatenate(grads), True)
+    return lax.psum_scatter(whole, BOTH, scatter_dimension=0, tiled=True).astype(F32)
+
+
+def everywhere(array):
+    for axis in ("dp", "seq"):
+        size = lax.axis_size(axis)
+        bit = 1
+        while bit < size:
+            array = array + lax.ppermute(array, axis, [(i, i ^ bit) for i in range(size)])
+            bit *= 2
+    return array
 
 
 def per_device(
@@ -364,7 +670,11 @@
     rows = tokens.shape[1]
     slots_per = 5 * rows // (4 * EXPERT_COUNT)
     slots = EXPERT_COUNT * slots_per
-    wide = DI // 6
+    half = DI // 2
+    wide = half // 3
+    core = lax.rem(lax.axis_index("dp"), 2)
+    side, depth = sides(), lax.axis_size("seq")
+    both = range(2)
 
     prior_tokens = passed_along(tokens[0, rows - REACH :], "seq", 1)
     prior_doc = passed_along(doc_ids[0, rows - REACH :], "seq", 1)
@@ -372,7 +682,6 @@
     gains_all = lines[:2].astype(F32)
     router_all = lines[2:].astype(F32)
 
-    in_full = gathered(in_proj.T)
     small = jnp.concatenate(
         [
             select_proj,
@@ -385,16 +694,31 @@
         ],
         1,
     )
-    small_full = gathered(small)
-    select_full = small_full[:, : R + 2 * NS]
-    step_full = small_full[:, R + 2 * NS : 2 * R + 2 * NS]
-    line_full = small_full[:, 2 * R + 2 * NS :].astype(F32).T
-    decay_rate = -jnp.exp(line_full[:NS])
-    conv_taps = line_full[NS : NS + KC]
-    bias_conv, bias_step, skip_wide = (line_full[NS + KC + k][None] for k in range(3))
-    out_full = gathered(out_proj)
-    up_full = [gathered(expert_up[e].T) for e in range(EXPERT_COUNT)]
-    down_full = [gathered(expert_down[e]) for e in range(EXPERT_COUNT)]
+    columns = small.shape[1]
+    spare = -columns % LANE
+
+    def expert_block(shards):
+        own = jnp.where(core == 0, shards[0], shards[1])
+        other = jnp.where(core == 0, shards[1], shards[0])
+        return jnp.concatenate([own, moved(other, "core")])
+
+    in_near, in_z, _ = plane_gather(in_proj.T)
+    in_near = in_near.reshape(DI, MODEL_WIDTH)
+    in_full = (in_near, moved(in_near, "core"))
+    small_full = unit_gather(jnp.pad(small, ((0, 0), (0, spare))))
+    out_full = unit_gather(out_proj)
+    up_block = expert_block(expert_up.swapaxes(1, 2))
+    down_block = expert_block(expert_down)
+
+    at = R + 2 * NS
+    select_full = [w[:, :at] for w in small_full]
+    step_full = [w[:, at : at + R] for w in small_full]
+    line_full = [w[:, at + R : columns].astype(F32).T for w in small_full]
+    decay_rate = [-jnp.exp(w[:NS]) for w in line_full]
+    conv_taps = [w[NS : NS + KC] for w in line_full]
+    bias_conv, bias_step, skip_wide = (
+        [w[NS + KC + k][None] for w in line_full] for k in range(3)
+    )
 
     mine = interleave(tokens[0])
     doc_row = interleave(doc_ids[0])
@@ -409,34 +733,57 @@
     stream, inv_first, hat_first, normed = (
         a[:rows] for a in (stream_ext, inv_ext, hat_ext, normed_ext)
     )
-    proj_ext = dot(normed_ext, in_full, ((1,), (1,))).astype(BF16)
-    front = proj_ext[:rows, :DI]
-    gate = proj_ext[:rows, DI:]
     ext_ids = with_earlier(doc_row, prior_doc)
-    ext_rows = with_earlier(front.astype(F32), proj_ext[rows : rows + REACH, :DI].astype(F32))
-    masks = [(ext_ids[k * SEG : k * SEG + rows] == doc_row)[:, None] for k in range(KC)]
-    taps = [jnp.where(masks[k], ext_rows[k * SEG : k * SEG + rows], 0.0) for k in range(KC)]
-    conv_sum = bias_conv
-    for k in range(KC):
-        conv_sum = conv_sum + conv_taps[k][None] * taps[k]
-    inner = jax.nn.silu(conv_sum).astype(BF16)
-    inner_wide = inner.astype(F32)
-    select = dot(inner, select_full, ((1,), (0,)))
+    same = jnp.stack(
+        [(ext_ids[k * SEG : k * SEG + rows] == doc_row).astype(F32) for k in range(REACH)]
+    )
+    same = jnp.broadcast_to(same[:, :, None], (REACH, rows, LANE))
+    kept = same[REACH - 1]
+
+    strip = DI // side
+    front, gate, conv_sum, inner = [], [], [], []
+    for h in both:
+        proj = dot(normed_ext, in_full[h], ((1,), (1,))).astype(BF16)
+        parts = by_place([proj[:, k * strip : (k + 1) * strip] for k in range(side)], "y")
+        front.append(jnp.concatenate(parts[: side // 2], 1))
+        gate.append(jnp.concatenate(parts[side // 2 :], 1)[:rows])
+        made = convolved(front[h], same, conv_taps[h], bias_conv[h], wide)
+        conv_sum.append(made[0])
+        inner.append(made[1])
+    select = sum(dot(inner[h], select_full[h], ((1,), (0,))) for h in both)
     steps_low = select[:, :R].astype(BF16)
     in_select = select[:, R : R + NS]
     out_select = select[:, R + NS :]
-    step_pre = dot(steps_low, step_full, ((1,), (1,))) + bias_step
-    delta = jax.nn.softplus(step_pre)
-    driven = delta * inner_wide
-    kept = jnp.broadcast_to(masks[REACH - 1].astype(F32), (rows, LANE))
-    rate = decay_rate * math.log2(math.e)
-
-    *pre, all_decay, all_state = segment_ends(delta, driven, kept, in_select, rate, False, wide)
-    state_in = entering(all_decay, all_state, False)
-    scanned, gated = scan_output(
-        delta, driven, inner, gate, kept, in_select, out_select, rate, skip_wide, pre, state_in, wide
-    )
-    mixed = dot(gated, out_full, ((1,), (0,)))
+    step_pre = [dot(steps_low, step_full[h], ((1,), (1,))) + bias_step[h] for h in both]
+    delta = [jax.nn.softplus(p) for p in step_pre]
+    driven = [d * x.astype(F32) for d, x in zip(delta, inner)]
+    rate = [r * math.log2(math.e) for r in decay_rate]
+
+    up_full, up_z, up_side = plane_gather(
+        up_block, ((in_z,), (in_near,), tuple(x[:SEG] for x in inner))
+    )
+    pre, state_in, marks = [], [], []
+    for h in both:
+        *ends, all_decay, all_state = segment_ends(
+            delta[h], driven[h], kept, in_select, rate[h], False, wide
+        )
+        marks.append(all_decay)
+        pre.append(ends)
+        state_in.append(entering(all_decay, all_state, False))
+    scanned, gated = zip(
+        *(
+            scan_output(
+                delta[h], driven[h], inner[h], gate[h], kept, in_select, out_select, rate[h],
+                skip_wide[h], pre[h], state_in[h], wide,
+            )
+            for h in both
+        )
+    )
+    down_full, _, _ = plane_gather(
+        down_block, ((up_z,), tuple(marks), tuple(g[:SEG] for g in gated))
+    )
+    up_full, down_full = (w.reshape(-1, MODEL_WIDTH) for w in (up_full, down_full))
+    mixed = sum(dot(gated[h], out_full[h], ((1,), (0,))) for h in both)
     resid = stream + mixed
     inv_second = lax.rsqrt(jnp.mean(resid * resid, -1, keepdims=True) + EPS)
     hat_second = resid * inv_second
@@ -451,41 +798,35 @@
     lower = (place[:, None] >= place[None, :]).astype(BF16)
     rank_in = dot(lower, route_hot.astype(BF16), ((1,), (0,))) - 1.0
     slot = jnp.sum(rank_in * hot_wide, 1).astype(jnp.int32)
-    target = route * slots_per + slot
+    target = jnp.where(route == core, 0, slots_per) + slot
     pick = (jnp.arange(slots, dtype=jnp.int32)[:, None] == target[None, :]).astype(BF16)
-
-    def to_slots(values):
-        placed = dot(pick, values, ((1,), (0,))).astype(BF16)
-        return [placed[e * slots_per : (e + 1) * slots_per] for e in range(EXPERT_COUNT)]
+    returned_grad = (chosen * out_cot).astype(BF16)
+    placed = dot(pick, jnp.concatenate([normed_moe, returned_grad], 1), ((1,), (0,))).astype(BF16)
+    placed = jnp.concatenate([placed[:slots_per], moved(placed[slots_per:], "core")])
+    buffer, grad_slots = placed[:, :MODEL_WIDTH], placed[:, MODEL_WIDTH:]
 
     def from_slots(parts):
-        return dot(pick.astype(F32), jnp.concatenate(parts), ((0,), (0,)), HIGHEST)
-
-    buffers = to_slots(normed_moe)
-    hidden = [dot(buffers[e], up_full[e], ((1,), (1,))) for e in range(EXPERT_COUNT)]
-    active = [jax.nn.gelu(h, approximate=False).astype(BF16) for h in hidden]
-    returned = from_slots(
-        [dot(active[e], down_full[e], ((1,), (0,))) for e in range(EXPERT_COUNT)]
-    )
+        parts = jnp.concatenate([parts[:slots_per], moved(parts[slots_per:], "core")])
+        return dot(pick.astype(F32), parts, ((0,), (0,)), HIGHEST)
+
+    def expert_scatter(left, right, waits):
+        left, right = (g.reshape(side, side, depth, -1, g.shape[1]) for g in (left, right))
+        own, other = jnp.split(plane_scatter(left, right, waits), 2)
+        other = moved(other, "core")
+        pair = jnp.where(core == 0, own, other), jnp.where(core == 0, other, own)
+        return jnp.stack(pair).astype(F32)
+
+    returned, buffer_grad, *expert_grads = expert_pass(
+        buffer, grad_slots, up_full, down_full, up_full.shape[0] // 12
+    )
+    returned = from_slots(returned)
+    buffer_grad = from_slots(buffer_grad)
     branch = chosen * returned
     layer_out = (resid + branch).astype(BF16)
     squared_values = jnp.stack(
         [jnp.sum(resid * resid), jnp.sum(mixed * mixed), jnp.sum(branch * branch)]
     )
     chosen_grad = jnp.sum(out_cot * returned, 1, keepdims=True)
-    returned_grad = to_slots((chosen * out_cot).astype(BF16))
-    grad_down = [dot(active[e], returned_grad[e], ((0,), (0,))) for e in range(EXPERT_COUNT)]
-    active_grad = [
-        dot(returned_grad[e], down_full[e], ((1,), (1,))) for e in range(EXPERT_COUNT)
-    ]
-    hidden_grad = [
-        (active_grad[e] * gelu_slope(hidden[e])).astype(BF16) for e in range(EXPERT_COUNT)
-    ]
-    grad_up = [dot(hidden_grad[e], buffers[e], ((0,), (0,))) for e in range(EXPERT_COUNT)]
-    expert_sums = [scattered(g) for g in (*grad_down, *grad_up)]
-    buffer_grad = from_slots(
-        [dot(hidden_grad[e], up_full[e], ((1,), (0,))) for e in range(EXPERT_COUNT)]
-    )
     logit_grad = chosen_grad * chosen * (hot_wide - probs)
     grad_router = dot(logit_grad, normed_wide, ((0,), (0,)), HIGHEST)
     moe_grad = buffer_grad + dot(logit_grad, router_all, ((1,), (0,)), HIGHEST)
@@ -495,86 +836,97 @@
         scaled_second - hat_second * jnp.mean(scaled_second * hat_second, -1, keepdims=True)
     )
     mixed_grad = resid_grad.astype(BF16)
-    grad_out = dot(gated, mixed_grad, ((0,), (0,)))
-    out_sum = scattered(grad_out)
-    gated_grad = dot(mixed_grad, out_full, ((1,), (1,)))
-    gate_half = gate.astype(F32)
-    scan_grad = gated_grad * jax.nn.silu(gate_half)
-    gate_grad = gated_grad * scanned * silu_slope(gate_half)
-    grad_skip = jnp.sum(scan_grad * inner_wide, 0)
-    *post, back_decay, back_adjoint = segment_ends(
-        delta, scan_grad, kept, out_select, rate, True, wide
-    )
-    adjoint_in = entering(back_decay, back_adjoint, True)
-    inner_scan_grad, delta_grad, rate_sum, in_select_grad, out_select_grad = scan_adjoint(
-        delta, driven, inner_wide, scan_grad, kept, in_select, out_select, rate, pre, state_in,
-        post, adjoint_in, wide,
-    )
-    grad_decay = rate_sum * decay_rate
-    pre_grad = delta_grad * jax.nn.sigmoid(step_pre)
-    grad_step_bias = jnp.sum(pre_grad, 0)
-    pre_low = pre_grad.astype(BF16)
-    grad_step = dot(pre_low, steps_low, ((0,), (0,)))
-    steps_grad = dot(pre_low, step_full, ((1,), (0,)))
-    select_low = jnp.concatenate([steps_grad, in_select_grad, out_select_grad], 1).astype(BF16)
-    grad_select = dot(inner, select_low, ((0,), (0,)))
-    inner_grad = (
-        scan_grad * skip_wide + inner_scan_grad + dot(select_low, select_full, ((1,), (1,)))
-    )
-    conv_back = inner_grad * silu_slope(conv_sum)
-    grad_lines = jnp.concatenate(
-        [
-            grad_decay,
-            jnp.stack(
-                [jnp.sum(conv_back * taps[k], 0) for k in range(KC)]
-                + [jnp.sum(conv_back, 0), grad_step_bias, grad_skip]
-            ),
-        ]
-    )
-    ext_grad = sum(
-        jnp.pad(
-            jnp.where(masks[k], conv_back * conv_taps[k][None], 0.0),
-            ((k * SEG, (REACH - k) * SEG), (0, 0)),
+    gated_grad = [dot(mixed_grad, out_full[h], ((1,), (1,))) for h in both]
+    gates = [g.astype(F32) for g in gate]
+    scan_grad = [gated_grad[h] * jax.nn.silu(gates[h]) for h in both]
+    gate_grad = [(gated_grad[h] * scanned[h] * silu_slope(gates[h])).astype(BF16) for h in both]
+    post, adjoint_in = [], []
+    for h in both:
+        *ends, all_decay, all_adjoint = segment_ends(
+            delta[h], scan_grad[h], kept, out_select, rate[h], True, wide
         )
-        for k in range(KC)
-    )
-    early = ext_grad[: REACH * SEG].reshape(REACH, SEG, DI)
-    incoming = passed_along(early[:, 0], "seq", -1)
-    tail = jnp.concatenate([early[:, 1:], incoming[:, None]], 1).reshape(REACH * SEG, DI)
-    front_grad = ext_grad[REACH * SEG :] + jnp.pad(tail, ((rows - REACH * SEG, 0), (0, 0)))
-    proj_grad = jnp.concatenate([front_grad, gate_grad], 1).astype(BF16)
-    grad_in = dot(proj_grad, normed, ((0,), (0,)))
-    in_sum = scattered(grad_in)
-    normed_grad = dot(proj_grad, in_full, ((1,), (0,)))
+        post.append(ends)
+        marks.append(all_decay)
+        adjoint_in.append(entering(all_decay, all_adjoint, True))
+    out_sum = unit_scatter(
+        [dot(gated[h], mixed_grad, ((0,), (0,))).astype(BF16) for h in both]
+    )
+    pre_low, inner_part, rate_sum, step_sum, skip_sum, in_grad, out_grads = zip(
+        *(
+            scan_adjoint(
+                delta[h], driven[h], inner[h], scan_grad[h], step_pre[h], kept, in_select,
+                out_select, rate[h], skip_wide[h], pre[h], state_in[h], post[h], adjoint_in[h],
+                wide,
+            )
+            for h in both
+        )
+    )
+    down_sum = expert_scatter(
+        *expert_grads[2:], (tuple(marks[2:]), (step_sum[0],))
+    )
+    up_sum = expert_scatter(*expert_grads[:2], ((step_sum[0],), (step_sum[1],)))
+    steps_grad = sum(dot(pre_low[h], step_full[h], ((1,), (0,))) for h in both)
+    select_low = jnp.concatenate(
+        [steps_grad, in_grad[0] + in_grad[1], out_grads[0] + out_grads[1]], 1
+    ).astype(BF16)
+    front_grad, early, tap_sums = zip(
+        *(
+            convolved_back(
+                front[h], same, conv_taps[h], conv_sum[h], inner_part[h], select_low,
+                select_full[h], wide,
+            )
+            for h in both
+        )
+    )
+    grad_small = []
+    for h in both:
+        lines = [rate_sum[h] * decay_rate[h], tap_sums[h][: KC + 1], step_sum[h], skip_sum[h]]
+        grad_small.append(
+            jnp.concatenate(
+                [
+                    dot(inner[h], select_low, ((0,), (0,))),
+                    dot(pre_low[h], steps_low, ((0,), (0,))),
+                    jnp.concatenate(lines).T,
+                    jnp.zeros((half, spare), F32),
+                ],
+                1,
+            ).astype(BF16)
+        )
+    proj_grad = []
+    for h in both:
+        incoming = passed_along(early[h].reshape(REACH, SEG, half)[:, 0], "seq", -1)
+        tail = jnp.pad(incoming[:, None], ((0, 0), (SEG - 1, 0), (0, 0)))
+        tail = jnp.pad(tail.reshape(REACH * SEG, half), ((rows - REACH * SEG, 0), (0, 0)))
+        whole = jnp.concatenate([(front_grad[h] + tail).astype(BF16), gate_grad[h]], 1)
+        parts = [whole[:, k * strip : (k + 1) * strip] for k in range(side)]
+        proj_grad.append(jnp.concatenate(by_place(parts, "y"), 1))
+    grad_in = [dot(proj_grad[h], normed, ((0,), (0,))).astype(BF16) for h in (1, 0)]
+    in_plane = added(grad_in[1], moved(grad_in[0], "core"))
+    in_plane = in_plane.reshape(side, side, depth, -1, MODEL_WIDTH)
+    cut = cut_of(MODEL_WIDTH)
+    in_sum = plane_scatter(in_plane[..., :cut], in_plane[..., cut:]).astype(F32)
+    small_sum = unit_scatter(grad_small)
+    normed_grad = sum(dot(proj_grad[h], in_full[h], ((1,), (0,))) for h in both)
     first_gain_grad = jnp.sum(normed_grad * hat_first, 0)
     scaled_first = normed_grad * gains_all[0]
     stream_grad = resid_grad + inv_first * (
         scaled_first - hat_first * jnp.mean(scaled_first * hat_first, -1, keepdims=True)
     )
 
+    line_sum = small_sum[:, at + R :]
+    squares = jnp.zeros((1, MODEL_WIDTH), F32).at[0, :3].set(squared_values)
+    early_sum = everywhere(jnp.concatenate([second_gain_grad[None], grad_router, squares]))
+    late_sum = everywhere(first_gain_grad[None])
     parts = lax.axis_size("dp")
-    repeats = lax.axis_size("seq")
-    grad_small = jnp.concatenate([grad_select, grad_step, grad_lines.T], 1)
-    columns = grad_small.shape[1]
-    unit = DI // (parts * repeats)
-    shared = jnp.concatenate([first_gain_grad[None], second_gain_grad[None], grad_router])
     width = MODEL_WIDTH // parts
-    shared = shared.reshape(4, parts, width).swapaxes(0, 1).reshape(parts, 1, 4 * width)
-    extra = -(-4 * width // unit)
-    shared = jnp.pad(shared, ((0, 0), (0, 0), (0, extra * unit - 4 * width)))
-    shared = jnp.broadcast_to(shared, (parts, repeats, extra * unit)).reshape(DI, extra)
-    small_sum = lax.psum_scatter(
-        jnp.concatenate([grad_small, shared], 1), BOTH, scatter_dimension=0, tiled=True
-    )
-    shared_sum = small_sum[:, columns:].reshape(extra * unit)[: 4 * width].reshape(4, width)
-    at = R + 2 * NS
-    square_total = lax.psum(squared_values, BOTH)
-    stats = jnp.sqrt(square_total / (rows * parts * repeats * MODEL_WIDTH))
-    line_sum = small_sum[:, at + R : columns]
+    shared = lax.dynamic_slice_in_dim(
+        jnp.concatenate([late_sum, early_sum[:3]]), lax.axis_index("dp") * width, width, 1
+    )
+    stats = jnp.sqrt(early_sum[3, :3] / (rows * parts * depth * MODEL_WIDTH))
     return (
         in_order(layer_out)[None],
         in_order(stream_grad.astype(BF16))[None],
-        shared_sum[:2],
+        shared[:2],
         in_sum.T,
         line_sum[:, NS : NS + KC].T,
         line_sum[:, NS + KC],
@@ -584,9 +936,9 @@
         line_sum[:, :NS],
         line_sum[:, NS + KC + 2],
         out_sum,
-        shared_sum[2:].T,
-        jnp.stack([s.T for s in expert_sums[EXPERT_COUNT:]]),
-        jnp.stack(expert_sums[:EXPERT_COUNT]),
+        shared[2:].T,
+        up_sum.swapaxes(1, 2),
+        down_sum,
         stats,
     )
 

time: 1500 us -> 791 us (0.53)
  waiting for transfers between devices: 983 us -> 321 us
  blocking collectives: 175 us -> 8.91 us
  matrix products: 144 us -> 54.5 us
  starting transfers between devices: 10.4 us -> 87.7 us
  other arithmetic: 31.2 us -> 84.7 us
  Pallas kernels: 84.5 us -> 122 us
  local copies, waits for them, and re-layouts: 48.9 us -> 85.1 us
    reduce_scatter x5 -> x1, waiting for transfers between devices: 640 us -> 0.02 us  [unit_scatter(): lax.psum_scatter(whole, BOTH, scatter_dimension=0, tiled=True).astype(F32)]
    ppermute x0 -> x61, waiting for transfers between devices: none -> 316 us  [the longest x33 173 us: moved(): return lax.ppermute(array, 'dp', pairs)]
    all_gather x6 -> x2, waiting for transfers between devices: 229 us -> 0.01 us  [unit_gather(): return unit_blocks(lax.all_gather(block, BOTH, axis=0, tiled=True))]
    all_gather x3 -> x0, blocking collectives: 127 us -> none  [the longest x1 91.6 us: gathered(): return lax.all_gather(shard, BOTH, axis=0, tiled=True)]
    unnamed x15 -> x5, waiting for transfers between devices: 112 us -> 0.07 us
    dot_general x32 -> x29, matrix products: 144 us -> 54.5 us  [dot(): lax.dot_general(left, right, (contract, ((), ())), precision=precision, p...]
    ppermute x0 -> x61, starting transfers between devices: none -> 57.8 us  [the longest x33 27.3 us: moved(): return lax.ppermute(array, 'dp', pairs)]
    psum x1 -> x0, blocking collectives: 38.7 us -> none  [per_device(): square_total = lax.psum(squared_values, BOTH)]
  transfers between devices with their start and end apart: 16 -> 81, of which waited for: 12 -> 38; matrix products, arithmetic and copies ran while one was open for 9% -> 24% of each run, Pallas kernels for 2% -> 13%
where the time goes in v2:
time: 791 us; the launch traced here: 781 us
  waiting for transfers between devices  321 us (41%)
  Pallas kernels  122 us (15%)
  starting transfers between devices  87.7 us (11%)
  local copies, waits for them, and re-layouts  85.1 us (11%)
  other arithmetic  84.7 us (11%)
  matrix products  54.5 us (7%)
  between operations  17.2 us (2%)
  blocking collectives  8.91 us (1%)
    ppermute x33, waiting for transfers between devices, moved(): return lax.ppermute(array, 'dp', pairs)  173 us
    ppermute x18, waiting for transfers between devices, moved(): lax.ppermute(array, 'seq', [(i, (i + by) % size) for i in range(size)])  130 us
    dot_general x29, matrix products, dot(): lax.dot_general(left, right, (contract, ((), ())), precision=precision, p...  54.5 us
    pallas_call x2, Pallas kernels, scan_adjoint(): pl.pallas_call(adjoint_kernel, grid=(channels // width,), in_specs=[block...  49.4 us
    ppermute x16, starting transfers between devices, passed_along(): return lax.ppermute(array, axis, pairs)  29.7 us
    ppermute x33, starting transfers between devices, moved(): return lax.ppermute(array, 'dp', pairs)  27.3 us
    pallas_call x4, Pallas kernels, segment_ends(): pl.pallas_call(functools.partial(ends_kernel, reverse), grid=(channels //...  25.3 us
    pallas_call x1, Pallas kernels, expert_pass(): pl.pallas_call(expert_kernel, grid=(units // tile,), in_specs=[whole, who...  24.4 us
  transfers between devices with their start and end apart: 81, of which 38 were waited for; matrix products, arithmetic and copies ran while one was open for 24% of the time, Pallas kernels for 13%

profile of v2, /device:TPU:0, one launch (start us, length us, event | category | flops | bytes accessed | tf_op | source)
XLA Modules:
  0.0 781.1 jit_solution(2591975957406532165)
XLA Ops:
  28.6 8.9 %all-gather = bf16[8,144,4]{1,2,0:T(4,128)(2,1)S(1)} all-gather(bf16[1,144,4]{1,2,0:T(4,128)(2,1)S(1)} %maximum_bitcast_fusion.9), channel_id=1, replica_groups=mesh['dp'=8,'seq'=4] {'dp'}, dimensions={0}, use_global_device_ids=true | all-gather | bytes 10368 | tf_op jit(solution)/shard_map/all_gather | solution.py:681
  46.4 11.3 %collective-permute-done.2 = bf16[144,1152]{1,0:T(8,128)(2,1)S(1)} collective-permute-done((bf16[144,1152]{1,0:T(8,128)(2,1)}, bf16[144,1152]{1,0:T(8,128)(2,1)S(1)}, u32[]{:S(2)}, u32[]{:S(2)}) %collective-permute-start.2) | collective-permute-done | bytes 331808 | tf_op jit(solution)/shard_map/ppermute | solution.py:531
  57.7 13.7 %collective-permute-done.3 = bf16[144,1152]{1,0:T(8,128)(2,1)S(1)} collective-permute-done((bf16[144,1152]{1,0:T(8,128)(2,1)S(1)}, bf16[144,1152]{1,0:T(8,128)(2,1)S(1)}, u32[]{:S(2)}, u32[]{:S(2)}) %collective-permute-start.3) | collective-permute-done | bytes 331808 | tf_op jit(solution)/shard_map/ppermute | solution.py:531
  76.4 8.4 %collective-permute-done.18 = bf16[192,1152]{1,0:T(8,128)(2,1)S(1)} collective-permute-done((bf16[192,1152]{1,0:T(8,128)(2,1)S(1)}, bf16[192,1152]{1,0:T(8,128)(2,1)S(1)}, u32[]{:S(2)}, u32[]{:S(2)}) %collective-permute-start.18) | collective-permute-done | bytes 442400 | tf_op jit(solution)/shard_map/ppermute | solution.py:531
  110.3 11.6 %collective-permute-done.7 = bf16[2,4,144,512]{3,2,1,0:T(8,128)(2,1)} collective-permute-done((bf16[2,4,144,512]{3,2,1,0:T(8,128)(2,1)}, bf16[2,4,144,512]{3,2,1,0:T(8,128)(2,1)}, u32[]{:S(2)}, u32[]{:S(2)}) %collective-permute-start.7) | collective-permute-done | bytes 1179680 | tf_op jit(solution)/shard_map/ppermute | solution.py:538
  121.9 9.2 %collective-permute-done.5 = bf16[2,4,144,640]{3,2,1,0:T(8,128)(2,1)} collective-permute-done((bf16[2,4,144,640]{3,2,1,0:T(8,128)(2,1)}, bf16[2,4,144,640]{3,2,1,0:T(8,128)(2,1)}, u32[]{:S(2)}, u32[]{:S(2)}) %collective-permute-start.5) | collective-permute-done | bytes 1474592 | tf_op jit(solution)/shard_map/ppermute | solution.py:538
  146.1 14.2 %collective-permute-done.26 = bf16[192,1152]{1,0:T(8,128)(2,1)S(1)} collective-permute-done((bf16[192,1152]{1,0:T(8,128)(2,1)S(1)}, bf16[192,1152]{1,0:T(8,128)(2,1)S(1)}, u32[]{:S(2)}, u32[]{:S(2)}) %collective-permute-start.26) | collective-permute-done | bytes 442400 | tf_op jit(solution)/shard_map/ppermute | solution.py:531
  165.3 8.6 %collective-permute-done.27 = bf16[192,1152]{1,0:T(8,128)(2,1)S(1)} collective-permute-done((bf16[192,1152]{1,0:T(8,128)(2,1)S(1)}, bf16[192,1152]{1,0:T(8,128)(2,1)S(1)}, u32[]{:S(2)}, u32[]{:S(2)}) %collective-permute-start.27) | collective-permute-done | bytes 442400 | tf_op jit(solution)/shard_map/ppermute | solution.py:531
  180.5 6.1 collective-permute-done.28
  197.6 6.3 shard_map.292
  205.3 5.8 collective-permute-start.14
  214.4 6.3 shard_map.290
  228.6 8.7 %shard_map.293 = (f32[256,1152]{1,0:T(8,128)S(1)}, bf16[256,1152]{1,0:T(8,128)(2,1)S(1)}) custom-call(f32[256,1152]{1,0:T(8,128)S(1)} %get-tuple-element.307.delta, f32[256,1152]{1,0:T(8,128)S(1)} %get-tuple-element.306.driven, bf16[256,1152]{1,0:T(8,128)(2,1)S(1)} %get-tuple-element.93.inner, bf16[256,1152]{1,0:T(8,128)(2,1)S(1)} %slice_select_fusion.gate, ...), custom_call_target="tpu_custom_call" | custom-call | bytes 28016640 | tf_op jit(solution)/shard_map/pallas_call | solution.py:334
  238.6 8.3 %shard_map.291 = (f32[256,1152]{1,0:T(8,128)S(1)}, bf16[256,1152]{1,0:T(8,128)(2,1)S(1)}) custom-call(f32[256,1152]{1,0:T(8,128)S(1)} %get-tuple-element.309.delta, f32[256,1152]{1,0:T(8,128)S(1)} %get-tuple-element.308.driven, bf16[256,1152]{1,0:T(8,128)(2,1)S(1)} %get-tuple-element.92.inner, bf16[256,1152]{1,0:T(8,128)(2,1)S(1)} %slice_select_fusion.1.gate, ...), custom_call_target="tpu_custom_call" | custom-call | bytes 28016640 | tf_op jit(solution)/shard_map/pallas_call | solution.py:334
  265.4 18.3 %collective-permute-done.24 = bf16[2,4,192,512]{3,2,1,0:T(8,128)(2,1)} collective-permute-done((bf16[2,4,192,512]{3,2,1,0:T(8,128)(2,1)}, bf16[2,4,192,512]{3,2,1,0:T(8,128)(2,1)}, u32[]{:S(2)}, u32[]{:S(2)}) %collective-permute-start.24) | collective-permute-done | bytes 1572896 | tf_op jit(solution)/shard_map/ppermute | solution.py:538
  289.6 6.3 pad_maximum_fusion
  295.9 18.3 %collective-permute-done.32 = bf16[2,4,192,512]{3,2,1,0:T(8,128)(2,1)} collective-permute-done((bf16[2,4,192,512]{3,2,1,0:T(8,128)(2,1)}, bf16[2,4,192,512]{3,2,1,0:T(8,128)(2,1)}, u32[]{:S(2)}, u32[]{:S(2)}) %collective-permute-start.32) | collective-permute-done | bytes 1572896 | tf_op jit(solution)/shard_map/ppermute | solution.py:538
  316.5 11.9 %collective-permute-done.30 = bf16[2,4,192,640]{3,2,1,0:T(8,128)(2,1)} collective-permute-done((bf16[2,4,192,640]{3,2,1,0:T(8,128)(2,1)}, bf16[2,4,192,640]{3,2,1,0:T(8,128)(2,1)}, u32[]{:S(2)}, u32[]{:S(2)}) %collective-permute-start.30) | collective-permute-done | bytes 1966112 | tf_op jit(solution)/shard_map/ppermute | solution.py:538
  334.0 24.4 %shard_map.294 = (f32[320,1152]{1,0:T(8,128)S(1)}, f32[320,1152]{1,0:T(8,128)S(1)}, bf16[3072,640]{1,0:T(8,128)(2,1)}, bf16[3072,512]{1,0:T(8,128)(2,1)S(1)}, bf...) custom-call(bf16[320,1152]{1,0:T(8,128)(2,1)S(1)} %get-tuple-element.287.buffer, ...), custom_call_target="tpu_custom_call" | custom-call | flops 13589544960 | bytes 28311552 | tf_op jit(solution)/shard_map/pallas_call | solution.py:449
  384.1 6.1 shard_map.295
  398.0 6.5 shard_map.297
  425.2 24.7 %shard_map.296 = (bf16[256,1152]{1,0:T(8,128)(2,1)S(1)}, f32[256,1152]{1,0:T(8,128)S(1)}, f32[16,1152]{1,0:T(8,128)S(1)}, f32[1,1152]{1,0:T(1,128)S(1)}, f32[1,1...) custom-call(f32[256,1152]{1,0:T(8,128)S(1)} %get-tuple-element.309.delta, f32[256,1152]{1,0:T(8,128)S(1)} %copy-done.1, ...), custom_call_target="tpu_custom_call" | custom-call | bytes 82575360 | tf_op jit(solution)/shard_map/pallas_call | solution.py:357
  456.3 24.7 %shard_map.298 = (bf16[256,1152]{1,0:T(8,128)(2,1)S(1)}, f32[256,1152]{1,0:T(8,128)S(1)}, f32[16,1152]{1,0:T(8,128)S(1)}, f32[1,1152]{1,0:T(1,128)S(1)}, f32[1,1...) custom-call(f32[256,1152]{1,0:T(8,128)S(1)} %get-tuple-element.307.delta, ...), custom_call_target="tpu_custom_call" | custom-call | bytes 82575360 | tf_op jit(solution)/shard_map/pallas_call | solution.py:357
  567.2 33.5 %collective-permute-done.61 = bf16[2,4,192,640]{3,2,1,0:T(8,128)(2,1)S(1)} collective-permute-done((bf16[2,4,192,640]{3,2,1,0:T(8,128)(2,1)S(1)}, bf16[2,4,192,640]{3,2,1,0:T(8,128)(2,1)S(1)}, u32[]{:S(2)}, u32[]{:S(2)}) %collective-permute-start.61) | collective-permute-done | bytes 1966112 | tf_op jit(solution)/shard_map/ppermute | solution.py:538
  602.9 14.7 %collective-permute-done.72 = bf16[4,192,512]{2,1,0:T(8,128)(2,1)S(1)} collective-permute-done((bf16[4,192,512]{2,1,0:T(8,128)(2,1)S(1)}, bf16[4,192,512]{2,1,0:T(8,128)(2,1)S(1)}, u32[]{:S(2)}, u32[]{:S(2)}) %collective-permute-start.72) | collective-permute-done | bytes 786464 | tf_op jit(solution)/shard_map/ppermute | solution.py:538
  617.8 13.2 %collective-permute-done.64 = bf16[4,192,512]{2,1,0:T(8,128)(2,1)S(1)} collective-permute-done((bf16[4,192,512]{2,1,0:T(8,128)(2,1)S(1)}, bf16[4,192,512]{2,1,0:T(8,128)(2,1)S(1)}, u32[]{:S(2)}, u32[]{:S(2)}) %collective-permute-start.64) | collective-permute-done | bytes 786464 | tf_op jit(solution)/shard_map/ppermute | solution.py:538
  648.0 9.6 %collective-permute-done.73 = bf16[192,1152]{1,0:T(8,128)(2,1)S(1)} collective-permute-done((bf16[192,1152]{1,0:T(8,128)(2,1)S(1)}, bf16[192,1152]{1,0:T(8,128)(2,1)S(1)}, u32[]{:S(2)}, u32[]{:S(2)}) %collective-permute-start.73) | collective-permute-done | bytes 442400 | tf_op jit(solution)/shard_map/ppermute | solution.py:531
  659.6 20.4 %collective-permute-done.65 = bf16[192,1152]{1,0:T(8,128)(2,1)S(1)} collective-permute-done((bf16[192,1152]{1,0:T(8,128)(2,1)S(1)}, bf16[192,1152]{1,0:T(8,128)(2,1)S(1)}, u32[]{:S(2)}, u32[]{:S(2)}) %collective-permute-start.65) | collective-permute-done | bytes 442400 | tf_op jit(solution)/shard_map/ppermute | solution.py:531
  680.2 10.5 %collective-permute-done.74 = bf16[192,1152]{1,0:T(8,128)(2,1)S(1)} collective-permute-done((bf16[192,1152]{1,0:T(8,128)(2,1)S(1)}, bf16[192,1152]{1,0:T(8,128)(2,1)S(1)}, u32[]{:S(2)}, u32[]{:S(2)}) %collective-permute-start.74) | collective-permute-done | bytes 442400 | tf_op jit(solution)/shard_map/ppermute | solution.py:531
  702.3 7.4 collective-permute-done.75
  717.4 16.2 %collective-permute-done.54 = bf16[2,4,144,640]{3,2,1,0:T(8,128)(2,1)S(1)} collective-permute-done((bf16[2,4,144,640]{3,2,1,0:T(8,128)(2,1)S(1)}, bf16[2,4,144,640]{3,2,1,0:T(8,128)(2,1)S(1)}, u32[]{:S(2)}, u32[]{:S(2)}) %collective-permute-start.54) | collective-permute-done | bytes 1474592 | tf_op jit(solution)/shard_map/ppermute | solution.py:538
  746.0 9.6 %collective-permute-done.58 = bf16[144,1152]{1,0:T(8,128)(2,1)S(1)} collective-permute-done((bf16[144,1152]{1,0:T(8,128)(2,1)S(1)}, bf16[144,1152]{1,0:T(8,128)(2,1)S(1)}, u32[]{:S(2)}, u32[]{:S(2)}) %collective-permute-start.58) | collective-permute-done | bytes 331808 | tf_op jit(solution)/shard_map/ppermute | solution.py:531
  (741 shorter events, 360.1 us)
Async XLA Ops:
  7.2 94.1 %all-gather.4.cloned.1.call-start = ((), (), s32[]{:S(2)}) async-start(), calls=%async_computation.2 | async-start | bytes 1216512 | tf_op jit(solution)/shard_map/all_gather | solution.py:633
  13.5 240.0 %all-gather.6.cloned.1.call-start = ((), (), s32[]{:S(2)}) async-start(), calls=%async_computation.3 | async-start | bytes 5474304 | tf_op jit(solution)/shard_map/all_gather | solution.py:633
  13.6 31.5 %collective-permute-start.1 = (bf16[144,1152]{1,0:T(8,128)(2,1)}, bf16[144,1152]{1,0:T(8,128)(2,1)}, u32[]{:S(2)}, u32[]{:S(2)}) collective-permute-start(bf16[144,1152]{1,0:T(8,128)(2,1)} %bitcast.435), channel_id=1, source_target_pairs={{0,1},{1,2},{2,3},{3,0},{4,5},{5,6},{6,7},{7,4},{8,9},{9,10},{10,1... | collective-permute-start | bytes 995336 | tf_op jit(solution)/shard_map/ppermute | solution.py:531
  26.2 605.1 %reduce-scatter.5.cloned.1.call-start = ((), (), s32[]{:S(2)}) async-start(), calls=%async_computation.4 | async-start | bytes 1216512 | tf_op jit(solution)/shard_map/reduce_scatter | solution.py:638
  89.0 32.8 %collective-permute-start.7 = (bf16[2,4,144,512]{3,2,1,0:T(8,128)(2,1)}, bf16[2,4,144,512]{3,2,1,0:T(8,128)(2,1)}, u32[]{:S(2)}, u32[]{:S(2)}) collective-permute-start(bf16[2,4,144,512]{3,2,1,0:T(8,128)(2,1)} %get-tuple-element.313), channel_id=1, source_target_pairs={{0,8},{4,12},{8,0},{12,4},{16,24},{20,28},{24,16},{28,20},{1,9},{5... | collective-permute-start | bytes 3538952 | tf_op jit(solution)/shard_map/ppermute | solution.py:538
  95.7 35.4 %collective-permute-start.5 = (bf16[2,4,144,640]{3,2,1,0:T(8,128)(2,1)}, bf16[2,4,144,640]{3,2,1,0:T(8,128)(2,1)}, u32[]{:S(2)}, u32[]{:S(2)}) collective-permute-start(bf16[2,4,144,640]{3,2,1,0:T(8,128)(2,1)} %get-tuple-element.291), channel_id=1, source_target_pairs={{0,16},{4,20},{8,24},{12,28},{16,0},{20,4},{24,8},{28,12},{1,17},{... | collective-permute-start | bytes 4423688 | tf_op jit(solution)/shard_map/ppermute | solution.py:538
  99.4 44.6 %collective-permute-start.20 = (bf16[192,1152]{1,0:T(8,128)(2,1)}, bf16[192,1152]{1,0:T(8,128)(2,1)}, u32[]{:S(2)}, u32[]{:S(2)}) collective-permute-start(bf16[192,1152]{1,0:T(8,128)(2,1)} %collective-permute-done.19), channel_id=1, source_target_pairs={{0,1},{1,2},{2,3},{3,0},{4,5},{5,6},{6,7},{7,4},{8,9},{9,10},{10,1... | collective-permute-start | bytes 1327112 | tf_op jit(solution)/shard_map/ppermute | solution.py:531
  135.6 53.9 %collective-permute-start.9 = (bf16[2304,1152]{1,0:T(8,128)(2,1)}, bf16[2304,1152]{1,0:T(8,128)(2,1)}, u32[]{:S(2)}, u32[]{:S(2)}) collective-permute-start(bf16[2304,1152]{1,0:T(8,128)(2,1)} %bitcast.22), channel_id=1, source_target_pairs={{0,4},{4,0},{8,12},{12,8},{16,20},{20,16},{24,28},{28,24},{1,5},{5... | collective-permute-start | bytes 15925256 | tf_op jit(solution)/shard_map/ppermute | solution.py:538
  237.4 46.3 %collective-permute-start.24 = (bf16[2,4,192,512]{3,2,1,0:T(8,128)(2,1)}, bf16[2,4,192,512]{3,2,1,0:T(8,128)(2,1)}, u32[]{:S(2)}, u32[]{:S(2)}) collective-permute-start(bf16[2,4,192,512]{3,2,1,0:T(8,128)(2,1)} %pad_maximum_fusion.11), channel_id=1, source_target_pairs={{0,8},{4,12},{8,0},{12,4},{16,24},{20,28},{24,16},{28,20},{1,9},{5... | collective-permute-start | bytes 4718600 | tf_op jit(solution)/shard_map/ppermute | solution.py:538
  237.8 51.8 %collective-permute-start.22 = (bf16[2,4,192,640]{3,2,1,0:T(8,128)(2,1)}, bf16[2,4,192,640]{3,2,1,0:T(8,128)(2,1)}, u32[]{:S(2)}, u32[]{:S(2)}) collective-permute-start(bf16[2,4,192,640]{3,2,1,0:T(8,128)(2,1)} %pad_maximum_fusion.7), channel_id=1, source_target_pairs={{0,16},{4,20},{8,24},{12,28},{16,0},{20,4},{24,8},{28,12},{1,17},{... | collective-permute-start | bytes 5898248 | tf_op jit(solution)/shard_map/ppermute | solution.py:538
  248.7 65.5 %collective-permute-start.32 = (bf16[2,4,192,512]{3,2,1,0:T(8,128)(2,1)}, bf16[2,4,192,512]{3,2,1,0:T(8,128)(2,1)}, u32[]{:S(2)}, u32[]{:S(2)}) collective-permute-start(bf16[2,4,192,512]{3,2,1,0:T(8,128)(2,1)} %pad_maximum_fusion.12), channel_id=1, source_target_pairs={{0,8},{4,12},{8,0},{12,4},{16,24},{20,28},{24,16},{28,20},{1,9},{5... | collective-permute-start | bytes 4718600 | tf_op jit(solution)/shard_map/ppermute | solution.py:538
  251.8 76.6 %collective-permute-start.30 = (bf16[2,4,192,640]{3,2,1,0:T(8,128)(2,1)}, bf16[2,4,192,640]{3,2,1,0:T(8,128)(2,1)}, u32[]{:S(2)}, u32[]{:S(2)}) collective-permute-start(bf16[2,4,192,640]{3,2,1,0:T(8,128)(2,1)} %pad_maximum_fusion.8), channel_id=1, source_target_pairs={{0,16},{4,20},{8,24},{12,28},{16,0},{20,4},{24,8},{28,12},{1,17},{... | collective-permute-start | bytes 5898248 | tf_op jit(solution)/shard_map/ppermute | solution.py:538
  265.4 51.1 %collective-permute-start.16 = (bf16[160,2304]{1,0:T(8,128)(2,1)S(1)}, bf16[160,2304]{1,0:T(8,128)(2,1)S(1)}, u32[]{:S(2)}, u32[]{:S(2)}) collective-permute-start(bf16[160,2304]{1,0:T(8,128)(2,1)S(1)} %get-tuple-element.288), channel_id=1, source_target_pairs={{0,4},{4,0},{8,12},{12,8},{16,20},{20,16},{24,28},{28,24},{1,5},{5... | collective-permute-start | bytes 2211848 | tf_op jit(solution)/shard_map/ppermute | solution.py:538
  364.1 199.7 %collective-permute-start.69 = (bf16[2,4,192,640]{3,2,1,0:T(8,128)(2,1)}, bf16[2,4,192,640]{3,2,1,0:T(8,128)(2,1)}, u32[]{:S(2)}, u32[]{:S(2)}) collective-permute-start(bf16[2,4,192,640]{3,2,1,0:T(8,128)(2,1)} %bitcast.162), channel_id=1, source_target_pairs={{0,16},{4,20},{8,24},{12,28},{16,0},{20,4},{24,8},{28,12},{1,17},{... | collective-permute-start | bytes 5898248 | tf_op jit(solution)/shard_map/ppermute | solution.py:538
  419.9 137.6 %collective-permute-start.71 = (bf16[2,4,192,512]{3,2,1,0:T(8,128)(2,1)}, bf16[2,4,192,512]{3,2,1,0:T(8,128)(2,1)}, u32[]{:S(2)}, u32[]{:S(2)}) collective-permute-start(bf16[2,4,192,512]{3,2,1,0:T(8,128)(2,1)} %slice_bitcast_fusion), channel_id=1, source_target_pairs={{0,8},{4,12},{8,0},{12,4},{16,24},{20,28},{24,16},{28,20},{1,9},{5... | collective-permute-start | bytes 4718600 | tf_op jit(solution)/shard_map/ppermute | solution.py:538
  421.1 31.5 %collective-permute-start.38 = (bf16[2,16,1152]{2,1,0:T(8,128)(2,1)S(1)}, bf16[2,16,1152]{2,1,0:T(8,128)(2,1)S(1)}, u32[]{:S(2)}, u32[]{:S(2)}) collective-permute-start(bf16[2,16,1152]{2,1,0:T(8,128)(2,1)S(1)} %pad_maximum_fusion.34), channel_id=1, source_target_pairs={{1,0},{2,1},{3,2},{5,4},{6,5},{7,6},{9,8},{10,9},{11,10},{13,12},{... | collective-permute-start | bytes 221192 | tf_op jit(solution)/shard_map/ppermute | solution.py:479
  422.4 31.6 %collective-permute-start.39 = (bf16[2,16,1152]{2,1,0:T(8,128)(2,1)S(1)}, bf16[2,16,1152]{2,1,0:T(8,128)(2,1)S(1)}, u32[]{:S(2)}, u32[]{:S(2)}) collective-permute-start(bf16[2,16,1152]{2,1,0:T(8,128)(2,1)S(1)} %pad_maximum_fusion.34), channel_id=1, source_target_pairs={{2,0},{3,1},{6,4},{7,5},{10,8},{11,9},{14,12},{15,13},{18,16},{19,... | collective-permute-start | bytes 221192 | tf_op jit(solution)/shard_map/ppermute | solution.py:479
  423.7 32.4 %collective-permute-start.40 = (bf16[2,16,1152]{2,1,0:T(8,128)(2,1)S(1)}, bf16[2,16,1152]{2,1,0:T(8,128)(2,1)S(1)}, u32[]{:S(2)}, u32[]{:S(2)}) collective-permute-start(bf16[2,16,1152]{2,1,0:T(8,128)(2,1)S(1)} %pad_maximum_fusion.34), channel_id=1, source_target_pairs={{3,0},{7,4},{11,8},{15,12},{19,16},{23,20},{27,24},{31,28}} | collective-permute-start | bytes 221192 | tf_op jit(solution)/shard_map/ppermute | solution.py:479
  452.6 108.6 %collective-permute-start.63 = (bf16[2,4,192,512]{3,2,1,0:T(8,128)(2,1)}, bf16[2,4,192,512]{3,2,1,0:T(8,128)(2,1)}, u32[]{:S(2)}, u32[]{:S(2)}) collective-permute-start(bf16[2,4,192,512]{3,2,1,0:T(8,128)(2,1)} %slice_bitcast_fusion.2), channel_id=1, source_target_pairs={{0,8},{4,12},{8,0},{12,4},{16,24},{20,28},{24,16},{28,20},{1,9},{5... | collective-permute-start | bytes 4718600 | tf_op jit(solution)/shard_map/ppermute | solution.py:538
  454.0 78.2 %collective-permute-start.51 = (f32[4,1152]{1,0:T(4,128)}, f32[4,1152]{1,0:T(4,128)}, u32[]{:S(2)}, u32[]{:S(2)}) collective-permute-start(f32[4,1152]{1,0:T(4,128)} %add.466), channel_id=1, source_target_pairs={{0,1},{1,0},{2,3},{3,2},{4,5},{5,4},{6,7},{7,6},{8,9},{9,8},{10,11... | collective-permute-start | bytes 55304 | tf_op jit(solution)/shard_map/ppermute | solution.py:646
  508.0 262.8 %reduce-scatter.7.cloned.1.call-start = ((), (), s32[]{:S(2)}) async-start(), calls=%async_computation.5 | async-start | bytes 5474304
  551.5 49.2 %collective-permute-start.61 = (bf16[2,4,192,640]{3,2,1,0:T(8,128)(2,1)S(1)}, bf16[2,4,192,640]{3,2,1,0:T(8,128)(2,1)S(1)}, u32[]{:S(2)}, u32[]{:S(2)}) collective-permute-start(bf16[2,4,192,640]{3,2,1,0:T(8,128)(2,1)S(1)} %bitcast.422), channel_id=1, source_target_pairs={{0,16},{4,20},{8,24},{12,28},{16,0},{20,4},{24,8},{28,12},{1,17},{... | collective-permute-start | bytes 5898248 | tf_op jit(solution)/shard_map/ppermute | solution.py:538
  556.8 136.1 %collective-permute-start.53 = (bf16[2304,1152]{1,0:T(8,128)(2,1)}, bf16[2304,1152]{1,0:T(8,128)(2,1)}, u32[]{:S(2)}, u32[]{:S(2)}) collective-permute-start(bf16[2304,1152]{1,0:T(8,128)(2,1)} %convolution_convert_fusion), channel_id=1, source_target_pairs={{0,4},{4,0},{8,12},{12,8},{16,20},{20,16},{24,28},{28,24},{1,5},{5... | collective-permute-start | bytes 15925256 | tf_op jit(solution)/shard_map/ppermute | solution.py:538
  559.6 58.0 %collective-permute-start.72 = (bf16[4,192,512]{2,1,0:T(8,128)(2,1)S(1)}, bf16[4,192,512]{2,1,0:T(8,128)(2,1)S(1)}, u32[]{:S(2)}, u32[]{:S(2)}) collective-permute-start(bf16[4,192,512]{2,1,0:T(8,128)(2,1)S(1)} %slice_bitcast_fusion.10), channel_id=1, source_target_pairs={{0,16},{4,20},{8,24},{12,28},{16,0},{20,4},{24,8},{28,12},{1,17},{... | collective-permute-start | bytes 2359304 | tf_op jit(solution)/shard_map/ppermute | solution.py:538
  563.2 67.8 %collective-permute-start.64 = (bf16[4,192,512]{2,1,0:T(8,128)(2,1)S(1)}, bf16[4,192,512]{2,1,0:T(8,128)(2,1)S(1)}, u32[]{:S(2)}, u32[]{:S(2)}) collective-permute-start(bf16[4,192,512]{2,1,0:T(8,128)(2,1)S(1)} %slice_bitcast_fusion.11), channel_id=1, source_target_pairs={{0,16},{4,20},{8,24},{12,28},{16,0},{20,4},{24,8},{28,12},{1,17},{... | collective-permute-start | bytes 2359304 | tf_op jit(solution)/shard_map/ppermute | solution.py:538
  567.0 75.2 %collective-permute-start.70 = (bf16[4,192,640]{2,1,0:T(8,128)(2,1)}, bf16[4,192,640]{2,1,0:T(8,128)(2,1)}, u32[]{:S(2)}, u32[]{:S(2)}) collective-permute-start(bf16[4,192,640]{2,1,0:T(8,128)(2,1)} %slice_bitcast_fusion.8), channel_id=1, source_target_pairs={{0,8},{4,12},{8,0},{12,4},{16,24},{20,28},{24,16},{28,20},{1,9},{5... | collective-permute-start | bytes 2949128 | tf_op jit(solution)/shard_map/ppermute | solution.py:538
  602.3 42.2 %collective-permute-start.62 = (bf16[4,192,640]{2,1,0:T(8,128)(2,1)}, bf16[4,192,640]{2,1,0:T(8,128)(2,1)}, u32[]{:S(2)}, u32[]{:S(2)}) collective-permute-start(bf16[4,192,640]{2,1,0:T(8,128)(2,1)} %slice_bitcast_fusion.9), channel_id=1, source_target_pairs={{0,8},{4,12},{8,0},{12,4},{16,24},{20,28},{24,16},{28,20},{1,9},{5... | collective-permute-start | bytes 2949128 | tf_op jit(solution)/shard_map/ppermute | solution.py:538
  646.2 33.8 %collective-permute-start.65 = (bf16[192,1152]{1,0:T(8,128)(2,1)S(1)}, bf16[192,1152]{1,0:T(8,128)(2,1)S(1)}, u32[]{:S(2)}, u32[]{:S(2)}) collective-permute-start(bf16[192,1152]{1,0:T(8,128)(2,1)S(1)} %dynamic-slice_bitcast_fusion.9), channel_id=1, source_target_pairs={{0,3},{1,0},{2,1},{3,2},{4,7},{5,4},{6,5},{7,6},{8,11},{9,8},{10,9... | collective-permute-start | bytes 1327112 | tf_op jit(solution)/shard_map/ppermute | solution.py:531
  657.7 33.0 %collective-permute-start.74 = (bf16[192,1152]{1,0:T(8,128)(2,1)S(1)}, bf16[192,1152]{1,0:T(8,128)(2,1)S(1)}, u32[]{:S(2)}, u32[]{:S(2)}) collective-permute-start(bf16[192,1152]{1,0:T(8,128)(2,1)S(1)} %fusion.43), channel_id=1, source_target_pairs={{0,3},{1,0},{2,1},{3,2},{4,7},{5,4},{6,5},{7,6},{8,11},{9,8},{10,9... | collective-permute-start | bytes 1327112 | tf_op jit(solution)/shard_map/ppermute | solution.py:531
  698.2 35.4 %collective-permute-start.54 = (bf16[2,4,144,640]{3,2,1,0:T(8,128)(2,1)S(1)}, bf16[2,4,144,640]{3,2,1,0:T(8,128)(2,1)S(1)}, u32[]{:S(2)}, u32[]{:S(2)}) collective-permute-start(bf16[2,4,144,640]{3,2,1,0:T(8,128)(2,1)S(1)} %slice_bitcast_fusion.4), channel_id=1, source_target_pairs={{0,16},{4,20},{8,24},{12,28},{16,0},{20,4},{24,8},{28,12},{1,17},{... | collective-permute-start | bytes 4423688 | tf_op jit(solution)/shard_map/ppermute | solution.py:538
  700.4 34.7 %collective-permute-start.67 = (bf16[192,1152]{1,0:T(8,128)(2,1)S(1)}, bf16[192,1152]{1,0:T(8,128)(2,1)S(1)}, u32[]{:S(2)}, u32[]{:S(2)}) collective-permute-start(bf16[192,1152]{1,0:T(8,128)(2,1)S(1)} %fusion.47), channel_id=1, source_target_pairs={{0,3},{1,0},{2,1},{3,2},{4,7},{5,4},{6,5},{7,6},{8,11},{9,8},{10,9... | collective-permute-start | bytes 1327112 | tf_op jit(solution)/shard_map/ppermute | solution.py:531
  709.9 36.1 %collective-permute-start.76 = (bf16[96,1152]{1,0:T(8,128)(2,1)S(1)}, bf16[96,1152]{1,0:T(8,128)(2,1)S(1)}, u32[]{:S(2)}, u32[]{:S(2)}) collective-permute-start(bf16[96,1152]{1,0:T(8,128)(2,1)S(1)} %split.19), channel_id=1, source_target_pairs={{0,4},{4,0},{8,12},{12,8},{16,20},{20,16},{24,28},{28,24},{1,5},{5... | collective-permute-start | bytes 663560 | tf_op jit(solution)/shard_map/ppermute | solution.py:538
  (195 other events, 2418.7 us)
Sparse Core Ops, SparseCore 0:
  13.6 58.1 all-gather.3
  74.6 71.8 all-gather.5
  508.1 99.8 reduce-scatter.4
  613.6 146.3 reduce-scatter.6

commit v3 on v2

--- a/solution.py
+++ b/solution.py
@@ -255,9 +255,7 @@
     front_grad[...] = ext[3 * SEG :, :]
 
 
-def expert_kernel(
-    buffer, grads, up, down, returned, buffer_grad, up_left, up_right, down_left, down_right
-):
+def expert_kernel(at, buffer, grads, up, down, returned, buffer_grad, weight_grads):
     def product(left, right, contract):
         return lax.dot_general(
             left, right, (contract, ((), ())), preferred_element_type=jnp.float32
@@ -269,21 +267,18 @@
         buffer_grad[...] = jnp.zeros_like(buffer_grad)
 
     values, cot = buffer[...], grads[...]
-    hidden = product(values, up[...], ((1,), (1,)))
+    ups, downs = (w[...].reshape(-1, values.shape[1]) for w in (up, down))
+    hidden = product(values, ups, ((1,), (1,)))
     below = 0.5 * (1.0 + lax.erf(hidden * math.sqrt(0.5)))
     density = jnp.exp(-0.5 * hidden * hidden) * (1.0 / math.sqrt(2.0 * math.pi))
     active = (hidden * below).astype(jnp.bfloat16)
-    active_grad = product(cot, down[...], ((1,), (1,)))
+    active_grad = product(cot, downs, ((1,), (1,)))
     hidden_grad = (active_grad * (below + hidden * density)).astype(jnp.bfloat16)
-    returned[...] += product(active, down[...], ((1,), (0,)))
-    buffer_grad[...] += product(hidden_grad, up[...], ((1,), (0,)))
-    cut = up_left.shape[1]
-    down_grad = product(active, cot, ((0,), (0,))).astype(jnp.bfloat16)
-    down_left[...] = down_grad[:, :cut]
-    down_right[...] = down_grad[:, cut:]
-    up_grad = product(hidden_grad, values, ((0,), (0,))).astype(jnp.bfloat16)
-    up_left[...] = up_grad[:, :cut]
-    up_right[...] = up_grad[:, cut:]
+    returned[...] += product(active, downs, ((1,), (0,)))
+    buffer_grad[...] += product(hidden_grad, ups, ((1,), (0,)))
+    pieces = weight_grads.shape[0], weight_grads.shape[3], weight_grads.shape[4]
+    for k, (left, right) in enumerate(((hidden_grad, values), (active, cot))):
+        weight_grads[:, 0, k] = product(left, right, ((0,), (0,))).astype(jnp.bfloat16).reshape(pieces)
 
 
 def column_specs(rows, width):
@@ -305,7 +300,7 @@
 
 def cost(rows, channels, passes):
     return pl.CostEstimate(
-        flops=0, bytes_accessed=int(rows * channels * passes), transcendentals=0
+        flops=0, bytes_accessed=int(rows * channels * passes) // 4, transcendentals=0
     )
 
 
@@ -439,25 +434,52 @@
     )(front, same, taps, conv_sum, inner_part, select_low, select)
 
 
-def expert_pass(buffer, grads, up, down, tile):
+def expert_pass(core, buffer, grads, weights, depth):
     slots, width = buffer.shape
-    units = up.shape[0]
-    whole = pl.BlockSpec((slots, width), lambda j: (0, 0))
-    strip = pl.BlockSpec((tile, width), lambda j: (j, 0))
-    cut = cut_of(width)
-    sizes = [cut, width - cut] * 2
-    return pl.pallas_call(
+    devices, _, part, _ = weights.shape
+    direct = part % 16 == 0
+    if direct:
+        tile, strip = depth, part
+    else:
+        tile, strip = 1, depth * part
+        weights = weights.swapaxes(0, 1).reshape(1, 4, devices * part, width)
+    steps = devices // depth
+    whole = pl.BlockSpec((slots, width), lambda j, at: (0, 0))
+
+    def weight(k):
+        def place(j, at):
+            return (j, 2 * at[0] + k, 0, 0) if direct else (0, 2 * at[0] + k, j, 0)
+
+        return pl.BlockSpec((tile, 1, strip, width), place)
+
+    returned, buffer_grad, weight_grads = pl.pallas_call(
         expert_kernel,
-        grid=(units // tile,),
-        in_specs=[whole, whole, strip, strip],
-        out_specs=[whole, whole] + [pl.BlockSpec((tile, n), lambda j: (j, 0)) for n in sizes],
+        grid_spec=pltpu.PrefetchScalarGridSpec(
+            num_scalar_prefetch=1,
+            grid=(steps,),
+            in_specs=[whole, whole, weight(0), weight(1)],
+            out_specs=[
+                whole,
+                whole,
+                pl.BlockSpec(
+                    (tile, 1, 2, strip, width),
+                    lambda j, at: (lax.div(j, 2), lax.rem(j, 2), 0, 0, 0),
+                ),
+            ],
+        ),
         out_shape=[jax.ShapeDtypeStruct((slots, width), jnp.float32)] * 2
-        + [jax.ShapeDtypeStruct((units, n), jnp.bfloat16) for n in sizes],
-        compiler_params=params(40),
+        + [jax.ShapeDtypeStruct((steps // 2 * tile, 2, 2, strip, width), jnp.bfloat16)],
+        compiler_params=params(52),
         cost_estimate=pl.CostEstimate(
-            flops=12 * slots * width * units, bytes_accessed=8 * units * width, transcendentals=0
+            flops=12 * slots * width * devices * part,
+            bytes_accessed=8 * devices * part * width,
+            transcendentals=0,
         ),
-    )(buffer, grads, up, down)
+    )(core.reshape(1).astype(jnp.int32), buffer, grads, weights, weights)
+    if not direct:
+        parts = weight_grads.reshape(steps // 2, 2, 2, depth, part, width)
+        weight_grads = parts.transpose(0, 3, 1, 2, 4, 5).reshape(-1, 2, 2, part, width)
+    return returned, buffer_grad, weight_grads
 
 
 MODEL_WIDTH = 1152
@@ -495,13 +517,17 @@
     return jnp.concatenate([front.reshape((REACH * SEG,) + array.shape[1:]), array])
 
 
-def entering(decay, value, reverse):
-    pair = jnp.stack([decay, value]).astype(BF16)
-    state = jnp.zeros_like(value)
-    for k in range(lax.axis_size("seq") - 1, 0, -1):
-        part = passed_along(pair, "seq", -k if reverse else k).astype(F32)
-        state = part[0] * state + part[1]
-    return state
+def entering(decays, values, reverse):
+    size, mine = lax.axis_size("seq"), lax.axis_index("seq")
+    pairs = jnp.stack([jnp.concatenate(decays, 1), jnp.concatenate(values, 1)]).astype(BF16)
+    gathered = lax.all_gather(pairs, "seq")
+    state = jnp.zeros(pairs.shape[1:], F32)
+    for k in range(size):
+        at = size - 1 - k if reverse else k
+        reached = at > mine if reverse else at < mine
+        part = gathered[at].astype(F32)
+        state = jnp.where(reached, part[0] * state + part[1], state)
+    return jnp.split(state, 2, 1)
 
 
 def silu_slope(value):
@@ -542,11 +568,11 @@
     return lax.axis_size("seq") if axis == "z" else 2 if axis == "core" else sides()
 
 
-def ring_gather(block, axis):
+def ring_gather(block, axis, absolute=False):
     pieces = [block]
-    for _ in range(size_of(axis) - 1):
-        pieces.append(moved(pieces[-1], axis))
-    if axis == "z":
+    for k in range(1, size_of(axis)):
+        pieces.append(moved(block, axis, k))
+    if absolute:
         whole = jnp.zeros((len(pieces),) + block.shape, block.dtype)
         for k, piece in enumerate(pieces):
             whole = lax.dynamic_update_index_in_dim(whole, piece, depth_of(k), 0)
@@ -563,14 +589,14 @@
     return (left.astype(F32) + right.astype(F32)).astype(BF16)
 
 
-def ring_scatter(parts, axis):
-    if axis == "z":
-        size = size_of(axis)
+def ring_scatter(parts, axis, absolute=False):
+    size = size_of(axis)
+    if absolute:
         parts = [lax.dynamic_index_in_dim(parts, depth_of(k), 0, False) for k in range(size)]
-    total = parts[-1]
-    for k in range(size_of(axis) - 2, -1, -1):
-        total = added(parts[k], moved(total, axis, -1))
-    return total
+    total = parts[0].astype(F32)
+    for k in range(1, size):
+        total = total + moved(parts[k], axis, -k).astype(F32)
+    return total.astype(BF16)
 
 
 def cut_of(columns):
@@ -578,36 +604,37 @@
 
 
 def after(value, *others):
-    if not others:
-        return value
-    return lax.optimization_barrier((value, *others))[0]
-
-
-def plane_gather(block, waits=((), (), ())):
-    cut = cut_of(block.shape[1])
-    pieces = ring_gather(after(block, *waits[0]), "z")
-    first = after(pieces, *waits[1])
-    left = after(ring_gather(first[..., :cut], "x"), *waits[2])
-    right = after(ring_gather(first[..., cut:], "y"), *waits[2])
-    left, right = ring_gather(left, "y"), ring_gather(right, "x")
-    return jnp.concatenate([left, right.swapaxes(0, 1)], -1), pieces, (left, right)
-
-
-def plane_scatter(left, right, waits=((), ())):
-    left = after(ring_scatter(left, "y"), *waits[0])
-    right = after(ring_scatter(right.swapaxes(0, 1), "x"), *waits[0])
-    left, right = ring_scatter(left, "x"), ring_scatter(right, "y")
-    return ring_scatter(after(jnp.concatenate([left, right], -1), *waits[1]), "z")
+    mark = sum(other[(0,) * other.ndim].astype(F32) for other in others)
+    return jnp.where(mark != mark, jnp.zeros_like(value), value)
+
+
+def wide_gather(pieces):
+    cut = cut_of(pieces.shape[-1])
+    left = ring_gather(pieces[..., :cut], "x")
+    right = ring_gather(pieces[..., cut:], "y")
+    return left, right
+
+
+def last_gather(left, right):
+    return ring_gather(left, "y"), ring_gather(right, "x")
+
+
+def first_scatter(left, right):
+    return ring_scatter(left, "y"), ring_scatter(right, "x")
+
+
+def second_scatter(left, right):
+    return jnp.concatenate([ring_scatter(left, "x"), ring_scatter(right, "y")], -1)
 
 
 def by_place(pieces, axis):
     size = size_of(axis)
-    mine = lax.axis_index("dp") // (2 * sides())
+    mine = lax.axis_index("dp") // {"core": 1, "x": 2, "y": 2 * sides()}[axis]
     order = []
     for j in range(size):
         piece = pieces[size - 1]
         for k in range(size - 1):
-            piece = jnp.where(lax.rem(mine - j + size, size) == k, pieces[k], piece)
+            piece = jnp.where(lax.rem(lax.rem(mine, size) - j + size, size) == k, pieces[k], piece)
         order.append(piece)
     return order
 
@@ -629,13 +656,52 @@
     return [jnp.stack([r[c] for r in rows], 1).reshape((-1,) + whole.shape[1:]) for c in range(2)]
 
 
-def unit_gather(block):
-    return unit_blocks(lax.all_gather(block, BOTH, axis=0, tiled=True))
-
-
-def unit_scatter(grads):
-    whole = unit_blocks(jnp.concatenate(grads), True)
-    return lax.psum_scatter(whole, BOTH, scatter_dimension=0, tiled=True).astype(F32)
+def unit_pairs():
+    side, depth = sides(), lax.axis_size("seq")
+    half = max(side // 2, 1)
+    pairs = []
+    for unit in range(lax.axis_size("dp") * depth):
+        k, b = unit // 2, unit % 2
+        high, low = divmod(k, side * 2 * depth)
+        pairs.append((unit, (high + b * half) * side * 2 * depth + low))
+    return pairs
+
+
+def halved_scatter(whole):
+    size, depth = lax.axis_size("dp"), lax.axis_size("seq")
+    rest = whole.reshape((size, depth, -1) + whole.shape[1:])
+    for axis, at in (("dp", 0), ("seq", 1)):
+        count, mine = lax.axis_size(axis), lax.axis_index(axis)
+        bits = [1 << k for k in range(count.bit_length() - 1)]
+        for bit in bits:
+            parts = rest.reshape(rest.shape[:at] + (rest.shape[at] // 2, 2) + rest.shape[at + 1 :])
+            low, high = (lax.index_in_dim(parts, k, at + 1, False) for k in range(2))
+            own = (mine & bit) == 0
+            sent = jnp.where(own, high, low)
+            got = lax.ppermute(sent, axis, [(i, i ^ bit) for i in range(count)])
+            rest = added(jnp.where(own, low, high), got)
+            yield rest
+
+
+def units_in_order(near, far):
+    side, depth = sides(), lax.axis_size("seq")
+    cores = []
+    for part in by_place([near, far], "core"):
+        rows = by_place([part[k] for k in range(side)], "y")
+        cores.append(jnp.stack([jnp.stack(by_place([r[k] for k in range(side)], "x")) for r in rows]))
+    whole = jnp.stack(cores, 2)
+    whole = whole.reshape(side, side, 2, depth, 2, -1, whole.shape[-1])
+    whole = jnp.concatenate([whole[..., 0, :, :], whole[..., 1, :, :]], -1)
+    return whole.reshape(-1, whole.shape[-1])
+
+
+def plane_rows(plane):
+    side, depth = sides(), lax.axis_size("seq")
+    columns = plane.shape[1]
+    parts = plane.reshape(side // 2, side, depth, 2, -1, columns)
+    parts = jnp.stack(by_place([parts[:, k] for k in range(side)], "x"))
+    parts = parts.transpose(3, 1, 0, 2, 4, 5).reshape(side * side, depth, -1, columns)
+    return jnp.pad(parts, ((0, 0), (0, 0), (0, -parts.shape[2] % 32), (0, 0)))
 
 
 def everywhere(array):
@@ -676,8 +742,10 @@
     side, depth = sides(), lax.axis_size("seq")
     both = range(2)
 
-    prior_tokens = passed_along(tokens[0, rows - REACH :], "seq", 1)
-    prior_doc = passed_along(doc_ids[0, rows - REACH :], "seq", 1)
+    last_doc = jnp.broadcast_to(doc_ids[0, rows - REACH :, None].astype(BF16), (REACH, LANE))
+    prior = passed_along(jnp.concatenate([tokens[0, rows - REACH :], last_doc], 1), "seq", 1)
+    prior_tokens = prior[:, :MODEL_WIDTH]
+    prior_doc = prior[:, MODEL_WIDTH].astype(jnp.int32)
     lines = lax.all_gather(jnp.concatenate([norm_gains, router.T]), "dp", axis=1, tiled=True)
     gains_all = lines[:2].astype(F32)
     router_all = lines[2:].astype(F32)
@@ -695,20 +763,23 @@
         1,
     )
     columns = small.shape[1]
-    spare = -columns % LANE
-
-    def expert_block(shards):
-        own = jnp.where(core == 0, shards[0], shards[1])
-        other = jnp.where(core == 0, shards[1], shards[0])
-        return jnp.concatenate([own, moved(other, "core")])
-
-    in_near, in_z, _ = plane_gather(in_proj.T)
-    in_near = in_near.reshape(DI, MODEL_WIDTH)
+
+    small = jnp.pad(small, ((0, 0), (0, 2 * LANE - columns)))
+    small = jnp.concatenate([small[:, :LANE], small[:, LANE:]])
+    in_z = ring_gather(jnp.concatenate([in_proj.T, small], 1), "z", True)
+    in_wide = wide_gather(in_z)
+    left, right = last_gather(*in_wide)
+    right = right.swapaxes(0, 1)
+    rest = MODEL_WIDTH - left.shape[-1]
+    in_near = jnp.concatenate([left, right[..., :rest]], -1).reshape(DI, MODEL_WIDTH)
     in_full = (in_near, moved(in_near, "core"))
-    small_full = unit_gather(jnp.pad(small, ((0, 0), (0, spare))))
-    out_full = unit_gather(out_proj)
-    up_block = expert_block(expert_up.swapaxes(1, 2))
-    down_block = expert_block(expert_down)
+    small_near = right[..., rest:]
+    small_full = unit_blocks(units_in_order(small_near, moved(small_near, "core")))
+    out_full = unit_blocks(lax.all_gather(out_proj, BOTH, axis=0, tiled=True))
+    experts = jnp.stack([expert_up.swapaxes(1, 2), expert_down], 1)
+    experts = after(experts.reshape(-1, MODEL_WIDTH), in_z)
+    experts = lax.all_gather(experts, BOTH, axis=0, tiled=True)
+    experts = experts.reshape(lax.axis_size("dp") * depth, 4, -1, MODEL_WIDTH)
 
     at = R + 2 * NS
     select_full = [w[:, :at] for w in small_full]
@@ -759,17 +830,11 @@
     driven = [d * x.astype(F32) for d, x in zip(delta, inner)]
     rate = [r * math.log2(math.e) for r in decay_rate]
 
-    up_full, up_z, up_side = plane_gather(
-        up_block, ((in_z,), (in_near,), tuple(x[:SEG] for x in inner))
-    )
-    pre, state_in, marks = [], [], []
-    for h in both:
-        *ends, all_decay, all_state = segment_ends(
-            delta[h], driven[h], kept, in_select, rate[h], False, wide
-        )
-        marks.append(all_decay)
-        pre.append(ends)
-        state_in.append(entering(all_decay, all_state, False))
+    ends = [
+        segment_ends(delta[h], driven[h], kept, in_select, rate[h], False, wide) for h in both
+    ]
+    pre = [e[:2] for e in ends]
+    state_in = entering([e[2] for e in ends], [e[3] for e in ends], False)
     scanned, gated = zip(
         *(
             scan_output(
@@ -779,10 +844,6 @@
             for h in both
         )
     )
-    down_full, _, _ = plane_gather(
-        down_block, ((up_z,), tuple(marks), tuple(g[:SEG] for g in gated))
-    )
-    up_full, down_full = (w.reshape(-1, MODEL_WIDTH) for w in (up_full, down_full))
     mixed = sum(dot(gated[h], out_full[h], ((1,), (0,))) for h in both)
     resid = stream + mixed
     inv_second = lax.rsqrt(jnp.mean(resid * resid, -1, keepdims=True) + EPS)
@@ -809,18 +870,14 @@
         parts = jnp.concatenate([parts[:slots_per], moved(parts[slots_per:], "core")])
         return dot(pick.astype(F32), parts, ((0,), (0,)), HIGHEST)
 
-    def expert_scatter(left, right, waits):
-        left, right = (g.reshape(side, side, depth, -1, g.shape[1]) for g in (left, right))
-        own, other = jnp.split(plane_scatter(left, right, waits), 2)
-        other = moved(other, "core")
-        pair = jnp.where(core == 0, own, other), jnp.where(core == 0, other, own)
-        return jnp.stack(pair).astype(F32)
-
-    returned, buffer_grad, *expert_grads = expert_pass(
-        buffer, grad_slots, up_full, down_full, up_full.shape[0] // 12
-    )
+    gated_other = moved(gated[1], "core")
+    returned, buffer_grad, expert_grads = expert_pass(core, buffer, grad_slots, experts, depth)
     returned = from_slots(returned)
     buffer_grad = from_slots(buffer_grad)
+    groups = [list(range(c, lax.axis_size("dp"), 2)) for c in range(2)]
+    expert_sum = lax.psum_scatter(
+        expert_grads, "dp", scatter_dimension=0, tiled=True, axis_index_groups=groups
+    )
     branch = chosen * returned
     layer_out = (resid + branch).astype(BF16)
     squared_values = jnp.stack(
@@ -836,35 +893,44 @@
         scaled_second - hat_second * jnp.mean(scaled_second * hat_second, -1, keepdims=True)
     )
     mixed_grad = resid_grad.astype(BF16)
+    crossed = moved(jnp.concatenate([mixed_grad, normed]), "core")
+    gated_near = jnp.concatenate([gated[0], gated_other])
+    grad_out = dot(gated_near, jnp.concatenate([mixed_grad, crossed[:rows]]), ((0,), (0,)))
     gated_grad = [dot(mixed_grad, out_full[h], ((1,), (1,))) for h in both]
     gates = [g.astype(F32) for g in gate]
     scan_grad = [gated_grad[h] * jax.nn.silu(gates[h]) for h in both]
     gate_grad = [(gated_grad[h] * scanned[h] * silu_slope(gates[h])).astype(BF16) for h in both]
-    post, adjoint_in = [], []
-    for h in both:
-        *ends, all_decay, all_adjoint = segment_ends(
-            delta[h], scan_grad[h], kept, out_select, rate[h], True, wide
+    ends = [
+        segment_ends(delta[h], scan_grad[h], kept, out_select, rate[h], True, wide) for h in both
+    ]
+    post = [e[:2] for e in ends]
+    adjoint_in = entering([e[2] for e in ends], [e[3] for e in ends], True)
+    out_sum = lax.psum_scatter(
+        plane_rows(grad_out.astype(BF16)), "dp", scatter_dimension=0, tiled=True,
+        axis_index_groups=groups,
+    )[0]
+    expert_sum = expert_sum.reshape(depth, -1, MODEL_WIDTH)
+    own_rows = expert_sum.shape[1]
+    both_sum = lax.psum_scatter(
+        jnp.concatenate([expert_sum, out_sum], 1), "seq", scatter_dimension=0, tiled=True
+    )[0]
+    out_sum = both_sum[own_rows : own_rows + out_proj.shape[0]]
+    out_sum = lax.ppermute(out_sum, BOTH, [(b, a) for a, b in unit_pairs()]).astype(F32)
+    expert_sum = both_sum[:own_rows].reshape(2, 2, -1, MODEL_WIDTH)
+    mine_sum = jnp.where(core == 0, expert_sum[0], expert_sum[1])
+    other_sum = moved(jnp.where(core == 0, expert_sum[1], expert_sum[0]), "core")
+    expert_sum = jnp.stack(
+        [jnp.where(core == e, mine_sum, other_sum) for e in range(EXPERT_COUNT)]
+    ).astype(F32)
+    rate = [after(r, grad_out) for r in rate]
+    made = [
+        scan_adjoint(
+            delta[h], driven[h], inner[h], scan_grad[h], step_pre[h], kept, in_select, out_select,
+            rate[h], skip_wide[h], pre[h], state_in[h], post[h], adjoint_in[h], wide,
         )
-        post.append(ends)
-        marks.append(all_decay)
-        adjoint_in.append(entering(all_decay, all_adjoint, True))
-    out_sum = unit_scatter(
-        [dot(gated[h], mixed_grad, ((0,), (0,))).astype(BF16) for h in both]
-    )
-    pre_low, inner_part, rate_sum, step_sum, skip_sum, in_grad, out_grads = zip(
-        *(
-            scan_adjoint(
-                delta[h], driven[h], inner[h], scan_grad[h], step_pre[h], kept, in_select,
-                out_select, rate[h], skip_wide[h], pre[h], state_in[h], post[h], adjoint_in[h],
-                wide,
-            )
-            for h in both
-        )
-    )
-    down_sum = expert_scatter(
-        *expert_grads[2:], (tuple(marks[2:]), (step_sum[0],))
-    )
-    up_sum = expert_scatter(*expert_grads[:2], ((step_sum[0],), (step_sum[1],)))
+        for h in both
+    ]
+    pre_low, inner_part, rate_sum, step_sum, skip_sum, in_grad, out_grads = map(list, zip(*made))
     steps_grad = sum(dot(pre_low[h], step_full[h], ((1,), (0,))) for h in both)
     select_low = jnp.concatenate(
         [steps_grad, in_grad[0] + in_grad[1], out_grads[0] + out_grads[1]], 1
@@ -887,7 +953,7 @@
                     dot(inner[h], select_low, ((0,), (0,))),
                     dot(pre_low[h], steps_low, ((0,), (0,))),
                     jnp.concatenate(lines).T,
-                    jnp.zeros((half, spare), F32),
+                    jnp.zeros((half, -columns % LANE), F32),
                 ],
                 1,
             ).astype(BF16)
@@ -900,12 +966,16 @@
         whole = jnp.concatenate([(front_grad[h] + tail).astype(BF16), gate_grad[h]], 1)
         parts = [whole[:, k * strip : (k + 1) * strip] for k in range(side)]
         proj_grad.append(jnp.concatenate(by_place(parts, "y"), 1))
-    grad_in = [dot(proj_grad[h], normed, ((0,), (0,))).astype(BF16) for h in (1, 0)]
-    in_plane = added(grad_in[1], moved(grad_in[0], "core"))
-    in_plane = in_plane.reshape(side, side, depth, -1, MODEL_WIDTH)
+    proj_other = moved(proj_grad[1], "core")
+    grad_in = dot(
+        jnp.concatenate([proj_grad[0], proj_other]),
+        jnp.concatenate([normed, crossed[rows:]]),
+        ((0,), (0,)),
+    ).astype(BF16)
+    in_plane = grad_in.reshape(side, side, depth, -1, MODEL_WIDTH)
     cut = cut_of(MODEL_WIDTH)
-    in_sum = plane_scatter(in_plane[..., :cut], in_plane[..., cut:]).astype(F32)
-    small_sum = unit_scatter(grad_small)
+    in_plane = first_scatter(in_plane[..., :cut], in_plane[..., cut:].swapaxes(0, 1))
+    grad_small = [after(g, grad_in) for g in grad_small]
     normed_grad = sum(dot(proj_grad[h], in_full[h], ((1,), (0,))) for h in both)
     first_gain_grad = jnp.sum(normed_grad * hat_first, 0)
     scaled_first = normed_grad * gains_all[0]
@@ -913,16 +983,24 @@
         scaled_first - hat_first * jnp.mean(scaled_first * hat_first, -1, keepdims=True)
     )
 
-    line_sum = small_sum[:, at + R :]
-    squares = jnp.zeros((1, MODEL_WIDTH), F32).at[0, :3].set(squared_values)
-    early_sum = everywhere(jnp.concatenate([second_gain_grad[None], grad_router, squares]))
-    late_sum = everywhere(first_gain_grad[None])
-    parts = lax.axis_size("dp")
-    width = MODEL_WIDTH // parts
-    shared = lax.dynamic_slice_in_dim(
-        jnp.concatenate([late_sum, early_sum[:3]]), lax.axis_index("dp") * width, width, 1
-    )
-    stats = jnp.sqrt(early_sum[3, :3] / (rows * parts * depth * MODEL_WIDTH))
+    parts, width = lax.axis_size("dp"), MODEL_WIDTH // lax.axis_size("dp")
+    unit = DI // (parts * depth)
+    shared = jnp.concatenate([first_gain_grad[None], second_gain_grad[None], grad_router])
+    shared = shared.reshape(4, parts, width).swapaxes(0, 1).reshape(parts, 1, 4 * width)
+    extra = -(-4 * width // unit)
+    shared = jnp.pad(shared, ((0, 0), (0, 0), (0, extra * unit - 4 * width)))
+    shared = jnp.broadcast_to(shared, (parts, depth, extra * unit)).reshape(DI, extra)
+    whole = unit_blocks(jnp.concatenate(grad_small), True)
+    shared = jnp.pad(shared, ((0, 0), (columns, whole.shape[1] - columns - extra)))
+    *_, small_sum = halved_scatter(whole + shared.astype(BF16))
+    in_last = second_scatter(*in_plane)
+    in_sum = ring_scatter(in_last, "z", True).astype(F32)
+    squared_values = after(squared_values, in_last)
+    small_sum = small_sum.reshape(unit, -1).astype(F32)
+    line_sum = small_sum[:, at + R : columns]
+    shared = small_sum[:, columns : columns + extra].reshape(-1)[: 4 * width].reshape(4, width)
+    square_total = everywhere(jnp.pad(squared_values, (0, LANE - 3))[None])[0, :3]
+    stats = jnp.sqrt(square_total / (rows * parts * depth * MODEL_WIDTH))
     return (
         in_order(layer_out)[None],
         in_order(stream_grad.astype(BF16))[None],
@@ -937,8 +1015,8 @@
         line_sum[:, NS + KC + 2],
         out_sum,
         shared[2:].T,
-        up_sum.swapaxes(1, 2),
-        down_sum,
+        expert_sum[:, 0].swapaxes(1, 2),
+        expert_sum[:, 1],
         stats,
     )
 

time: 791 us -> 669 us (0.85)
  waiting for transfers between devices: 321 us -> 183 us
  blocking collectives: 8.91 us -> 49.6 us
  starting transfers between devices: 87.7 us -> 51.9 us
  local copies, waits for them, and re-layouts: 85.1 us -> 114 us
  other arithmetic: 84.7 us -> 61.6 us
    ppermute x33 -> x17, waiting for transfers between devices: 173 us -> 86.9 us  [moved(): return lax.ppermute(array, 'dp', pairs)]
    ppermute x18 -> x6, waiting for transfers between devices: 130 us -> 49.9 us  [moved(): lax.ppermute(array, 'seq', [(i, (i + by) % size) for i in range(size)])]
    all_gather x0 -> x2, blocking collectives: none -> 40.6 us  [entering(): gathered = lax.all_gather(pairs, 'seq')]
    unnamed x299 -> x386, local copies, waits for them, and re-layouts: 21.3 us -> 47.7 us
    all_gather x2, waiting for transfers between devices: 0.01 us -> 22 us  [the longest x1 22 us: per_device(): experts = lax.all_gather(experts, BOTH, axis=0, tiled=True)]
    ppermute x0 -> x6, waiting for transfers between devices: none -> 18.1 us  [the longest x5 18.1 us: halved_scatter(): got = lax.ppermute(sent, axis, [(i, i ^ bit) for i in range(count)])]
    ppermute x33 -> x17, starting transfers between devices: 27.3 us -> 10.7 us  [moved(): return lax.ppermute(array, 'dp', pairs)]
    ppermute x16 -> x3, starting transfers between devices: 29.7 us -> 13.8 us  [passed_along(): return lax.ppermute(array, axis, pairs)]
  transfers between devices with their start and end apart: 81 -> 42, of which waited for: 38 -> 21; matrix products, arithmetic and copies ran while one was open for 24% -> 26% of each run, Pallas kernels for 13% -> 15%
where the time goes in v3:
time: 669 us; the launch traced here: 662 us
  waiting for transfers between devices  183 us (27%)
  Pallas kernels  123 us (18%)
  local copies, waits for them, and re-layouts  114 us (17%)
  other arithmetic  61.6 us (9%)
  matrix products  56.4 us (8%)
  starting transfers between devices  51.9 us (8%)
  blocking collectives  49.6 us (7%)
  between operations  22 us (3%)
    ppermute x17, waiting for transfers between devices, moved(): return lax.ppermute(array, 'dp', pairs)  86.9 us
    dot_general x27, matrix products, dot(): lax.dot_general(left, right, (contract, ((), ())), precision=precision, p...  56.4 us
    ppermute x6, waiting for transfers between devices, moved(): lax.ppermute(array, 'seq', [(i, (i + by) % size) for i in range(size)])  49.9 us
    pallas_call x2, Pallas kernels, scan_adjoint(): pl.pallas_call(adjoint_kernel, grid=(channels // width,), in_specs=[block...  49.4 us
    unnamed x386, local copies, waits for them, and re-layouts  47.7 us
    all_gather x2, blocking collectives, entering(): gathered = lax.all_gather(pairs, 'seq')  40.6 us
    pallas_call x1, Pallas kernels, expert_pass(): pl.pallas_call(expert_kernel, grid_spec=pltpu.PrefetchScalarGridSpec(num_...  25.7 us
    pallas_call x4, Pallas kernels, segment_ends(): pl.pallas_call(functools.partial(ends_kernel, reverse), grid=(channels //...  25.6 us
  transfers between devices with their start and end apart: 42, of which 21 were waited for; matrix products, arithmetic and copies ran while one was open for 26% of the time, Pallas kernels for 15%

profile of v3, /device:TPU:0, one launch (start us, length us, event | category | flops | bytes accessed | tf_op | source)
XLA Modules:
  0.0 661.8 jit_solution(13758664347404971188)
XLA Ops:
  21.5 9.5 %collective-permute-done.1 = bf16[144,1280]{1,0:T(8,128)(2,1)} collective-permute-done((bf16[144,1280]{1,0:T(8,128)(2,1)}, bf16[144,1280]{1,0:T(8,128)(2,1)}, u32[]{:S(2)}, u32[]{:S(2)}) %collective-permute-start.1) | collective-permute-done | bytes 368672 | tf_op jit(solution)/shard_map/ppermute | solution.py:557
  32.0 15.8 %collective-permute-done.2 = bf16[144,1280]{1,0:T(8,128)(2,1)S(1)} collective-permute-done((bf16[144,1280]{1,0:T(8,128)(2,1)}, bf16[144,1280]{1,0:T(8,128)(2,1)S(1)}, u32[]{:S(2)}, u32[]{:S(2)}) %collective-permute-start.2) | collective-permute-done | bytes 368672 | tf_op jit(solution)/shard_map/ppermute | solution.py:557
  51.7 10.8 %collective-permute-start = (bf16[3,1280]{1,0:T(4,128)(2,1)}, bf16[3,1280]{1,0:T(4,128)(2,1)}, u32[]{:S(2)}, u32[]{:S(2)}) collective-permute-start(bf16[3,1280]{1,0:T(4,128)(2,1)} %pad_maximum_fusion.23), channel_id=1, source_target_pairs={{0,1},{1,2},{2,3},{4,5},{5,6},{6,7},{8,9},{9,10},{10,11},{12,13},{... | collective-permute-start | bytes 23048 | tf_op jit(solution)/shard_map/ppermute | solution.py:501
  64.7 8.9 %all-gather = bf16[8,144,4]{1,2,0:T(4,128)(2,1)S(1)} all-gather(bf16[1,144,4]{1,2,0:T(4,128)(2,1)S(1)} %maximum_bitcast_fusion.10), channel_id=1, replica_groups=mesh['dp'=8,'seq'=4] {'dp'}, dimensions={0}, use_global_device_ids=true | all-gather | bytes 10368 | tf_op jit(solution)/shard_map/all_gather | solution.py:749
  83.4 18.3 %collective-permute-done.6 = bf16[4,144,640]{2,1,0:T(8,128)(2,1)S(1)} collective-permute-done((bf16[4,144,640]{2,1,0:T(8,128)(2,1)}, bf16[4,144,640]{2,1,0:T(8,128)(2,1)S(1)}, u32[]{:S(2)}, u32[]{:S(2)}) %collective-permute-start.6) | collective-permute-done | bytes 737312 | tf_op jit(solution)/shard_map/ppermute | solution.py:564
  110.0 34.6 %collective-permute-done.7 = bf16[2,4,144,640]{3,2,1,0:T(8,128)(2,1)S(1)} collective-permute-done((bf16[2,4,144,640]{3,2,1,0:T(8,128)(2,1)S(1)}, bf16[2,4,144,640]{3,2,1,0:T(8,128)(2,1)S(1)}, u32[]{:S(2)}, u32[]{:S(2)}) %collective-permute-start.7) | collective-permute-done | bytes 1474592 | tf_op jit(solution)/shard_map/ppermute | solution.py:564
  150.1 4.3 convolution_convert_fusion.3
  175.6 4.3 convolution_convert_fusion.2
  183.7 6.3 shard_map.291
  192.1 6.8 %shard_map.290 = (f32[16,8,1152]{2,1,0:T(8,128)S(1)}, f32[16,8,1152]{2,1,0:T(8,128)S(1)}, f32[16,1152]{1,0:T(8,128)S(1)}, f32[16,1152]{1,0:T(8,128)S(1)}) custom-call(f32[256,1152]{1,0:T(8,128)S(1)} %get-tuple-element.260.delta, f32[256,1152]{1,0:T(8,128)S(1)} %get-tuple-element.259.driven, f32[256,128]{1,0:T(8,128)S(1)} %broadcast_in_dim.95.kept, ...), custom_call_target="tpu_custom_call" | custom-call | bytes 5529600 | tf_op jit(solution)/shard_map/pallas_call | solution.py:310
  199.1 24.2 %all_gather.18 = bf16[4,2,16,2304]{3,2,1,0:T(8,128)(2,1)S(1)} all-gather(bf16[1,2,16,2304]{3,2,1,0:T(8,128)(2,1)S(1)} %pad_maximum_fusion.20), channel_id=1, replica_groups=mesh['dp'=8,'seq'=4] {'seq'}, dimensions={0}, use_global_device_ids=true | all-gather | bytes 737280 | tf_op jit(solution)/shard_map/all_gather | solution.py:523
  225.6 8.3 %shard_map.293 = (f32[256,1152]{1,0:T(8,128)S(1)}, bf16[256,1152]{1,0:T(8,128)(2,1)S(1)}) custom-call(f32[256,1152]{1,0:T(8,128)S(1)} %get-tuple-element.258.delta, f32[256,1152]{1,0:T(8,128)S(1)} %get-tuple-element.257.driven, bf16[256,1152]{1,0:T(8,128)(2,1)S(1)} %get-tuple-element.64.inner, bf16[256,1152]{1,0:T(8,128)(2,1)S(1)} %get-tuple-element.334.gate, ...), custom_call_target="tpu_custom_call" | custom-call | bytes 7004160 | tf_op jit(solution)/shard_map/pallas_call | solution.py:329
  235.8 8.3 %shard_map.292 = (f32[256,1152]{1,0:T(8,128)S(1)}, bf16[256,1152]{1,0:T(8,128)(2,1)S(1)}) custom-call(f32[256,1152]{1,0:T(8,128)S(1)} %get-tuple-element.260.delta, f32[256,1152]{1,0:T(8,128)S(1)} %get-tuple-element.259.driven, bf16[256,1152]{1,0:T(8,128)(2,1)S(1)} %get-tuple-element.63.inner, bf16[256,1152]{1,0:T(8,128)(2,1)S(1)} %get-tuple-element.335.gate, ...), custom_call_target="tpu_custom_call" | custom-call | bytes 7004160 | tf_op jit(solution)/shard_map/pallas_call | solution.py:329
  262.8 22.0 %all-gather.6.cloned.1.call-done = bf16[12288,1152]{1,0:T(8,128)(2,1)} async-done(((bf16[384,1152]{1,0:T(8,128)(2,1)}), bf16[12288,1152]{1,0:T(8,128)(2,1)}) %all-gather.6.cloned.1.call-update) | async-done | bytes 28311568 | tf_op jit(solution)/shard_map/all_gather | solution.py:781
  287.0 25.7 %shard_map.294 = (f32[320,1152]{1,0:T(8,128)}, f32[320,1152]{1,0:T(8,128)}, bf16[16,2,2,96,1152]{4,3,2,1,0:T(8,128)(2,1)}) custom-call(s32[1]{0:T(128)} %bitcast.69.at, bf16[320,1152]{1,0:T(8,128)(2,1)S(1)} %copy-done.35, bf16[320,1152]{1,0:T(8,128)(2,1)S(1)} %copy-done.34, bf16[32,4,96,1152]{3,2,1,0:T(8,128)(2,1)} %bitcast.467, ...), custom_call_target="tpu_custom_call" | custom-call | flops 13589544960 | bytes 28311552 | tf_op jit(solution)/shard_map/pallas_call | solution.py:455
  329.1 4.1 fusion.166
  340.8 4.6 fusion.19
  345.4 6.3 shard_map.295
  355.3 6.1 shard_map.296
  371.6 16.4 %all_gather.21 = bf16[4,2,16,2304]{3,2,1,0:T(8,128)(2,1)S(1)} all-gather(bf16[1,2,16,2304]{3,2,1,0:T(8,128)(2,1)S(1)} %pad_maximum_fusion.21), channel_id=1, replica_groups=mesh['dp'=8,'seq'=4] {'seq'}, dimensions={0}, use_global_device_ids=true | all-gather | bytes 737280 | tf_op jit(solution)/shard_map/all_gather | solution.py:523
  413.1 24.7 %shard_map.297 = (bf16[256,1152]{1,0:T(8,128)(2,1)S(1)}, f32[256,1152]{1,0:T(8,128)S(1)}, f32[16,1152]{1,0:T(8,128)S(1)}, f32[1,1152]{1,0:T(1,128)S(1)}, f32[1,1...) custom-call(f32[256,1152]{1,0:T(8,128)S(1)} %get-tuple-element.260.delta, f32[256,1152]{1,0:T(8,128)S(1)} %copy-done.1, ...), custom_call_target="tpu_custom_call" | custom-call | bytes 20643840 | tf_op jit(solution)/shard_map/pallas_call | solution.py:352
  439.0 24.7 %shard_map.298 = (bf16[256,1152]{1,0:T(8,128)(2,1)S(1)}, f32[256,1152]{1,0:T(8,128)S(1)}, f32[16,1152]{1,0:T(8,128)S(1)}, f32[1,1152]{1,0:T(1,128)S(1)}, f32[1,1...) custom-call(f32[256,1152]{1,0:T(8,128)S(1)} %get-tuple-element.258.delta, ...), custom_call_target="tpu_custom_call" | custom-call | bytes 20643840 | tf_op jit(solution)/shard_map/pallas_call | solution.py:352
  499.5 4.8 fusion.144
  504.4 5.5 multiply_reduce_fusion.4
  510.6 5.1 convolution_convert_fusion
  523.5 4.7 pad_maximum_fusion.1
  536.5 5.9 collective-permute-done.19
  553.1 4.8 collective-permute-done.21
  560.9 4.2 collective-permute-done.22
  565.1 14.2 %collective-permute-done.23 = bf16[2,4,144,640]{3,2,1,0:T(8,128)(2,1)S(1)} collective-permute-done((bf16[2,4,144,640]{3,2,1,0:T(8,128)(2,1)S(1)}, bf16[2,4,144,640]{3,2,1,0:T(8,128)(2,1)S(1)}, u32[]{:S(2)}, u32[]{:S(2)}) %collective-permute-start.23) | collective-permute-done | bytes 1474592 | tf_op jit(solution)/shard_map/ppermute | solution.py:564
  584.7 13.5 %collective-permute-done.24 = bf16[4,144,640]{2,1,0:T(8,128)(2,1)S(1)} collective-permute-done((bf16[4,144,640]{2,1,0:T(8,128)(2,1)S(1)}, bf16[4,144,640]{2,1,0:T(8,128)(2,1)S(1)}, u32[]{:S(2)}, u32[]{:S(2)}) %collective-permute-start.24) | collective-permute-done | bytes 737312 | tf_op jit(solution)/shard_map/ppermute | solution.py:564
  631.1 20.6 %collective-permute-done.28 = bf16[144,1152]{1,0:T(8,128)(2,1)S(1)} collective-permute-done((bf16[144,1152]{1,0:T(8,128)(2,1)S(1)}, bf16[144,1152]{1,0:T(8,128)(2,1)S(1)}, u32[]{:S(2)}, u32[]{:S(2)}) %collective-permute-start.28) | collective-permute-done | bytes 331808 | tf_op jit(solution)/shard_map/ppermute | solution.py:557
  (730 shorter events, 261.0 us)
Async XLA Ops:
  7.2 238.8 %all-gather.4.cloned.1.call-start = ((), (), s32[]{:S(2)}) async-start(), calls=%async_computation.3 | async-start | bytes 5474304 | tf_op jit(solution)/shard_map/all_gather | solution.py:778
  7.9 276.8 %all-gather.6.cloned.1.call-start = ((), (), s32[]{:S(2)}) async-start(), calls=%async_computation.4 | async-start | bytes 29196288 | tf_op jit(solution)/shard_map/all_gather | solution.py:781
  14.5 16.5 %collective-permute-start.1 = (bf16[144,1280]{1,0:T(8,128)(2,1)}, bf16[144,1280]{1,0:T(8,128)(2,1)}, u32[]{:S(2)}, u32[]{:S(2)}) collective-permute-start(bf16[144,1280]{1,0:T(8,128)(2,1)} %get-tuple-element.213), channel_id=1, source_target_pairs={{0,1},{1,2},{2,3},{3,0},{4,5},{5,6},{6,7},{7,4},{8,9},{9,10},{10,1... | collective-permute-start | bytes 1105928 | tf_op jit(solution)/shard_map/ppermute | solution.py:557
  17.5 30.3 %collective-permute-start.2 = (bf16[144,1280]{1,0:T(8,128)(2,1)}, bf16[144,1280]{1,0:T(8,128)(2,1)S(1)}, u32[]{:S(2)}, u32[]{:S(2)}) collective-permute-start(bf16[144,1280]{1,0:T(8,128)(2,1)} %get-tuple-element.213), channel_id=1, source_target_pairs={{0,2},{1,3},{2,0},{3,1},{4,6},{5,7},{6,4},{7,5},{8,10},{9,11},{10,... | collective-permute-start | bytes 1105928 | tf_op jit(solution)/shard_map/ppermute | solution.py:557
  20.1 27.8 %collective-permute-start.3 = (bf16[144,1280]{1,0:T(8,128)(2,1)}, bf16[144,1280]{1,0:T(8,128)(2,1)S(1)}, u32[]{:S(2)}, u32[]{:S(2)}) collective-permute-start(bf16[144,1280]{1,0:T(8,128)(2,1)} %get-tuple-element.213), channel_id=1, source_target_pairs={{0,3},{1,0},{2,1},{3,2},{4,7},{5,4},{6,5},{7,6},{8,11},{9,8},{10,9... | collective-permute-start | bytes 1105928 | tf_op jit(solution)/shard_map/ppermute | solution.py:557
  50.8 472.6 %reduce-scatter.10.cloned.1.call-start = ((), (), s32[]{:S(2)}) async-start(), calls=%async_computation.7 | async-start | bytes 4423680
  51.7 28.5 %collective-permute-start = (bf16[3,1280]{1,0:T(4,128)(2,1)}, bf16[3,1280]{1,0:T(4,128)(2,1)}, u32[]{:S(2)}, u32[]{:S(2)}) collective-permute-start(bf16[3,1280]{1,0:T(4,128)(2,1)} %pad_maximum_fusion.23), channel_id=1, source_target_pairs={{0,1},{1,2},{2,3},{4,5},{5,6},{6,7},{8,9},{9,10},{10,11},{12,13},{... | collective-permute-start | bytes 23048 | tf_op jit(solution)/shard_map/ppermute | solution.py:501
  78.7 23.0 %collective-permute-start.6 = (bf16[4,144,640]{2,1,0:T(8,128)(2,1)}, bf16[4,144,640]{2,1,0:T(8,128)(2,1)S(1)}, u32[]{:S(2)}, u32[]{:S(2)}) collective-permute-start(bf16[4,144,640]{2,1,0:T(8,128)(2,1)} %get-tuple-element.238), channel_id=1, source_target_pairs={{0,16},{4,20},{8,24},{12,28},{16,0},{20,4},{24,8},{28,12},{1,17},{... | collective-permute-start | bytes 2211848 | tf_op jit(solution)/shard_map/ppermute | solution.py:564
  80.8 24.6 %collective-permute-start.4 = (bf16[4,144,640]{2,1,0:T(8,128)(2,1)}, bf16[4,144,640]{2,1,0:T(8,128)(2,1)}, u32[]{:S(2)}, u32[]{:S(2)}) collective-permute-start(bf16[4,144,640]{2,1,0:T(8,128)(2,1)} %get-tuple-element.239), channel_id=1, source_target_pairs={{0,8},{4,12},{8,0},{12,4},{16,24},{20,28},{24,16},{28,20},{1,9},{5... | collective-permute-start | bytes 2211848 | tf_op jit(solution)/shard_map/ppermute | solution.py:564
  103.9 40.6 %collective-permute-start.7 = (bf16[2,4,144,640]{3,2,1,0:T(8,128)(2,1)S(1)}, bf16[2,4,144,640]{3,2,1,0:T(8,128)(2,1)S(1)}, u32[]{:S(2)}, u32[]{:S(2)}) collective-permute-start(bf16[2,4,144,640]{3,2,1,0:T(8,128)(2,1)S(1)} %get-tuple-element.241), channel_id=1, source_target_pairs={{0,8},{4,12},{8,0},{12,4},{16,24},{20,28},{24,16},{28,20},{1,9},{5... | collective-permute-start | bytes 4423688 | tf_op jit(solution)/shard_map/ppermute | solution.py:564
  106.8 40.2 %collective-permute-start.5 = (bf16[2,4,144,640]{3,2,1,0:T(8,128)(2,1)S(1)}, bf16[2,4,144,640]{3,2,1,0:T(8,128)(2,1)S(1)}, u32[]{:S(2)}, u32[]{:S(2)}) collective-permute-start(bf16[2,4,144,640]{3,2,1,0:T(8,128)(2,1)S(1)} %get-tuple-element.235), channel_id=1, source_target_pairs={{0,16},{4,20},{8,24},{12,28},{16,0},{20,4},{24,8},{28,12},{1,17},{... | collective-permute-start | bytes 4423688 | tf_op jit(solution)/shard_map/ppermute | solution.py:564
  145.2 10.4 %collective-permute-start.8 = (bf16[2,2,4,144,128]{4,3,2,1,0:T(8,128)(2,1)S(1)}, bf16[2,2,4,144,128]{4,3,2,1,0:T(8,128)(2,1)S(1)}, u32[]{:S(2)}, u32[]{:S(2)}) collective-permute-start(bf16[2,2,4,144,128]{4,3,2,1,0:T(8,128)(2,1)S(1)} %slice.688), channel_id=1, source_target_pairs={{0,4},{4,0},{8,12},{12,8},{16,20},{20,16},{24,28},{28,24},{1,5},{5... | collective-permute-start | bytes 1769480 | tf_op jit(solution)/shard_map/ppermute | solution.py:564
  150.1 25.5 %collective-permute-start.9 = (bf16[2304,1152]{1,0:T(8,128)(2,1)}, bf16[2304,1152]{1,0:T(8,128)(2,1)}, u32[]{:S(2)}, u32[]{:S(2)}) collective-permute-start(bf16[2304,1152]{1,0:T(8,128)(2,1)} %bitcast.29), channel_id=1, source_target_pairs={{0,4},{4,0},{8,12},{12,8},{16,20},{20,16},{24,28},{28,24},{1,5},{5... | collective-permute-start | bytes 15925256 | tf_op jit(solution)/shard_map/ppermute | solution.py:564
  314.8 6.2 collective-permute-start.12
  336.0 187.5 %reduce-scatter.6.cloned.1.call-start = ((), (), s32[]{:S(2)}) async-start(), calls=%async_computation.5 | async-start | bytes 17694720 | tf_op jit(solution)/shard_map/reduce_scatter | solution.py:878
  336.6 287.7 %reduce-scatter.8.cloned.1.call-start = ((), (), s32[]{:S(2)}) async-start(), calls=%async_computation.6 | async-start | bytes 5529600 | tf_op jit(solution)/shard_map/reduce_scatter | solution.py:914
  472.1 22.8 %collective-permute-start.16 = (f32[3,1152]{1,0:T(4,128)}, f32[3,1152]{1,0:T(4,128)}, u32[]{:S(2)}, u32[]{:S(2)}) collective-permute-start(f32[3,1152]{1,0:T(4,128)} %bitcast.463), channel_id=1, source_target_pairs={{1,0},{2,1},{3,2},{5,4},{6,5},{7,6},{9,8},{10,9},{11,10},{13,12},{... | collective-permute-start | bytes 41480 | tf_op jit(solution)/shard_map/ppermute | solution.py:501
  476.3 21.5 %collective-permute-start.15 = (f32[3,1152]{1,0:T(4,128)}, f32[3,1152]{1,0:T(4,128)}, u32[]{:S(2)}, u32[]{:S(2)}) collective-permute-start(f32[3,1152]{1,0:T(4,128)} %bitcast.464), channel_id=1, source_target_pairs={{1,0},{2,1},{3,2},{5,4},{6,5},{7,6},{9,8},{10,9},{11,10},{13,12},{... | collective-permute-start | bytes 41480 | tf_op jit(solution)/shard_map/ppermute | solution.py:501
  497.7 12.8 %collective-permute-start.17 = (bf16[256,2304]{1,0:T(8,128)(2,1)}, bf16[256,2304]{1,0:T(8,128)(2,1)}, u32[]{:S(2)}, u32[]{:S(2)}) collective-permute-start(bf16[256,2304]{1,0:T(8,128)(2,1)} %pad_maximum_fusion.9), channel_id=1, source_target_pairs={{0,4},{4,0},{8,12},{12,8},{16,20},{20,16},{24,28},{28,24},{1,5},{5... | collective-permute-start | bytes 3538952 | tf_op jit(solution)/shard_map/ppermute | solution.py:564
  533.3 9.1 %collective-permute-start.19 = (bf16[2,4,72,256]{3,2,1,0:T(8,128)(2,1)S(1)}, bf16[2,4,72,256]{3,2,1,0:T(8,128)(2,1)S(1)}, u32[]{:S(2)}, u32[]{:S(2)}) collective-permute-start(bf16[2,4,72,256]{3,2,1,0:T(8,128)(2,1)S(1)} %fusion.82), channel_id=1, source_target_pairs={{0,8},{4,12},{8,0},{12,4},{16,24},{20,28},{24,16},{28,20},{1,9},{5... | collective-permute-start | bytes 884744 | tf_op jit(solution)/shard_map/ppermute | solution.py:681
  545.6 33.7 %collective-permute-start.23 = (bf16[2,4,144,640]{3,2,1,0:T(8,128)(2,1)S(1)}, bf16[2,4,144,640]{3,2,1,0:T(8,128)(2,1)S(1)}, u32[]{:S(2)}, u32[]{:S(2)}) collective-permute-start(bf16[2,4,144,640]{3,2,1,0:T(8,128)(2,1)S(1)} %slice_bitcast_fusion), channel_id=1, source_target_pairs={{0,16},{4,20},{8,24},{12,28},{16,0},{20,4},{24,8},{28,12},{1,17},{... | collective-permute-start | bytes 4423688 | tf_op jit(solution)/shard_map/ppermute | solution.py:564
  548.4 9.6 %collective-permute-start.21 = (bf16[1,2,72,256]{3,2,1,0:T(8,128)(2,1)S(1)}, bf16[1,2,72,256]{3,2,1,0:T(8,128)(2,1)S(1)}, u32[]{:S(2)}, u32[]{:S(2)}) collective-permute-start(bf16[1,2,72,256]{3,2,1,0:T(8,128)(2,1)S(1)} %fusion.117), channel_id=1, source_target_pairs={{0,1},{1,0},{2,3},{3,2},{4,5},{5,4},{6,7},{7,6},{8,9},{9,8},{10,11... | collective-permute-start | bytes 221192 | tf_op jit(solution)/shard_map/ppermute | solution.py:681
  551.6 31.0 %collective-permute-start.25 = (bf16[2,4,144,512]{3,2,1,0:T(8,128)(2,1)S(1)}, bf16[2,4,144,512]{3,2,1,0:T(8,128)(2,1)S(1)}, u32[]{:S(2)}, u32[]{:S(2)}) collective-permute-start(bf16[2,4,144,512]{3,2,1,0:T(8,128)(2,1)S(1)} %slice_bitcast_fusion.2), channel_id=1, source_target_pairs={{0,8},{4,12},{8,0},{12,4},{16,24},{20,28},{24,16},{28,20},{1,9},{5... | collective-permute-start | bytes 3538952 | tf_op jit(solution)/shard_map/ppermute | solution.py:564
  558.0 7.1 %collective-permute-start.22 = (bf16[1,1,72,256]{3,2,1,0:T(8,128)(2,1)S(1)}, bf16[1,1,72,256]{3,2,1,0:T(8,128)(2,1)S(1)}, u32[]{:S(2)}, u32[]{:S(2)}) collective-permute-start(bf16[1,1,72,256]{3,2,1,0:T(8,128)(2,1)S(1)} %select_bitcast_fusion.12), channel_id=1, source_target_pairs={{0,2},{1,3},{2,0},{3,1},{4,6},{5,7},{6,4},{7,5},{8,10},{9,11},{10,... | collective-permute-start | bytes 110600 | tf_op jit(solution)/shard_map/ppermute | solution.py:681
  581.2 17.1 %collective-permute-start.24 = (bf16[4,144,640]{2,1,0:T(8,128)(2,1)S(1)}, bf16[4,144,640]{2,1,0:T(8,128)(2,1)S(1)}, u32[]{:S(2)}, u32[]{:S(2)}) collective-permute-start(bf16[4,144,640]{2,1,0:T(8,128)(2,1)S(1)} %slice_bitcast_fusion.6), channel_id=1, source_target_pairs={{0,8},{4,12},{8,0},{12,4},{16,24},{20,28},{24,16},{28,20},{1,9},{5... | collective-permute-start | bytes 2211848 | tf_op jit(solution)/shard_map/ppermute | solution.py:564
  583.1 33.7 %collective-permute-start.26 = (bf16[4,144,512]{2,1,0:T(8,128)(2,1)S(1)}, bf16[4,144,512]{2,1,0:T(8,128)(2,1)S(1)}, u32[]{:S(2)}, u32[]{:S(2)}) collective-permute-start(bf16[4,144,512]{2,1,0:T(8,128)(2,1)S(1)} %slice_bitcast_fusion.8), channel_id=1, source_target_pairs={{0,16},{4,20},{8,24},{12,28},{16,0},{20,4},{24,8},{28,12},{1,17},{... | collective-permute-start | bytes 1769480 | tf_op jit(solution)/shard_map/ppermute | solution.py:564
  607.0 6.5 collective-permute-start.34
  621.7 9.5 %collective-permute-start.27 = (bf16[144,1152]{1,0:T(8,128)(2,1)S(1)}, bf16[144,1152]{1,0:T(8,128)(2,1)S(1)}, u32[]{:S(2)}, u32[]{:S(2)}) collective-permute-start(bf16[144,1152]{1,0:T(8,128)(2,1)S(1)} %get-tuple-element.242), channel_id=1, source_target_pairs={{0,3},{1,0},{2,1},{3,2},{4,7},{5,4},{6,5},{7,6},{8,11},{9,8},{10,9... | collective-permute-start | bytes 995336 | tf_op jit(solution)/shard_map/ppermute | solution.py:557
  622.9 28.9 %collective-permute-start.28 = (bf16[144,1152]{1,0:T(8,128)(2,1)S(1)}, bf16[144,1152]{1,0:T(8,128)(2,1)S(1)}, u32[]{:S(2)}, u32[]{:S(2)}) collective-permute-start(bf16[144,1152]{1,0:T(8,128)(2,1)S(1)} %get-tuple-element.243), channel_id=1, source_target_pairs={{0,2},{1,3},{2,0},{3,1},{4,6},{5,7},{6,4},{7,5},{8,10},{9,11},{10,... | collective-permute-start | bytes 995336 | tf_op jit(solution)/shard_map/ppermute | solution.py:557
  623.2 28.5 %collective-permute-start.29 = (bf16[144,1152]{1,0:T(8,128)(2,1)S(1)}, bf16[144,1152]{1,0:T(8,128)(2,1)S(1)}, u32[]{:S(2)}, u32[]{:S(2)}) collective-permute-start(bf16[144,1152]{1,0:T(8,128)(2,1)S(1)} %get-tuple-element.244), channel_id=1, source_target_pairs={{0,1},{1,2},{2,3},{3,0},{4,5},{5,6},{6,7},{7,4},{8,9},{9,10},{10,1... | collective-permute-start | bytes 995336 | tf_op jit(solution)/shard_map/ppermute | solution.py:557
  625.5 28.0 %collective-permute-start.31 = (bf16[2,96,1152]{2,1,0:T(8,128)(2,1)S(1)}, bf16[2,96,1152]{2,1,0:T(8,128)(2,1)S(1)}, u32[]{:S(2)}, u32[]{:S(2)}) collective-permute-start(bf16[2,96,1152]{2,1,0:T(8,128)(2,1)S(1)} %bitcast.518), channel_id=1, source_target_pairs={{0,4},{4,0},{8,12},{12,8},{16,20},{20,16},{24,28},{28,24},{1,5},{5... | collective-permute-start | bytes 1327112 | tf_op jit(solution)/shard_map/ppermute | solution.py:564
  626.5 26.2 %collective-permute-start.30 = (bf16[72,1152]{1,0:T(8,128)(2,1)S(1)}, bf16[72,1152]{1,0:T(8,128)(2,1)S(1)}, u32[]{:S(2)}, u32[]{:S(2)}) collective-permute-start(bf16[72,1152]{1,0:T(8,128)(2,1)S(1)} %slice_bitcast_fusion.12), channel_id=1, source_target_pairs={{0,0},{16,1},{1,2},{17,3},{2,4},{18,5},{3,6},{19,7},{4,8},{20,9},{... | collective-permute-start | bytes 497672 | tf_op jit(solution)/shard_map/ppermute | solution.py:918
  (199 other events, 1802.6 us)
Sparse Core Ops, SparseCore 0:
  10.9 90.1 all-gather.3
  104.4 180.2 all-gather.5
  336.1 46.3 reduce-scatter.9
  385.5 133.6 reduce-scatter.5
  528.4 84.8 reduce-scatter.7

commit v4 on v3

--- a/solution.py
+++ b/solution.py
@@ -276,9 +276,9 @@
     hidden_grad = (active_grad * (below + hidden * density)).astype(jnp.bfloat16)
     returned[...] += product(active, downs, ((1,), (0,)))
     buffer_grad[...] += product(hidden_grad, ups, ((1,), (0,)))
-    pieces = weight_grads.shape[0], weight_grads.shape[3], weight_grads.shape[4]
+    pieces = weight_grads.shape[0], weight_grads.shape[2], weight_grads.shape[3]
     for k, (left, right) in enumerate(((hidden_grad, values), (active, cot))):
-        weight_grads[:, 0, k] = product(left, right, ((0,), (0,))).astype(jnp.bfloat16).reshape(pieces)
+        weight_grads[:, k] = product(left, right, ((0,), (0,))).astype(jnp.bfloat16).reshape(pieces)
 
 
 def column_specs(rows, width):
@@ -462,13 +462,12 @@
                 whole,
                 whole,
                 pl.BlockSpec(
-                    (tile, 1, 2, strip, width),
-                    lambda j, at: (lax.div(j, 2), lax.rem(j, 2), 0, 0, 0),
+                    (tile, 2, strip, width), lambda j, at: (lax.div(j, 2), lax.rem(j, 2), 0, 0)
                 ),
             ],
         ),
         out_shape=[jax.ShapeDtypeStruct((slots, width), jnp.float32)] * 2
-        + [jax.ShapeDtypeStruct((steps // 2 * tile, 2, 2, strip, width), jnp.bfloat16)],
+        + [jax.ShapeDtypeStruct((steps // 2 * tile, 5, strip, width), jnp.bfloat16)],
         compiler_params=params(52),
         cost_estimate=pl.CostEstimate(
             flops=12 * slots * width * devices * part,
@@ -477,8 +476,8 @@
         ),
     )(core.reshape(1).astype(jnp.int32), buffer, grads, weights, weights)
     if not direct:
-        parts = weight_grads.reshape(steps // 2, 2, 2, depth, part, width)
-        weight_grads = parts.transpose(0, 3, 1, 2, 4, 5).reshape(-1, 2, 2, part, width)
+        parts = weight_grads.reshape(steps // 2, 5, depth, part, width)
+        weight_grads = parts.swapaxes(1, 2).reshape(-1, 5, part, width)
     return returned, buffer_grad, weight_grads
 
 
@@ -667,22 +666,6 @@
     return pairs
 
 
-def halved_scatter(whole):
-    size, depth = lax.axis_size("dp"), lax.axis_size("seq")
-    rest = whole.reshape((size, depth, -1) + whole.shape[1:])
-    for axis, at in (("dp", 0), ("seq", 1)):
-        count, mine = lax.axis_size(axis), lax.axis_index(axis)
-        bits = [1 << k for k in range(count.bit_length() - 1)]
-        for bit in bits:
-            parts = rest.reshape(rest.shape[:at] + (rest.shape[at] // 2, 2) + rest.shape[at + 1 :])
-            low, high = (lax.index_in_dim(parts, k, at + 1, False) for k in range(2))
-            own = (mine & bit) == 0
-            sent = jnp.where(own, high, low)
-            got = lax.ppermute(sent, axis, [(i, i ^ bit) for i in range(count)])
-            rest = added(jnp.where(own, low, high), got)
-            yield rest
-
-
 def units_in_order(near, far):
     side, depth = sides(), lax.axis_size("seq")
     cores = []
@@ -695,13 +678,22 @@
     return whole.reshape(-1, whole.shape[-1])
 
 
+def units_from_order(whole):
+    side, depth = sides(), lax.axis_size("seq")
+    parts = whole.reshape(side, side, 2, depth, -1, 2, LANE)
+    parts = jnp.concatenate([parts[..., 0, :], parts[..., 1, :]], 4)
+    near, far = by_place([parts[:, :, k] for k in range(2)], "core")
+    near = added(near, moved(far, "core"))
+    rows = [jnp.stack(by_place([near[j, k] for k in range(side)], "x")) for j in range(side)]
+    return jnp.stack(by_place(rows, "y"))
+
+
 def plane_rows(plane):
     side, depth = sides(), lax.axis_size("seq")
     columns = plane.shape[1]
     parts = plane.reshape(side // 2, side, depth, 2, -1, columns)
     parts = jnp.stack(by_place([parts[:, k] for k in range(side)], "x"))
-    parts = parts.transpose(3, 1, 0, 2, 4, 5).reshape(side * side, depth, -1, columns)
-    return jnp.pad(parts, ((0, 0), (0, 0), (0, -parts.shape[2] % 32), (0, 0)))
+    return parts.transpose(3, 1, 0, 2, 4, 5).reshape(side * side * depth, -1, columns)
 
 
 def everywhere(array):
@@ -874,10 +866,6 @@
     returned, buffer_grad, expert_grads = expert_pass(core, buffer, grad_slots, experts, depth)
     returned = from_slots(returned)
     buffer_grad = from_slots(buffer_grad)
-    groups = [list(range(c, lax.axis_size("dp"), 2)) for c in range(2)]
-    expert_sum = lax.psum_scatter(
-        expert_grads, "dp", scatter_dimension=0, tiled=True, axis_index_groups=groups
-    )
     branch = chosen * returned
     layer_out = (resid + branch).astype(BF16)
     squared_values = jnp.stack(
@@ -905,24 +893,23 @@
     ]
     post = [e[:2] for e in ends]
     adjoint_in = entering([e[2] for e in ends], [e[3] for e in ends], True)
-    out_sum = lax.psum_scatter(
-        plane_rows(grad_out.astype(BF16)), "dp", scatter_dimension=0, tiled=True,
-        axis_index_groups=groups,
-    )[0]
-    expert_sum = expert_sum.reshape(depth, -1, MODEL_WIDTH)
-    own_rows = expert_sum.shape[1]
+    groups = [list(range(c, lax.axis_size("dp"), 2)) for c in range(2)]
+    out_rows = plane_rows(grad_out.astype(BF16))
+    unit = out_rows.shape[1]
+    out_rows = jnp.pad(out_rows, ((0, 0), (0, expert_grads.shape[2] - unit), (0, 0)))
+    both_sum = lax.dynamic_update_slice(expert_grads, out_rows[:, None], (0, 4, 0, 0))
     both_sum = lax.psum_scatter(
-        jnp.concatenate([expert_sum, out_sum], 1), "seq", scatter_dimension=0, tiled=True
-    )[0]
-    out_sum = both_sum[own_rows : own_rows + out_proj.shape[0]]
-    out_sum = lax.ppermute(out_sum, BOTH, [(b, a) for a, b in unit_pairs()]).astype(F32)
-    expert_sum = both_sum[:own_rows].reshape(2, 2, -1, MODEL_WIDTH)
+        both_sum, "dp", scatter_dimension=0, tiled=True, axis_index_groups=groups
+    )
+    both_sum = lax.psum_scatter(both_sum, "seq", scatter_dimension=0, tiled=True)[0]
+    out_sum = lax.ppermute(both_sum[4, :unit], BOTH, [(b, a) for a, b in unit_pairs()])
+    out_sum = out_sum.astype(F32)
+    expert_sum = both_sum[:4].reshape(2, 2, -1, MODEL_WIDTH)
     mine_sum = jnp.where(core == 0, expert_sum[0], expert_sum[1])
     other_sum = moved(jnp.where(core == 0, expert_sum[1], expert_sum[0]), "core")
     expert_sum = jnp.stack(
         [jnp.where(core == e, mine_sum, other_sum) for e in range(EXPERT_COUNT)]
     ).astype(F32)
-    rate = [after(r, grad_out) for r in rate]
     made = [
         scan_adjoint(
             delta[h], driven[h], inner[h], scan_grad[h], step_pre[h], kept, in_select, out_select,
@@ -972,10 +959,27 @@
         jnp.concatenate([normed, crossed[rows:]]),
         ((0,), (0,)),
     ).astype(BF16)
+    parts, width = lax.axis_size("dp"), MODEL_WIDTH // lax.axis_size("dp")
+    unit = DI // (parts * depth)
+    shared = jnp.concatenate([second_gain_grad[None], grad_router]).astype(BF16)
+    shared = shared.reshape(3, parts, width).swapaxes(0, 1).reshape(parts, 1, 3 * width)
+    extra = -(-3 * width // unit)
+    shared = jnp.pad(shared, ((0, 0), (0, 0), (0, extra * unit - 3 * width)))
+    shared = jnp.broadcast_to(shared, (parts, depth, extra * unit)).reshape(DI, extra)
+    whole = unit_blocks(jnp.concatenate(grad_small), True)
+    shared = jnp.pad(shared, ((0, 0), (columns, whole.shape[1] - columns - extra)))
+    small_near = units_from_order(whole + shared)
     in_plane = grad_in.reshape(side, side, depth, -1, MODEL_WIDTH)
-    cut = cut_of(MODEL_WIDTH)
-    in_plane = first_scatter(in_plane[..., :cut], in_plane[..., cut:].swapaxes(0, 1))
-    grad_small = [after(g, grad_in) for g in grad_small]
+    cut = cut_of(MODEL_WIDTH + LANE)
+    right = jnp.concatenate([in_plane[..., cut:], small_near], -1)
+    in_plane = first_scatter(in_plane[..., :cut], right.swapaxes(0, 1))
+    in_last = second_scatter(*in_plane)
+    in_total = ring_scatter(in_last, "z", True).astype(F32)
+    in_sum = in_total[:, :MODEL_WIDTH]
+    small_sum = jnp.concatenate(jnp.split(in_total[:, MODEL_WIDTH:], 2), 1)
+    line_sum = small_sum[:, at + R : columns]
+    shared = small_sum[:, columns : columns + extra].reshape(-1)[: 3 * width].reshape(3, width)
+    proj_grad = [after(p, grad_in) for p in proj_grad]
     normed_grad = sum(dot(proj_grad[h], in_full[h], ((1,), (0,))) for h in both)
     first_gain_grad = jnp.sum(normed_grad * hat_first, 0)
     scaled_first = normed_grad * gains_all[0]
@@ -983,28 +987,14 @@
         scaled_first - hat_first * jnp.mean(scaled_first * hat_first, -1, keepdims=True)
     )
 
-    parts, width = lax.axis_size("dp"), MODEL_WIDTH // lax.axis_size("dp")
-    unit = DI // (parts * depth)
-    shared = jnp.concatenate([first_gain_grad[None], second_gain_grad[None], grad_router])
-    shared = shared.reshape(4, parts, width).swapaxes(0, 1).reshape(parts, 1, 4 * width)
-    extra = -(-4 * width // unit)
-    shared = jnp.pad(shared, ((0, 0), (0, 0), (0, extra * unit - 4 * width)))
-    shared = jnp.broadcast_to(shared, (parts, depth, extra * unit)).reshape(DI, extra)
-    whole = unit_blocks(jnp.concatenate(grad_small), True)
-    shared = jnp.pad(shared, ((0, 0), (columns, whole.shape[1] - columns - extra)))
-    *_, small_sum = halved_scatter(whole + shared.astype(BF16))
-    in_last = second_scatter(*in_plane)
-    in_sum = ring_scatter(in_last, "z", True).astype(F32)
-    squared_values = after(squared_values, in_last)
-    small_sum = small_sum.reshape(unit, -1).astype(F32)
-    line_sum = small_sum[:, at + R : columns]
-    shared = small_sum[:, columns : columns + extra].reshape(-1)[: 4 * width].reshape(4, width)
-    square_total = everywhere(jnp.pad(squared_values, (0, LANE - 3))[None])[0, :3]
-    stats = jnp.sqrt(square_total / (rows * parts * depth * MODEL_WIDTH))
+    last = jnp.stack([first_gain_grad, jnp.pad(squared_values, (0, MODEL_WIDTH - 3))])
+    last = everywhere(after(last, in_last))
+    first_part = lax.dynamic_slice_in_dim(last[:1], lax.axis_index("dp") * width, width, 1)
+    stats = jnp.sqrt(last[1, :3] / (rows * parts * depth * MODEL_WIDTH))
     return (
         in_order(layer_out)[None],
         in_order(stream_grad.astype(BF16))[None],
-        shared[:2],
+        jnp.concatenate([first_part, shared[:1]]),
         in_sum.T,
         line_sum[:, NS : NS + KC].T,
         line_sum[:, NS + KC],
@@ -1014,7 +1004,7 @@
         line_sum[:, :NS],
         line_sum[:, NS + KC + 2],
         out_sum,
-        shared[2:].T,
+        shared[1:].T,
         expert_sum[:, 0].swapaxes(1, 2),
         expert_sum[:, 1],
         stats,

time: 669 us -> 640 us (0.957)
  waiting for transfers between devices: 183 us -> 198 us
  other arithmetic: 61.6 us -> 48.1 us
  local copies, waits for them, and re-layouts: 114 us -> 101 us
  starting transfers between devices: 51.9 us -> 40 us
  matrix products: 56.4 us -> 48.9 us
    ppermute x5, waiting for transfers between devices: 4.42 us -> 31.1 us  [everywhere(): lax.ppermute(array, axis, [(i, i ^ bit) for i in range(size)])]
    ppermute x6, waiting for transfers between devices: 49.9 us -> 25.4 us  [moved(): lax.ppermute(array, 'seq', [(i, (i + by) % size) for i in range(size)])]
    ppermute x17 -> x18, waiting for transfers between devices: 86.9 us -> 109 us  [moved(): return lax.ppermute(array, 'dp', pairs)]
    ppermute x6 -> x1, waiting for transfers between devices: 18.1 us -> 0.01 us  [per_device(): lax.ppermute(both_sum[4, :unit], BOTH, [(b, a) for a, b in unit_pairs()])]
    unnamed x386 -> x344, local copies, waits for them, and re-layouts: 47.7 us -> 36.1 us
    ppermute x6 -> x1, starting transfers between devices: 8.51 us -> 0.67 us  [per_device(): lax.ppermute(both_sum[4, :unit], BOTH, [(b, a) for a, b in unit_pairs()])]
    reduce_scatter x2, waiting for transfers between devices: 0.02 us -> 7.85 us  [the longest x1 7.84 us: per_device(): lax.psum_scatter(both_sum, 'dp', scatter_dimension=0, tiled=True, axis_in...]
    dot_general x27, matrix products: 56.4 us -> 48.9 us  [dot(): lax.dot_general(left, right, (contract, ((), ())), precision=precision, p...]
  transfers between devices with their start and end apart: 42 -> 37, of which waited for: 21 -> 17; matrix products, arithmetic and copies ran while one was open for 26% -> 24% of each run, Pallas kernels for 15% -> 16%
where the time goes in v4:
time: 640 us; the launch traced here: 630 us
  waiting for transfers between devices  198 us (31%)
  Pallas kernels  124 us (19%)
  local copies, waits for them, and re-layouts  101 us (16%)
  blocking collectives  49.8 us (8%)
  matrix products  48.9 us (8%)
  other arithmetic  48.1 us (8%)
  starting transfers between devices  40 us (6%)
  between operations  20.7 us (3%)
    ppermute x18, waiting for transfers between devices, moved(): return lax.ppermute(array, 'dp', pairs)  109 us
    pallas_call x2, Pallas kernels, scan_adjoint(): pl.pallas_call(adjoint_kernel, grid=(channels // width,), in_specs=[block...  49.8 us
    dot_general x27, matrix products, dot(): lax.dot_general(left, right, (contract, ((), ())), precision=precision, p...  48.9 us
    all_gather x2, blocking collectives, entering(): gathered = lax.all_gather(pairs, 'seq')  40.9 us
    unnamed x344, local copies, waits for them, and re-layouts  36.1 us
    ppermute x5, waiting for transfers between devices, everywhere(): lax.ppermute(array, axis, [(i, i ^ bit) for i in range(size)])  31.1 us
    pallas_call x1, Pallas kernels, expert_pass(): pl.pallas_call(expert_kernel, grid_spec=pltpu.PrefetchScalarGridSpec(num_...  25.7 us
    ppermute x6, waiting for transfers between devices, moved(): lax.ppermute(array, 'seq', [(i, (i + by) % size) for i in range(size)])  25.4 us
  transfers between devices with their start and end apart: 37, of which 17 were waited for; matrix products, arithmetic and copies ran while one was open for 24% of the time, Pallas kernels for 16%

profile of v4, /device:TPU:0, one launch (start us, length us, event | category | flops | bytes accessed | tf_op | source)
XLA Modules:
  0.0 630.2 jit_solution(7294063816032685349)
XLA Ops:
  14.5 3.0 collective-permute-start.1
  21.5 9.5 %collective-permute-done.1 = bf16[144,1280]{1,0:T(8,128)(2,1)} collective-permute-done((bf16[144,1280]{1,0:T(8,128)(2,1)}, bf16[144,1280]{1,0:T(8,128)(2,1)}, u32[]{:S(2)}, u32[]{:S(2)}) %collective-permute-start.1) | collective-permute-done | bytes 368672 | tf_op jit(solution)/shard_map/ppermute | solution.py:556
  32.0 15.8 %collective-permute-done.2 = bf16[144,1280]{1,0:T(8,128)(2,1)S(1)} collective-permute-done((bf16[144,1280]{1,0:T(8,128)(2,1)}, bf16[144,1280]{1,0:T(8,128)(2,1)S(1)}, u32[]{:S(2)}, u32[]{:S(2)}) %collective-permute-start.2) | collective-permute-done | bytes 368672 | tf_op jit(solution)/shard_map/ppermute | solution.py:556
  51.7 10.8 %collective-permute-start = (bf16[3,1280]{1,0:T(4,128)(2,1)}, bf16[3,1280]{1,0:T(4,128)(2,1)}, u32[]{:S(2)}, u32[]{:S(2)}) collective-permute-start(bf16[3,1280]{1,0:T(4,128)(2,1)} %pad_maximum_fusion.26), channel_id=1, source_target_pairs={{0,1},{1,2},{2,3},{4,5},{5,6},{6,7},{8,9},{9,10},{10,11},{12,13},{... | collective-permute-start | bytes 23048 | tf_op jit(solution)/shard_map/ppermute | solution.py:500
  64.7 8.9 %all-gather = bf16[8,144,4]{1,2,0:T(4,128)(2,1)S(1)} all-gather(bf16[1,144,4]{1,2,0:T(4,128)(2,1)S(1)} %maximum_bitcast_fusion.11), channel_id=1, replica_groups=mesh['dp'=8,'seq'=4] {'dp'}, dimensions={0}, use_global_device_ids=true | all-gather | bytes 10368 | tf_op jit(solution)/shard_map/all_gather | solution.py:741
  83.4 18.3 %collective-permute-done.6 = bf16[4,144,640]{2,1,0:T(8,128)(2,1)S(1)} collective-permute-done((bf16[4,144,640]{2,1,0:T(8,128)(2,1)}, bf16[4,144,640]{2,1,0:T(8,128)(2,1)S(1)}, u32[]{:S(2)}, u32[]{:S(2)}) %collective-permute-start.6) | collective-permute-done | bytes 737312 | tf_op jit(solution)/shard_map/ppermute | solution.py:563
  110.0 34.6 %collective-permute-done.7 = bf16[2,4,144,640]{3,2,1,0:T(8,128)(2,1)S(1)} collective-permute-done((bf16[2,4,144,640]{3,2,1,0:T(8,128)(2,1)S(1)}, bf16[2,4,144,640]{3,2,1,0:T(8,128)(2,1)S(1)}, u32[]{:S(2)}, u32[]{:S(2)}) %collective-permute-start.7) | collective-permute-done | bytes 1474592 | tf_op jit(solution)/shard_map/ppermute | solution.py:563
  150.1 4.3 convolution_convert_fusion.4
  175.5 4.3 convolution_convert_fusion.3
  183.6 6.3 %shard_map.291 = (f32[16,8,1152]{2,1,0:T(8,128)S(1)}, f32[16,8,1152]{2,1,0:T(8,128)S(1)}, f32[16,1152]{1,0:T(8,128)S(1)}, f32[16,1152]{1,0:T(8,128)S(1)}) custom-call(f32[256,1152]{1,0:T(8,128)S(1)} %get-tuple-element.280.delta, f32[256,1152]{1,0:T(8,128)S(1)} %get-tuple-element.279.driven, f32[256,128]{1,0:T(8,128)S(1)} %broadcast_in_dim.97.kept, ...), custom_call_target="tpu_custom_call" | custom-call | bytes 5529600 | tf_op jit(solution)/shard_map/pallas_call | solution.py:310
  192.0 6.7 %shard_map.290 = (f32[16,8,1152]{2,1,0:T(8,128)S(1)}, f32[16,8,1152]{2,1,0:T(8,128)S(1)}, f32[16,1152]{1,0:T(8,128)S(1)}, f32[16,1152]{1,0:T(8,128)S(1)}) custom-call(f32[256,1152]{1,0:T(8,128)S(1)} %get-tuple-element.282.delta, f32[256,1152]{1,0:T(8,128)S(1)} %get-tuple-element.281.driven, f32[256,128]{1,0:T(8,128)S(1)} %broadcast_in_dim.97.kept, ...), custom_call_target="tpu_custom_call" | custom-call | bytes 5529600 | tf_op jit(solution)/shard_map/pallas_call | solution.py:310
  198.8 24.2 %all_gather.18 = bf16[4,2,16,2304]{3,2,1,0:T(8,128)(2,1)S(1)} all-gather(bf16[1,2,16,2304]{3,2,1,0:T(8,128)(2,1)S(1)} %pad_maximum_fusion.22), channel_id=1, replica_groups=mesh['dp'=8,'seq'=4] {'seq'}, dimensions={0}, use_global_device_ids=true | all-gather | bytes 737280 | tf_op jit(solution)/shard_map/all_gather | solution.py:522
  225.3 8.3 %shard_map.293 = (f32[256,1152]{1,0:T(8,128)S(1)}, bf16[256,1152]{1,0:T(8,128)(2,1)S(1)}) custom-call(f32[256,1152]{1,0:T(8,128)S(1)} %get-tuple-element.280.delta, f32[256,1152]{1,0:T(8,128)S(1)} %get-tuple-element.279.driven, bf16[256,1152]{1,0:T(8,128)(2,1)S(1)} %get-tuple-element.64.inner, bf16[256,1152]{1,0:T(8,128)(2,1)S(1)} %get-tuple-element.354.gate, ...), custom_call_target="tpu_custom_call" | custom-call | bytes 7004160 | tf_op jit(solution)/shard_map/pallas_call | solution.py:329
  235.6 8.3 %shard_map.292 = (f32[256,1152]{1,0:T(8,128)S(1)}, bf16[256,1152]{1,0:T(8,128)(2,1)S(1)}) custom-call(f32[256,1152]{1,0:T(8,128)S(1)} %get-tuple-element.282.delta, f32[256,1152]{1,0:T(8,128)S(1)} %get-tuple-element.281.driven, bf16[256,1152]{1,0:T(8,128)(2,1)S(1)} %get-tuple-element.63.inner, bf16[256,1152]{1,0:T(8,128)(2,1)S(1)} %get-tuple-element.355.gate, ...), custom_call_target="tpu_custom_call" | custom-call | bytes 7004160 | tf_op jit(solution)/shard_map/pallas_call | solution.py:329
  245.8 3.4 dynamic-slice_bitcast_fusion.1
  262.7 22.1 %all-gather.6.cloned.1.call-done = bf16[12288,1152]{1,0:T(8,128)(2,1)} async-done(((bf16[384,1152]{1,0:T(8,128)(2,1)}), bf16[12288,1152]{1,0:T(8,128)(2,1)}) %all-gather.6.cloned.1.call-update) | async-done | bytes 28311568 | tf_op jit(solution)/shard_map/all_gather | solution.py:773
  287.0 25.7 %shard_map.294 = (f32[320,1152]{1,0:T(8,128)}, f32[320,1152]{1,0:T(8,128)}, bf16[16,5,96,1152]{3,2,1,0:T(8,128)(2,1)}) custom-call(s32[1]{0:T(128)} %bitcast.69.at, bf16[320,1152]{1,0:T(8,128)(2,1)S(1)} %copy-done.28, bf16[320,1152]{1,0:T(8,128)(2,1)S(1)} %copy-done.27, bf16[32,4,96,1152]{3,2,1,0:T(8,128)(2,1)} %bitcast.397, bf16[32,4,96,1152]{3,2,1,0:T(8,128)(2,1)} %bitcast.398), custom_call_target="tpu_custom_call" | custom-call | flops 13589544960 | bytes 28311552 | tf_op jit(solution)/shard_map/pallas_call | solution.py:455
  316.7 3.6 multiply_reduce_fusion.2
  349.3 4.2 fusion.19
  353.6 6.1 shard_map.295
  361.9 6.1 shard_map.296
  368.1 16.7 %all_gather.21 = bf16[4,2,16,2304]{3,2,1,0:T(8,128)(2,1)S(1)} all-gather(bf16[1,2,16,2304]{3,2,1,0:T(8,128)(2,1)S(1)} %pad_maximum_fusion.23), channel_id=1, replica_groups=mesh['dp'=8,'seq'=4] {'seq'}, dimensions={0}, use_global_device_ids=true | all-gather | bytes 737280 | tf_op jit(solution)/shard_map/all_gather | solution.py:522
  386.7 25.1 %shard_map.297 = (bf16[256,1152]{1,0:T(8,128)(2,1)S(1)}, f32[256,1152]{1,0:T(8,128)S(1)}, f32[16,1152]{1,0:T(8,128)S(1)}, f32[1,1152]{1,0:T(1,128)S(1)}, f32[1,1...) custom-call(f32[256,1152]{1,0:T(8,128)S(1)} %get-tuple-element.282.delta, f32[256,1152]{1,0:T(8,128)S(1)} %copy-done.1, ...), custom_call_target="tpu_custom_call" | custom-call | bytes 20643840 | tf_op jit(solution)/shard_map/pallas_call | solution.py:352
  413.0 24.7 %shard_map.298 = (bf16[256,1152]{1,0:T(8,128)(2,1)S(1)}, f32[256,1152]{1,0:T(8,128)S(1)}, f32[16,1152]{1,0:T(8,128)S(1)}, f32[1,1152]{1,0:T(1,128)S(1)}, f32[1,1...) custom-call(f32[256,1152]{1,0:T(8,128)S(1)} %get-tuple-element.280.delta, ...), custom_call_target="tpu_custom_call" | custom-call | bytes 20643840 | tf_op jit(solution)/shard_map/pallas_call | solution.py:352
  486.4 7.8 %reduce-scatter.3.cloned.1.call-done = bf16[4,5,96,1152]{3,2,1,0:T(8,128)(2,1)} async-done(((bf16[16,5,96,1152]{3,2,1,0:T(8,128)(2,1)}), bf16[4,5,96,1152]{3,2,1,0:T(8,128)(2,1)}) %reduce-scatter.3.cloned.1.call-update) | async-done | bytes 4423696 | tf_op jit(solution)/shard_map/reduce_scatter | solution.py:901
  495.9 4.5 convolution_convert_fusion
  506.6 4.2 fusion.49
  510.8 23.7 %collective-permute-done.17 = bf16[2,4,144,640]{3,2,1,0:T(8,128)(2,1)S(1)} collective-permute-done((bf16[2,4,144,640]{3,2,1,0:T(8,128)(2,1)S(1)}, bf16[2,4,144,640]{3,2,1,0:T(8,128)(2,1)S(1)}, u32[]{:S(2)}, u32[]{:S(2)}) %collective-permute-start.17) | collective-permute-done | bytes 1474592 | tf_op jit(solution)/shard_map/ppermute | solution.py:563
  536.5 4.4 multiply_reduce_fusion.4
  541.3 12.9 %collective-permute-done.18 = bf16[4,144,640]{2,1,0:T(8,128)(2,1)S(1)} collective-permute-done((bf16[4,144,640]{2,1,0:T(8,128)(2,1)S(1)}, bf16[4,144,640]{2,1,0:T(8,128)(2,1)S(1)}, u32[]{:S(2)}, u32[]{:S(2)}) %collective-permute-start.18) | collective-permute-done | bytes 737312 | tf_op jit(solution)/shard_map/ppermute | solution.py:563
  562.3 13.1 %collective-permute-done.26 = bf16[4,144,640]{2,1,0:T(8,128)(2,1)S(1)} collective-permute-done((bf16[4,144,640]{2,1,0:T(8,128)(2,1)S(1)}, bf16[4,144,640]{2,1,0:T(8,128)(2,1)S(1)}, u32[]{:S(2)}, u32[]{:S(2)}) %collective-permute-start.26) | collective-permute-done | bytes 737312 | tf_op jit(solution)/shard_map/ppermute | solution.py:563
  584.0 28.0 %collective-permute-done.23 = f32[2,1152]{1,0:T(2,128)S(1)} collective-permute-done((f32[2,1152]{1,0:T(2,128)S(1)}, f32[2,1152]{1,0:T(2,128)S(1)}, u32[]{:S(2)}, u32[]{:S(2)}) %collective-permute-start.23) | collective-permute-done | bytes 9248 | tf_op jit(solution)/shard_map/ppermute | solution.py:704
  (673 shorter events, 209.5 us)
Async XLA Ops:
  7.2 238.6 %all-gather.4.cloned.1.call-start = ((), (), s32[]{:S(2)}) async-start(), calls=%async_computation.2 | async-start | bytes 5474304 | tf_op jit(solution)/shard_map/all_gather | solution.py:770
  7.9 276.8 %all-gather.6.cloned.1.call-start = ((), (), s32[]{:S(2)}) async-start(), calls=%async_computation.3 | async-start | bytes 29196288 | tf_op jit(solution)/shard_map/all_gather | solution.py:773
  14.5 16.5 %collective-permute-start.1 = (bf16[144,1280]{1,0:T(8,128)(2,1)}, bf16[144,1280]{1,0:T(8,128)(2,1)}, u32[]{:S(2)}, u32[]{:S(2)}) collective-permute-start(bf16[144,1280]{1,0:T(8,128)(2,1)} %get-tuple-element.229), channel_id=1, source_target_pairs={{0,1},{1,2},{2,3},{3,0},{4,5},{5,6},{6,7},{7,4},{8,9},{9,10},{10,1... | collective-permute-start | bytes 1105928 | tf_op jit(solution)/shard_map/ppermute | solution.py:556
  17.5 30.3 %collective-permute-start.2 = (bf16[144,1280]{1,0:T(8,128)(2,1)}, bf16[144,1280]{1,0:T(8,128)(2,1)S(1)}, u32[]{:S(2)}, u32[]{:S(2)}) collective-permute-start(bf16[144,1280]{1,0:T(8,128)(2,1)} %get-tuple-element.229), channel_id=1, source_target_pairs={{0,2},{1,3},{2,0},{3,1},{4,6},{5,7},{6,4},{7,5},{8,10},{9,11},{10,... | collective-permute-start | bytes 1105928 | tf_op jit(solution)/shard_map/ppermute | solution.py:556
  20.1 27.8 %collective-permute-start.3 = (bf16[144,1280]{1,0:T(8,128)(2,1)}, bf16[144,1280]{1,0:T(8,128)(2,1)S(1)}, u32[]{:S(2)}, u32[]{:S(2)}) collective-permute-start(bf16[144,1280]{1,0:T(8,128)(2,1)} %get-tuple-element.229), channel_id=1, source_target_pairs={{0,3},{1,0},{2,1},{3,2},{4,7},{5,4},{6,5},{7,6},{8,11},{9,8},{10,9... | collective-permute-start | bytes 1105928 | tf_op jit(solution)/shard_map/ppermute | solution.py:556
  50.8 443.4 %reduce-scatter.3.cloned.1.call-start = ((), (), s32[]{:S(2)}) async-start(), calls=%async_computation.4 | async-start | bytes 22118400 | tf_op jit(solution)/shard_map/reduce_scatter | solution.py:901
  51.7 28.5 %collective-permute-start = (bf16[3,1280]{1,0:T(4,128)(2,1)}, bf16[3,1280]{1,0:T(4,128)(2,1)}, u32[]{:S(2)}, u32[]{:S(2)}) collective-permute-start(bf16[3,1280]{1,0:T(4,128)(2,1)} %pad_maximum_fusion.26), channel_id=1, source_target_pairs={{0,1},{1,2},{2,3},{4,5},{5,6},{6,7},{8,9},{9,10},{10,11},{12,13},{... | collective-permute-start | bytes 23048 | tf_op jit(solution)/shard_map/ppermute | solution.py:500
  78.7 23.0 %collective-permute-start.6 = (bf16[4,144,640]{2,1,0:T(8,128)(2,1)}, bf16[4,144,640]{2,1,0:T(8,128)(2,1)S(1)}, u32[]{:S(2)}, u32[]{:S(2)}) collective-permute-start(bf16[4,144,640]{2,1,0:T(8,128)(2,1)} %get-tuple-element.261), channel_id=1, source_target_pairs={{0,16},{4,20},{8,24},{12,28},{16,0},{20,4},{24,8},{28,12},{1,17},{... | collective-permute-start | bytes 2211848 | tf_op jit(solution)/shard_map/ppermute | solution.py:563
  80.9 24.6 %collective-permute-start.4 = (bf16[4,144,640]{2,1,0:T(8,128)(2,1)}, bf16[4,144,640]{2,1,0:T(8,128)(2,1)}, u32[]{:S(2)}, u32[]{:S(2)}) collective-permute-start(bf16[4,144,640]{2,1,0:T(8,128)(2,1)} %get-tuple-element.262), channel_id=1, source_target_pairs={{0,8},{4,12},{8,0},{12,4},{16,24},{20,28},{24,16},{28,20},{1,9},{5... | collective-permute-start | bytes 2211848 | tf_op jit(solution)/shard_map/ppermute | solution.py:563
  103.9 40.6 %collective-permute-start.7 = (bf16[2,4,144,640]{3,2,1,0:T(8,128)(2,1)S(1)}, bf16[2,4,144,640]{3,2,1,0:T(8,128)(2,1)S(1)}, u32[]{:S(2)}, u32[]{:S(2)}) collective-permute-start(bf16[2,4,144,640]{3,2,1,0:T(8,128)(2,1)S(1)} %get-tuple-element.264), channel_id=1, source_target_pairs={{0,8},{4,12},{8,0},{12,4},{16,24},{20,28},{24,16},{28,20},{1,9},{5... | collective-permute-start | bytes 4423688 | tf_op jit(solution)/shard_map/ppermute | solution.py:563
  106.8 40.2 %collective-permute-start.5 = (bf16[2,4,144,640]{3,2,1,0:T(8,128)(2,1)S(1)}, bf16[2,4,144,640]{3,2,1,0:T(8,128)(2,1)S(1)}, u32[]{:S(2)}, u32[]{:S(2)}) collective-permute-start(bf16[2,4,144,640]{3,2,1,0:T(8,128)(2,1)S(1)} %get-tuple-element.258), channel_id=1, source_target_pairs={{0,16},{4,20},{8,24},{12,28},{16,0},{20,4},{24,8},{28,12},{1,17},{... | collective-permute-start | bytes 4423688 | tf_op jit(solution)/shard_map/ppermute | solution.py:563
  145.2 10.3 %collective-permute-start.8 = (bf16[2,2,4,144,128]{4,3,2,1,0:T(8,128)(2,1)S(1)}, bf16[2,2,4,144,128]{4,3,2,1,0:T(8,128)(2,1)S(1)}, u32[]{:S(2)}, u32[]{:S(2)}) collective-permute-start(bf16[2,2,4,144,128]{4,3,2,1,0:T(8,128)(2,1)S(1)} %slice.685), channel_id=1, source_target_pairs={{0,4},{4,0},{8,12},{12,8},{16,20},{20,16},{24,28},{28,24},{1,5},{5... | collective-permute-start | bytes 1769480 | tf_op jit(solution)/shard_map/ppermute | solution.py:563
  150.1 25.5 %collective-permute-start.9 = (bf16[2304,1152]{1,0:T(8,128)(2,1)}, bf16[2304,1152]{1,0:T(8,128)(2,1)}, u32[]{:S(2)}, u32[]{:S(2)}) collective-permute-start(bf16[2304,1152]{1,0:T(8,128)(2,1)} %bitcast.29), channel_id=1, source_target_pairs={{0,4},{4,0},{8,12},{12,8},{16,20},{20,16},{24,28},{28,24},{1,5},{5... | collective-permute-start | bytes 15925256 | tf_op jit(solution)/shard_map/ppermute | solution.py:563
  314.8 6.2 collective-permute-start.12
  333.7 280.4 %reduce-scatter.5.cloned.1.call-start = ((), (), s32[]{:S(2)}) async-start(), calls=%async_computation.5 | async-start | bytes 5529600 | tf_op jit(solution)/shard_map/reduce_scatter | solution.py:904
  470.8 31.2 %collective-permute-start.24 = (bf16[2,2,4,144,128]{4,3,2,1,0:T(8,128)(2,1)}, bf16[2,2,4,144,128]{4,3,2,1,0:T(8,128)(2,1)}, u32[]{:S(2)}, u32[]{:S(2)}) collective-permute-start(bf16[2,2,4,144,128]{4,3,2,1,0:T(8,128)(2,1)} %select_bitcast_fusion), channel_id=1, source_target_pairs={{0,4},{4,0},{8,12},{12,8},{16,20},{20,16},{24,28},{28,24},{1,5},{5... | collective-permute-start | bytes 1769480 | tf_op jit(solution)/shard_map/ppermute | solution.py:563
  472.1 11.1 %collective-permute-start.13 = (f32[3,1152]{1,0:T(4,128)S(1)}, f32[3,1152]{1,0:T(4,128)S(1)}, u32[]{:S(2)}, u32[]{:S(2)}) collective-permute-start(f32[3,1152]{1,0:T(4,128)S(1)} %bitcast.454), channel_id=1, source_target_pairs={{1,0},{2,1},{3,2},{5,4},{6,5},{7,6},{9,8},{10,9},{11,10},{13,12},{... | collective-permute-start | bytes 41480 | tf_op jit(solution)/shard_map/ppermute | solution.py:500
  474.3 6.3 collective-permute-start.14
  483.2 11.1 %collective-permute-start.15 = (bf16[256,2304]{1,0:T(8,128)(2,1)}, bf16[256,2304]{1,0:T(8,128)(2,1)}, u32[]{:S(2)}, u32[]{:S(2)}) collective-permute-start(bf16[256,2304]{1,0:T(8,128)(2,1)} %pad_maximum_fusion.9), channel_id=1, source_target_pairs={{0,4},{4,0},{8,12},{12,8},{16,20},{20,16},{24,28},{28,24},{1,5},{5... | collective-permute-start | bytes 3538952 | tf_op jit(solution)/shard_map/ppermute | solution.py:563
  500.5 34.0 %collective-permute-start.17 = (bf16[2,4,144,640]{3,2,1,0:T(8,128)(2,1)S(1)}, bf16[2,4,144,640]{3,2,1,0:T(8,128)(2,1)S(1)}, u32[]{:S(2)}, u32[]{:S(2)}) collective-permute-start(bf16[2,4,144,640]{3,2,1,0:T(8,128)(2,1)S(1)} %slice_bitcast_fusion.2), channel_id=1, source_target_pairs={{0,16},{4,20},{8,24},{12,28},{16,0},{20,4},{24,8},{28,12},{1,17},{... | collective-permute-start | bytes 4423688 | tf_op jit(solution)/shard_map/ppermute | solution.py:563
  504.8 36.1 %collective-permute-start.25 = (bf16[2,4,144,640]{3,2,1,0:T(8,128)(2,1)S(1)}, bf16[2,4,144,640]{3,2,1,0:T(8,128)(2,1)S(1)}, u32[]{:S(2)}, u32[]{:S(2)}) collective-permute-start(bf16[2,4,144,640]{3,2,1,0:T(8,128)(2,1)S(1)} %slice_bitcast_fusion), channel_id=1, source_target_pairs={{0,8},{4,12},{8,0},{12,4},{16,24},{20,28},{24,16},{28,20},{1,9},{5... | collective-permute-start | bytes 4423688 | tf_op jit(solution)/shard_map/ppermute | solution.py:563
  535.1 19.1 %collective-permute-start.18 = (bf16[4,144,640]{2,1,0:T(8,128)(2,1)S(1)}, bf16[4,144,640]{2,1,0:T(8,128)(2,1)S(1)}, u32[]{:S(2)}, u32[]{:S(2)}) collective-permute-start(bf16[4,144,640]{2,1,0:T(8,128)(2,1)S(1)} %slice_bitcast_fusion.8), channel_id=1, source_target_pairs={{0,8},{4,12},{8,0},{12,4},{16,24},{20,28},{24,16},{28,20},{1,9},{5... | collective-permute-start | bytes 2211848 | tf_op jit(solution)/shard_map/ppermute | solution.py:563
  556.4 19.0 %collective-permute-start.26 = (bf16[4,144,640]{2,1,0:T(8,128)(2,1)S(1)}, bf16[4,144,640]{2,1,0:T(8,128)(2,1)S(1)}, u32[]{:S(2)}, u32[]{:S(2)}) collective-permute-start(bf16[4,144,640]{2,1,0:T(8,128)(2,1)S(1)} %slice_bitcast_fusion.6), channel_id=1, source_target_pairs={{0,16},{4,20},{8,24},{12,28},{16,0},{20,4},{24,8},{28,12},{1,17},{... | collective-permute-start | bytes 2211848 | tf_op jit(solution)/shard_map/ppermute | solution.py:563
  557.5 3.7 collective-permute-start.20
  561.2 14.4 %collective-permute-start.21 = (f32[2,1152]{1,0:T(2,128)S(1)}, f32[2,1152]{1,0:T(2,128)S(1)}, u32[]{:S(2)}, u32[]{:S(2)}) collective-permute-start(f32[2,1152]{1,0:T(2,128)S(1)} %fusion.197), channel_id=1, source_target_pairs={{0,16},{4,20},{8,24},{12,28},{16,0},{20,4},{24,8},{28,12},{1,17},{... | collective-permute-start | bytes 27656 | tf_op jit(solution)/shard_map/ppermute | solution.py:704
  575.7 6.1 collective-permute-start.22
  577.3 35.3 %collective-permute-start.27 = (bf16[144,1280]{1,0:T(8,128)(2,1)S(1)}, bf16[144,1280]{1,0:T(8,128)(2,1)S(1)}, u32[]{:S(2)}, u32[]{:S(2)}) collective-permute-start(bf16[144,1280]{1,0:T(8,128)(2,1)S(1)} %get-tuple-element.246), channel_id=1, source_target_pairs={{0,3},{1,0},{2,1},{3,2},{4,7},{5,4},{6,5},{7,6},{8,11},{9,8},{10,9... | collective-permute-start | bytes 1105928 | tf_op jit(solution)/shard_map/ppermute | solution.py:556
  579.8 32.9 %collective-permute-start.28 = (bf16[144,1280]{1,0:T(8,128)(2,1)S(1)}, bf16[144,1280]{1,0:T(8,128)(2,1)S(1)}, u32[]{:S(2)}, u32[]{:S(2)}) collective-permute-start(bf16[144,1280]{1,0:T(8,128)(2,1)S(1)} %get-tuple-element.247), channel_id=1, source_target_pairs={{0,2},{1,3},{2,0},{3,1},{4,6},{5,7},{6,4},{7,5},{8,10},{9,11},{10,... | collective-permute-start | bytes 1105928 | tf_op jit(solution)/shard_map/ppermute | solution.py:556
  579.9 32.8 %collective-permute-start.29 = (bf16[144,1280]{1,0:T(8,128)(2,1)S(1)}, bf16[144,1280]{1,0:T(8,128)(2,1)S(1)}, u32[]{:S(2)}, u32[]{:S(2)}) collective-permute-start(bf16[144,1280]{1,0:T(8,128)(2,1)S(1)} %get-tuple-element.248), channel_id=1, source_target_pairs={{0,1},{1,2},{2,3},{3,0},{4,5},{5,6},{6,7},{7,4},{8,9},{9,10},{10,1... | collective-permute-start | bytes 1105928 | tf_op jit(solution)/shard_map/ppermute | solution.py:556
  581.8 30.2 %collective-permute-start.23 = (f32[2,1152]{1,0:T(2,128)S(1)}, f32[2,1152]{1,0:T(2,128)S(1)}, u32[]{:S(2)}, u32[]{:S(2)}) collective-permute-start(f32[2,1152]{1,0:T(2,128)S(1)} %add.374), channel_id=1, source_target_pairs={{0,2},{1,3},{2,0},{3,1},{4,6},{5,7},{6,4},{7,5},{8,10},{9,11},{10,... | collective-permute-start | bytes 27656 | tf_op jit(solution)/shard_map/ppermute | solution.py:704
  615.4 6.5 %collective-permute-start.32 = (bf16[2,96,1152]{2,1,0:T(8,128)(2,1)S(1)}, bf16[2,96,1152]{2,1,0:T(8,128)(2,1)S(1)}, u32[]{:S(2)}, u32[]{:S(2)}) collective-permute-start(bf16[2,96,1152]{2,1,0:T(8,128)(2,1)S(1)} %select_bitcast_fusion.1), channel_id=1, source_target_pairs={{0,4},{4,0},{8,12},{12,8},{16,20},{20,16},{24,28},{28,24},{1,5},{5... | collective-permute-start | bytes 1327112 | tf_op jit(solution)/shard_map/ppermute | solution.py:563
  615.6 5.5 collective-permute-start.31
  (172 other events, 1536.5 us)
Sparse Core Ops, SparseCore 0:
  10.9 90.1 all-gather.3
  104.4 180.3 all-gather.5
  333.8 160.4 reduce-scatter.2
  496.5 80.4 reduce-scatter.4

commit v5 on v4

--- a/solution.py
+++ b/solution.py
@@ -697,7 +697,7 @@
 
 
 def everywhere(array):
-    for axis in ("dp", "seq"):
+    for axis in ("seq", "dp"):
         size = lax.axis_size(axis)
         bit = 1
         while bit < size:
@@ -776,7 +776,8 @@
     at = R + 2 * NS
     select_full = [w[:, :at] for w in small_full]
     step_full = [w[:, at : at + R] for w in small_full]
-    line_full = [w[:, at + R : columns].astype(F32).T for w in small_full]
+    unit_lines = jnp.eye(columns - at - R, dtype=BF16)
+    line_full = [dot(unit_lines, w[:, at + R : columns], ((1,), (1,))) for w in small_full]
     decay_rate = [-jnp.exp(w[:NS]) for w in line_full]
     conv_taps = [w[NS : NS + KC] for w in line_full]
     bias_conv, bias_step, skip_wide = (
@@ -939,7 +940,7 @@
                 [
                     dot(inner[h], select_low, ((0,), (0,))),
                     dot(pre_low[h], steps_low, ((0,), (0,))),
-                    jnp.concatenate(lines).T,
+                    dot(jnp.concatenate(lines).astype(BF16), unit_lines, ((0,), (0,))),
                     jnp.zeros((half, -columns % LANE), F32),
                 ],
                 1,
@@ -988,7 +989,7 @@
     )
 
     last = jnp.stack([first_gain_grad, jnp.pad(squared_values, (0, MODEL_WIDTH - 3))])
-    last = everywhere(after(last, in_last))
+    last = everywhere(after(last, in_plane[0]))
     first_part = lax.dynamic_slice_in_dim(last[:1], lax.axis_index("dp") * width, width, 1)
     stats = jnp.sqrt(last[1, :3] / (rows * parts * depth * MODEL_WIDTH))
     return (

time: 640 us -> 636 us (level)
  waiting for transfers between devices: 198 us -> 229 us
  local copies, waits for them, and re-layouts: 101 us -> 82.2 us
  matrix products: 48.9 us -> 41.7 us
    ppermute x6, waiting for transfers between devices: 25.4 us -> 61.8 us  [moved(): lax.ppermute(array, 'seq', [(i, (i + by) % size) for i in range(size)])]
    all_gather x1, waiting for transfers between devices: 22.1 us -> 49.1 us  [per_device(): experts = lax.all_gather(experts, BOTH, axis=0, tiled=True)]
    ppermute x18, waiting for transfers between devices: 109 us -> 85.3 us  [moved(): return lax.ppermute(array, 'dp', pairs)]
    ppermute x5, waiting for transfers between devices: 31.1 us -> 13.7 us  [everywhere(): lax.ppermute(array, axis, [(i, i ^ bit) for i in range(size)])]
    reduce_scatter x1, waiting for transfers between devices: 7.84 us -> 15.8 us  [per_device(): lax.psum_scatter(both_sum, 'dp', scatter_dimension=0, tiled=True, axis_in...]
    slice x6 -> x2, local copies, waits for them, and re-layouts: 7.56 us -> 0.05 us  [per_device(): w[NS + KC + k][None]]
    dot_general x27 -> x31, matrix products: 48.9 us -> 41.7 us  [dot(): lax.dot_general(left, right, (contract, ((), ())), precision=precision, p...]
    unnamed x344 -> x340, local copies, waits for them, and re-layouts: 36.1 us -> 32.5 us
  transfers between devices with their start and end apart: 37 -> 37, of which waited for: 17 -> 19; matrix products, arithmetic and copies ran while one was open for 24% -> 20% of each run, Pallas kernels for 16% -> 16%
where the time goes in v5:
time: 636 us; the launch traced here: 626 us
  waiting for transfers between devices  229 us (36%)
  Pallas kernels  123 us (19%)
  local copies, waits for them, and re-layouts  82.2 us (13%)
  blocking collectives  47.1 us (7%)
  other arithmetic  42.8 us (7%)
  matrix products  41.7 us (7%)
  starting transfers between devices  39.1 us (6%)
  between operations  20.9 us (3%)
    ppermute x18, waiting for transfers between devices, moved(): return lax.ppermute(array, 'dp', pairs)  85.3 us
    ppermute x6, waiting for transfers between devices, moved(): lax.ppermute(array, 'seq', [(i, (i + by) % size) for i in range(size)])  61.8 us
    pallas_call x2, Pallas kernels, scan_adjoint(): pl.pallas_call(adjoint_kernel, grid=(channels // width,), in_specs=[block...  49.6 us
    all_gather x1, waiting for transfers between devices, per_device(): experts = lax.all_gather(experts, BOTH, axis=0, tiled=True)  49.1 us
    dot_general x31, matrix products, dot(): lax.dot_general(left, right, (contract, ((), ())), precision=precision, p...  41.7 us
    all_gather x2, blocking collectives, entering(): gathered = lax.all_gather(pairs, 'seq')  38.2 us
    unnamed x340, local copies, waits for them, and re-layouts  32.5 us
    pallas_call x1, Pallas kernels, expert_pass(): pl.pallas_call(expert_kernel, grid_spec=pltpu.PrefetchScalarGridSpec(num_...  26 us
  transfers between devices with their start and end apart: 37, of which 19 were waited for; matrix products, arithmetic and copies ran while one was open for 20% of the time, Pallas kernels for 16%

profile of v5, /device:TPU:0, one launch (start us, length us, event | category | flops | bytes accessed | tf_op | source)
XLA Modules:
  0.0 626.4 jit_solution(8667310029644931233)
XLA Ops:
  14.5 3.0 collective-permute-start.1
  21.5 9.5 %collective-permute-done.1 = bf16[144,1280]{1,0:T(8,128)(2,1)} collective-permute-done((bf16[144,1280]{1,0:T(8,128)(2,1)}, bf16[144,1280]{1,0:T(8,128)(2,1)}, u32[]{:S(2)}, u32[]{:S(2)}) %collective-permute-start.1) | collective-permute-done | bytes 368672 | tf_op jit(solution)/shard_map/ppermute | solution.py:556
  32.0 15.8 %collective-permute-done.2 = bf16[144,1280]{1,0:T(8,128)(2,1)S(1)} collective-permute-done((bf16[144,1280]{1,0:T(8,128)(2,1)}, bf16[144,1280]{1,0:T(8,128)(2,1)S(1)}, u32[]{:S(2)}, u32[]{:S(2)}) %collective-permute-start.2) | collective-permute-done | bytes 368672 | tf_op jit(solution)/shard_map/ppermute | solution.py:556
  51.7 10.8 %collective-permute-start = (bf16[3,1280]{1,0:T(4,128)(2,1)}, bf16[3,1280]{1,0:T(4,128)(2,1)}, u32[]{:S(2)}, u32[]{:S(2)}) collective-permute-start(bf16[3,1280]{1,0:T(4,128)(2,1)} %pad_maximum_fusion.26), channel_id=1, source_target_pairs={{0,1},{1,2},{2,3},{4,5},{5,6},{6,7},{8,9},{9,10},{10,11},{12,13},{... | collective-permute-start | bytes 23048 | tf_op jit(solution)/shard_map/ppermute | solution.py:500
  64.7 8.9 %all-gather = bf16[8,144,4]{1,2,0:T(4,128)(2,1)S(1)} all-gather(bf16[1,144,4]{1,2,0:T(4,128)(2,1)S(1)} %maximum_bitcast_fusion.9), channel_id=1, replica_groups=mesh['dp'=8,'seq'=4] {'dp'}, dimensions={0}, use_global_device_ids=true | all-gather | bytes 10368 | tf_op jit(solution)/shard_map/all_gather | solution.py:741
  82.8 19.0 %collective-permute-done.6 = bf16[4,144,640]{2,1,0:T(8,128)(2,1)S(1)} collective-permute-done((bf16[4,144,640]{2,1,0:T(8,128)(2,1)}, bf16[4,144,640]{2,1,0:T(8,128)(2,1)S(1)}, u32[]{:S(2)}, u32[]{:S(2)}) %collective-permute-start.6) | collective-permute-done | bytes 737312 | tf_op jit(solution)/shard_map/ppermute | solution.py:563
  110.0 34.6 %collective-permute-done.7 = bf16[2,4,144,640]{3,2,1,0:T(8,128)(2,1)S(1)} collective-permute-done((bf16[2,4,144,640]{3,2,1,0:T(8,128)(2,1)S(1)}, bf16[2,4,144,640]{3,2,1,0:T(8,128)(2,1)S(1)}, u32[]{:S(2)}, u32[]{:S(2)}) %collective-permute-start.7) | collective-permute-done | bytes 1474592 | tf_op jit(solution)/shard_map/ppermute | solution.py:563
  162.6 6.3 %shard_map.291 = (f32[16,8,1152]{2,1,0:T(8,128)S(1)}, f32[16,8,1152]{2,1,0:T(8,128)S(1)}, f32[16,1152]{1,0:T(8,128)S(1)}, f32[16,1152]{1,0:T(8,128)S(1)}) custom-call(f32[256,1152]{1,0:T(8,128)S(1)} %get-tuple-element.280.delta, f32[256,1152]{1,0:T(8,128)S(1)} %get-tuple-element.279.driven, f32[256,128]{1,0:T(8,128)S(1)} %broadcast_in_dim.97.kept, ...), custom_call_target="tpu_custom_call" | custom-call | bytes 5529600 | tf_op jit(solution)/shard_map/pallas_call | solution.py:310
  171.0 6.3 %shard_map.290 = (f32[16,8,1152]{2,1,0:T(8,128)S(1)}, f32[16,8,1152]{2,1,0:T(8,128)S(1)}, f32[16,1152]{1,0:T(8,128)S(1)}, f32[16,1152]{1,0:T(8,128)S(1)}) custom-call(f32[256,1152]{1,0:T(8,128)S(1)} %get-tuple-element.282.delta, f32[256,1152]{1,0:T(8,128)S(1)} %get-tuple-element.281.driven, f32[256,128]{1,0:T(8,128)S(1)} %broadcast_in_dim.97.kept, ...), custom_call_target="tpu_custom_call" | custom-call | bytes 5529600 | tf_op jit(solution)/shard_map/pallas_call | solution.py:310
  177.4 21.3 %all_gather.18 = bf16[4,2,16,2304]{3,2,1,0:T(8,128)(2,1)S(1)} all-gather(bf16[1,2,16,2304]{3,2,1,0:T(8,128)(2,1)S(1)} %pad_maximum_fusion.22), channel_id=1, replica_groups=mesh['dp'=8,'seq'=4] {'seq'}, dimensions={0}, use_global_device_ids=true | all-gather | bytes 737280 | tf_op jit(solution)/shard_map/all_gather | solution.py:522
  199.6 8.5 %shard_map.293 = (f32[256,1152]{1,0:T(8,128)S(1)}, bf16[256,1152]{1,0:T(8,128)(2,1)S(1)}) custom-call(f32[256,1152]{1,0:T(8,128)S(1)} %get-tuple-element.280.delta, f32[256,1152]{1,0:T(8,128)S(1)} %get-tuple-element.279.driven, bf16[256,1152]{1,0:T(8,128)(2,1)S(1)} %get-tuple-element.64.inner, bf16[256,1152]{1,0:T(8,128)(2,1)S(1)} %get-tuple-element.354.gate, ...), custom_call_target="tpu_custom_call" | custom-call | bytes 7004160 | tf_op jit(solution)/shard_map/pallas_call | solution.py:329
  210.0 8.3 %shard_map.292 = (f32[256,1152]{1,0:T(8,128)S(1)}, bf16[256,1152]{1,0:T(8,128)(2,1)S(1)}) custom-call(f32[256,1152]{1,0:T(8,128)S(1)} %get-tuple-element.282.delta, f32[256,1152]{1,0:T(8,128)S(1)} %get-tuple-element.281.driven, bf16[256,1152]{1,0:T(8,128)(2,1)S(1)} %get-tuple-element.63.inner, bf16[256,1152]{1,0:T(8,128)(2,1)S(1)} %get-tuple-element.355.gate, ...), custom_call_target="tpu_custom_call" | custom-call | bytes 7004160 | tf_op jit(solution)/shard_map/pallas_call | solution.py:329
  220.2 3.0 dynamic-slice_bitcast_fusion.1
  236.6 49.1 %all-gather.6.cloned.1.call-done = bf16[12288,1152]{1,0:T(8,128)(2,1)} async-done(((bf16[384,1152]{1,0:T(8,128)(2,1)}), bf16[12288,1152]{1,0:T(8,128)(2,1)}) %all-gather.6.cloned.1.call-update) | async-done | bytes 28311568 | tf_op jit(solution)/shard_map/all_gather | solution.py:773
  288.0 26.0 %shard_map.294 = (f32[320,1152]{1,0:T(8,128)}, f32[320,1152]{1,0:T(8,128)}, bf16[16,5,96,1152]{3,2,1,0:T(8,128)(2,1)}) custom-call(s32[1]{0:T(128)} %bitcast.67.at, bf16[320,1152]{1,0:T(8,128)(2,1)S(1)} %copy-done.28, bf16[320,1152]{1,0:T(8,128)(2,1)S(1)} %copy-done.27, bf16[32,4,96,1152]{3,2,1,0:T(8,128)(2,1)} %bitcast.389, bf16[32,4,96,1152]{3,2,1,0:T(8,128)(2,1)} %bitcast.390), custom_call_target="tpu_custom_call" | custom-call | flops 13589544960 | bytes 28311552 | tf_op jit(solution)/shard_map/pallas_call | solution.py:455
  317.9 3.6 multiply_reduce_fusion.2
  350.6 4.4 fusion.19
  355.1 6.1 shard_map.295
  363.4 6.1 shard_map.296
  369.6 16.8 %all_gather.21 = bf16[4,2,16,2304]{3,2,1,0:T(8,128)(2,1)S(1)} all-gather(bf16[1,2,16,2304]{3,2,1,0:T(8,128)(2,1)S(1)} %pad_maximum_fusion.23), channel_id=1, replica_groups=mesh['dp'=8,'seq'=4] {'seq'}, dimensions={0}, use_global_device_ids=true | all-gather | bytes 737280 | tf_op jit(solution)/shard_map/all_gather | solution.py:522
  388.4 24.9 %shard_map.297 = (bf16[256,1152]{1,0:T(8,128)(2,1)S(1)}, f32[256,1152]{1,0:T(8,128)S(1)}, f32[16,1152]{1,0:T(8,128)S(1)}, f32[1,1152]{1,0:T(1,128)S(1)}, f32[1,1...) custom-call(f32[256,1152]{1,0:T(8,128)S(1)} %get-tuple-element.282.delta, f32[256,1152]{1,0:T(8,128)S(1)} %copy-done.1, ...), custom_call_target="tpu_custom_call" | custom-call | bytes 20643840 | tf_op jit(solution)/shard_map/pallas_call | solution.py:352
  414.5 24.7 %shard_map.298 = (bf16[256,1152]{1,0:T(8,128)(2,1)S(1)}, f32[256,1152]{1,0:T(8,128)S(1)}, f32[16,1152]{1,0:T(8,128)S(1)}, f32[1,1152]{1,0:T(1,128)S(1)}, f32[1,1...) custom-call(f32[256,1152]{1,0:T(8,128)S(1)} %get-tuple-element.280.delta, ...), custom_call_target="tpu_custom_call" | custom-call | bytes 20643840 | tf_op jit(solution)/shard_map/pallas_call | solution.py:352
  457.5 2.8 reshape.613
  470.3 2.7 collective-permute-done.14
  478.8 15.8 %reduce-scatter.3.cloned.1.call-done = bf16[4,5,96,1152]{3,2,1,0:T(8,128)(2,1)} async-done(((bf16[16,5,96,1152]{3,2,1,0:T(8,128)(2,1)}), bf16[4,5,96,1152]{3,2,1,0:T(8,128)(2,1)}) %reduce-scatter.3.cloned.1.call-update) | async-done | bytes 4423696 | tf_op jit(solution)/shard_map/reduce_scatter | solution.py:902
  497.6 4.7 convolution_convert_fusion
  509.7 3.4 multiply_reduce_fusion.4
  513.0 23.7 %collective-permute-done.17 = bf16[2,4,144,640]{3,2,1,0:T(8,128)(2,1)S(1)} collective-permute-done((bf16[2,4,144,640]{3,2,1,0:T(8,128)(2,1)S(1)}, bf16[2,4,144,640]{3,2,1,0:T(8,128)(2,1)S(1)}, u32[]{:S(2)}, u32[]{:S(2)}) %collective-permute-start.17) | collective-permute-done | bytes 1474592 | tf_op jit(solution)/shard_map/ppermute | solution.py:563
  548.2 4.2 collective-permute-done.19
  557.4 6.3 %collective-permute-done.21 = f32[2,1152]{1,0:T(2,128)S(1)} collective-permute-done((f32[2,1152]{1,0:T(2,128)S(1)}, f32[2,1152]{1,0:T(2,128)S(1)}, u32[]{:S(2)}, u32[]{:S(2)}) %collective-permute-start.21) | collective-permute-done | bytes 9248 | tf_op jit(solution)/shard_map/ppermute | solution.py:704
  572.5 11.8 %collective-permute-done.27 = bf16[144,1280]{1,0:T(8,128)(2,1)S(1)} collective-permute-done((bf16[144,1280]{1,0:T(8,128)(2,1)S(1)}, bf16[144,1280]{1,0:T(8,128)(2,1)S(1)}, u32[]{:S(2)}, u32[]{:S(2)}) %collective-permute-start.27) | collective-permute-done | bytes 368672 | tf_op jit(solution)/shard_map/ppermute | solution.py:556
  584.3 24.6 %collective-permute-done.28 = bf16[144,1280]{1,0:T(8,128)(2,1)S(1)} collective-permute-done((bf16[144,1280]{1,0:T(8,128)(2,1)S(1)}, bf16[144,1280]{1,0:T(8,128)(2,1)S(1)}, u32[]{:S(2)}, u32[]{:S(2)}) %collective-permute-start.28) | collective-permute-done | bytes 368672 | tf_op jit(solution)/shard_map/ppermute | solution.py:556
  (659 shorter events, 188.3 us)
Async XLA Ops:
  7.2 213.0 %all-gather.4.cloned.1.call-start = ((), (), s32[]{:S(2)}) async-start(), calls=%async_computation.2 | async-start | bytes 5474304 | tf_op jit(solution)/shard_map/all_gather | solution.py:770
  7.9 277.9 %all-gather.6.cloned.1.call-start = ((), (), s32[]{:S(2)}) async-start(), calls=%async_computation.3 | async-start | bytes 29196288 | tf_op jit(solution)/shard_map/all_gather | solution.py:773
  14.5 16.5 %collective-permute-start.1 = (bf16[144,1280]{1,0:T(8,128)(2,1)}, bf16[144,1280]{1,0:T(8,128)(2,1)}, u32[]{:S(2)}, u32[]{:S(2)}) collective-permute-start(bf16[144,1280]{1,0:T(8,128)(2,1)} %get-tuple-element.229), channel_id=1, source_target_pairs={{0,1},{1,2},{2,3},{3,0},{4,5},{5,6},{6,7},{7,4},{8,9},{9,10},{10,1... | collective-permute-start | bytes 1105928 | tf_op jit(solution)/shard_map/ppermute | solution.py:556
  17.5 30.3 %collective-permute-start.2 = (bf16[144,1280]{1,0:T(8,128)(2,1)}, bf16[144,1280]{1,0:T(8,128)(2,1)S(1)}, u32[]{:S(2)}, u32[]{:S(2)}) collective-permute-start(bf16[144,1280]{1,0:T(8,128)(2,1)} %get-tuple-element.229), channel_id=1, source_target_pairs={{0,2},{1,3},{2,0},{3,1},{4,6},{5,7},{6,4},{7,5},{8,10},{9,11},{10,... | collective-permute-start | bytes 1105928 | tf_op jit(solution)/shard_map/ppermute | solution.py:556
  20.1 27.8 %collective-permute-start.3 = (bf16[144,1280]{1,0:T(8,128)(2,1)}, bf16[144,1280]{1,0:T(8,128)(2,1)S(1)}, u32[]{:S(2)}, u32[]{:S(2)}) collective-permute-start(bf16[144,1280]{1,0:T(8,128)(2,1)} %get-tuple-element.229), channel_id=1, source_target_pairs={{0,3},{1,0},{2,1},{3,2},{4,7},{5,4},{6,5},{7,6},{8,11},{9,8},{10,9... | collective-permute-start | bytes 1105928 | tf_op jit(solution)/shard_map/ppermute | solution.py:556
  50.8 443.8 %reduce-scatter.3.cloned.1.call-start = ((), (), s32[]{:S(2)}) async-start(), calls=%async_computation.4 | async-start | bytes 22118400 | tf_op jit(solution)/shard_map/reduce_scatter | solution.py:902
  51.7 28.5 %collective-permute-start = (bf16[3,1280]{1,0:T(4,128)(2,1)}, bf16[3,1280]{1,0:T(4,128)(2,1)}, u32[]{:S(2)}, u32[]{:S(2)}) collective-permute-start(bf16[3,1280]{1,0:T(4,128)(2,1)} %pad_maximum_fusion.26), channel_id=1, source_target_pairs={{0,1},{1,2},{2,3},{4,5},{5,6},{6,7},{8,9},{9,10},{10,11},{12,13},{... | collective-permute-start | bytes 23048 | tf_op jit(solution)/shard_map/ppermute | solution.py:500
  78.7 23.0 %collective-permute-start.6 = (bf16[4,144,640]{2,1,0:T(8,128)(2,1)}, bf16[4,144,640]{2,1,0:T(8,128)(2,1)S(1)}, u32[]{:S(2)}, u32[]{:S(2)}) collective-permute-start(bf16[4,144,640]{2,1,0:T(8,128)(2,1)} %get-tuple-element.261), channel_id=1, source_target_pairs={{0,16},{4,20},{8,24},{12,28},{16,0},{20,4},{24,8},{28,12},{1,17},{... | collective-permute-start | bytes 2211848 | tf_op jit(solution)/shard_map/ppermute | solution.py:563
  80.9 24.6 %collective-permute-start.4 = (bf16[4,144,640]{2,1,0:T(8,128)(2,1)}, bf16[4,144,640]{2,1,0:T(8,128)(2,1)}, u32[]{:S(2)}, u32[]{:S(2)}) collective-permute-start(bf16[4,144,640]{2,1,0:T(8,128)(2,1)} %get-tuple-element.262), channel_id=1, source_target_pairs={{0,8},{4,12},{8,0},{12,4},{16,24},{20,28},{24,16},{28,20},{1,9},{5... | collective-permute-start | bytes 2211848 | tf_op jit(solution)/shard_map/ppermute | solution.py:563
  103.9 40.6 %collective-permute-start.7 = (bf16[2,4,144,640]{3,2,1,0:T(8,128)(2,1)S(1)}, bf16[2,4,144,640]{3,2,1,0:T(8,128)(2,1)S(1)}, u32[]{:S(2)}, u32[]{:S(2)}) collective-permute-start(bf16[2,4,144,640]{3,2,1,0:T(8,128)(2,1)S(1)} %get-tuple-element.264), channel_id=1, source_target_pairs={{0,8},{4,12},{8,0},{12,4},{16,24},{20,28},{24,16},{28,20},{1,9},{5... | collective-permute-start | bytes 4423688 | tf_op jit(solution)/shard_map/ppermute | solution.py:563
  106.8 40.2 %collective-permute-start.5 = (bf16[2,4,144,640]{3,2,1,0:T(8,128)(2,1)S(1)}, bf16[2,4,144,640]{3,2,1,0:T(8,128)(2,1)S(1)}, u32[]{:S(2)}, u32[]{:S(2)}) collective-permute-start(bf16[2,4,144,640]{3,2,1,0:T(8,128)(2,1)S(1)} %get-tuple-element.258), channel_id=1, source_target_pairs={{0,16},{4,20},{8,24},{12,28},{16,0},{20,4},{24,8},{28,12},{1,17},{... | collective-permute-start | bytes 4423688 | tf_op jit(solution)/shard_map/ppermute | solution.py:563
  145.2 5.1 collective-permute-start.8
  147.8 8.8 %collective-permute-start.9 = (bf16[2304,1152]{1,0:T(8,128)(2,1)S(1)}, bf16[2304,1152]{1,0:T(8,128)(2,1)S(1)}, u32[]{:S(2)}, u32[]{:S(2)}) collective-permute-start(bf16[2304,1152]{1,0:T(8,128)(2,1)S(1)} %bitcast.411), channel_id=1, source_target_pairs={{0,4},{4,0},{8,12},{12,8},{16,20},{20,16},{24,28},{28,24},{1,5},{5... | collective-permute-start | bytes 15925256 | tf_op jit(solution)/shard_map/ppermute | solution.py:563
  316.1 6.2 collective-permute-start.12
  334.9 275.4 %reduce-scatter.5.cloned.1.call-start = ((), (), s32[]{:S(2)}) async-start(), calls=%async_computation.5 | async-start | bytes 5529600 | tf_op jit(solution)/shard_map/reduce_scatter | solution.py:905
  463.6 31.0 %collective-permute-start.24 = (bf16[2,2,4,144,128]{4,3,2,1,0:T(8,128)(2,1)}, bf16[2,2,4,144,128]{4,3,2,1,0:T(8,128)(2,1)}, u32[]{:S(2)}, u32[]{:S(2)}) collective-permute-start(bf16[2,2,4,144,128]{4,3,2,1,0:T(8,128)(2,1)} %select_bitcast_fusion), channel_id=1, source_target_pairs={{0,4},{4,0},{8,12},{12,8},{16,20},{20,16},{24,28},{28,24},{1,5},{5... | collective-permute-start | bytes 1769480 | tf_op jit(solution)/shard_map/ppermute | solution.py:563
  464.5 11.1 %collective-permute-start.13 = (f32[3,1152]{1,0:T(4,128)S(1)}, f32[3,1152]{1,0:T(4,128)S(1)}, u32[]{:S(2)}, u32[]{:S(2)}) collective-permute-start(f32[3,1152]{1,0:T(4,128)S(1)} %bitcast.451), channel_id=1, source_target_pairs={{1,0},{2,1},{3,2},{5,4},{6,5},{7,6},{9,8},{10,9},{11,10},{13,12},{... | collective-permute-start | bytes 41480 | tf_op jit(solution)/shard_map/ppermute | solution.py:500
  466.7 6.3 %collective-permute-start.14 = (f32[3,1152]{1,0:T(4,128)S(1)}, f32[3,1152]{1,0:T(4,128)S(1)}, u32[]{:S(2)}, u32[]{:S(2)}) collective-permute-start(f32[3,1152]{1,0:T(4,128)S(1)} %bitcast.452), channel_id=1, source_target_pairs={{1,0},{2,1},{3,2},{5,4},{6,5},{7,6},{9,8},{10,9},{11,10},{13,12},{... | collective-permute-start | bytes 41480 | tf_op jit(solution)/shard_map/ppermute | solution.py:500
  475.6 20.6 %collective-permute-start.15 = (bf16[256,2304]{1,0:T(8,128)(2,1)}, bf16[256,2304]{1,0:T(8,128)(2,1)}, u32[]{:S(2)}, u32[]{:S(2)}) collective-permute-start(bf16[256,2304]{1,0:T(8,128)(2,1)} %pad_maximum_fusion.9), channel_id=1, source_target_pairs={{0,4},{4,0},{8,12},{12,8},{16,20},{20,16},{24,28},{28,24},{1,5},{5... | collective-permute-start | bytes 3538952 | tf_op jit(solution)/shard_map/ppermute | solution.py:563
  502.7 34.0 %collective-permute-start.17 = (bf16[2,4,144,640]{3,2,1,0:T(8,128)(2,1)S(1)}, bf16[2,4,144,640]{3,2,1,0:T(8,128)(2,1)S(1)}, u32[]{:S(2)}, u32[]{:S(2)}) collective-permute-start(bf16[2,4,144,640]{3,2,1,0:T(8,128)(2,1)S(1)} %slice_bitcast_fusion.2), channel_id=1, source_target_pairs={{0,16},{4,20},{8,24},{12,28},{16,0},{20,4},{24,8},{28,12},{1,17},{... | collective-permute-start | bytes 4423688 | tf_op jit(solution)/shard_map/ppermute | solution.py:563
  505.1 35.4 %collective-permute-start.25 = (bf16[2,4,144,640]{3,2,1,0:T(8,128)(2,1)S(1)}, bf16[2,4,144,640]{3,2,1,0:T(8,128)(2,1)S(1)}, u32[]{:S(2)}, u32[]{:S(2)}) collective-permute-start(bf16[2,4,144,640]{3,2,1,0:T(8,128)(2,1)S(1)} %slice_bitcast_fusion), channel_id=1, source_target_pairs={{0,8},{4,12},{8,0},{12,4},{16,24},{20,28},{24,16},{28,20},{1,9},{5... | collective-permute-start | bytes 4423688 | tf_op jit(solution)/shard_map/ppermute | solution.py:563
  538.9 6.9 %collective-permute-start.18 = (f32[2,1152]{1,0:T(2,128)S(1)}, f32[2,1152]{1,0:T(2,128)S(1)}, u32[]{:S(2)}, u32[]{:S(2)}) collective-permute-start(f32[2,1152]{1,0:T(2,128)S(1)} %maximum_select_fusion.5), channel_id=1, source_target_pairs={{0,1},{1,0},{2,3},{3,2},{4,5},{5,4},{6,7},{7,6},{8,9},{9,8},{10,11... | collective-permute-start | bytes 27656 | tf_op jit(solution)/shard_map/ppermute | solution.py:704
  541.8 22.9 %collective-permute-start.26 = (bf16[4,144,640]{2,1,0:T(8,128)(2,1)}, bf16[4,144,640]{2,1,0:T(8,128)(2,1)}, u32[]{:S(2)}, u32[]{:S(2)}) collective-permute-start(bf16[4,144,640]{2,1,0:T(8,128)(2,1)} %slice_bitcast_fusion.6), channel_id=1, source_target_pairs={{0,16},{4,20},{8,24},{12,28},{16,0},{20,4},{24,8},{28,12},{1,17},{... | collective-permute-start | bytes 2211848 | tf_op jit(solution)/shard_map/ppermute | solution.py:563
  545.8 6.5 %collective-permute-start.19 = (f32[2,1152]{1,0:T(2,128)S(1)}, f32[2,1152]{1,0:T(2,128)S(1)}, u32[]{:S(2)}, u32[]{:S(2)}) collective-permute-start(f32[2,1152]{1,0:T(2,128)S(1)} %fusion.214), channel_id=1, source_target_pairs={{0,2},{1,3},{2,0},{3,1},{4,6},{5,7},{6,4},{7,5},{8,10},{9,11},{10,... | collective-permute-start | bytes 27656 | tf_op jit(solution)/shard_map/ppermute | solution.py:704
  546.8 19.2 %collective-permute-start.23 = (bf16[4,144,640]{2,1,0:T(8,128)(2,1)}, bf16[4,144,640]{2,1,0:T(8,128)(2,1)}, u32[]{:S(2)}, u32[]{:S(2)}) collective-permute-start(bf16[4,144,640]{2,1,0:T(8,128)(2,1)} %slice_bitcast_fusion.8), channel_id=1, source_target_pairs={{0,8},{4,12},{8,0},{12,4},{16,24},{20,28},{24,16},{28,20},{1,9},{5... | collective-permute-start | bytes 2211848 | tf_op jit(solution)/shard_map/ppermute | solution.py:563
  555.2 8.5 %collective-permute-start.21 = (f32[2,1152]{1,0:T(2,128)S(1)}, f32[2,1152]{1,0:T(2,128)S(1)}, u32[]{:S(2)}, u32[]{:S(2)}) collective-permute-start(f32[2,1152]{1,0:T(2,128)S(1)} %add.372), channel_id=1, source_target_pairs={{0,8},{4,12},{8,0},{12,4},{16,24},{20,28},{24,16},{28,20},{1,9},{5... | collective-permute-start | bytes 27656 | tf_op jit(solution)/shard_map/ppermute | solution.py:704
  563.7 8.1 %collective-permute-start.22 = (f32[2,1152]{1,0:T(2,128)S(1)}, f32[2,1152]{1,0:T(2,128)S(1)}, u32[]{:S(2)}, u32[]{:S(2)}) collective-permute-start(f32[2,1152]{1,0:T(2,128)S(1)} %add.373), channel_id=1, source_target_pairs={{0,16},{4,20},{8,24},{12,28},{16,0},{20,4},{24,8},{28,12},{1,17},{... | collective-permute-start | bytes 27656 | tf_op jit(solution)/shard_map/ppermute | solution.py:704
  567.6 16.7 %collective-permute-start.27 = (bf16[144,1280]{1,0:T(8,128)(2,1)S(1)}, bf16[144,1280]{1,0:T(8,128)(2,1)S(1)}, u32[]{:S(2)}, u32[]{:S(2)}) collective-permute-start(bf16[144,1280]{1,0:T(8,128)(2,1)S(1)} %get-tuple-element.246), channel_id=1, source_target_pairs={{0,3},{1,0},{2,1},{3,2},{4,7},{5,4},{6,5},{7,6},{8,11},{9,8},{10,9... | collective-permute-start | bytes 1105928 | tf_op jit(solution)/shard_map/ppermute | solution.py:556
  569.1 39.8 %collective-permute-start.28 = (bf16[144,1280]{1,0:T(8,128)(2,1)S(1)}, bf16[144,1280]{1,0:T(8,128)(2,1)S(1)}, u32[]{:S(2)}, u32[]{:S(2)}) collective-permute-start(bf16[144,1280]{1,0:T(8,128)(2,1)S(1)} %get-tuple-element.247), channel_id=1, source_target_pairs={{0,2},{1,3},{2,0},{3,1},{4,6},{5,7},{6,4},{7,5},{8,10},{9,11},{10,... | collective-permute-start | bytes 1105928 | tf_op jit(solution)/shard_map/ppermute | solution.py:556
  570.6 38.3 %collective-permute-start.29 = (bf16[144,1280]{1,0:T(8,128)(2,1)S(1)}, bf16[144,1280]{1,0:T(8,128)(2,1)S(1)}, u32[]{:S(2)}, u32[]{:S(2)}) collective-permute-start(bf16[144,1280]{1,0:T(8,128)(2,1)S(1)} %get-tuple-element.248), channel_id=1, source_target_pairs={{0,1},{1,2},{2,3},{3,0},{4,5},{5,6},{6,7},{7,4},{8,9},{9,10},{10,1... | collective-permute-start | bytes 1105928 | tf_op jit(solution)/shard_map/ppermute | solution.py:556
  611.6 6.5 %collective-permute-start.32 = (bf16[2,96,1152]{2,1,0:T(8,128)(2,1)S(1)}, bf16[2,96,1152]{2,1,0:T(8,128)(2,1)S(1)}, u32[]{:S(2)}, u32[]{:S(2)}) collective-permute-start(bf16[2,96,1152]{2,1,0:T(8,128)(2,1)S(1)} %select_bitcast_fusion.1), channel_id=1, source_target_pairs={{0,4},{4,0},{8,12},{12,8},{16,20},{20,16},{24,28},{28,24},{1,5},{5... | collective-permute-start | bytes 1327112 | tf_op jit(solution)/shard_map/ppermute | solution.py:563
  611.8 5.5 collective-permute-start.31
  (170 other events, 1527.4 us)
Sparse Core Ops, SparseCore 0:
  10.9 90.0 all-gather.3
  104.4 181.3 all-gather.5
  335.0 159.5 reduce-scatter.2
  496.9 87.7 reduce-scatter.4
